TPU v7x, 32 devices: a whole 2x2x4 slice. The times are simulated.
32 devices in a mesh: dp: 8 (over z, x), mp: 4 (over y, core).
Axes of the slice: x: 2, y: 2, z: 4, core: 2. Of those that a mesh axis runs over, the one named last changes fastest.
Arguments:
- latent: bfloat16 [16, 256, 1280], P('dp', 'mp'), may hold values from -30 to 30
- text_embeds: bfloat16 [16, 77, 2048], P('dp'), may hold values from -6 to 6
- cotangent: bfloat16 [16, 256, 1280], P('dp', 'mp'), may hold values from -11 to 11
- item_count: int32 [8], P('dp'), may hold values from 1 to 2, as said below
- bucket: int32 [16], P('dp'), may hold values from 0 to 2
- timestep: int32 [16], P('dp'), may hold values from 0 to 999
- conv_in: bfloat16 [3, 3, 1280, 1280], P(None, None, 'dp', 'mp'), may hold values from -0.0546875 to 0.0546875
- conv_out: bfloat16 [3, 3, 1280, 1280], P(None, None, 'mp', 'dp'), may hold values from -0.078125 to 0.078125
- time_weight: bfloat16 [1280, 1280], P('dp', 'mp'), may hold values from -0.15625 to 0.15625
- self_query: bfloat16 [1280, 1280], P('dp', 'mp'), may hold values from -0.15625 to 0.15625
- self_key: bfloat16 [1280, 1280], P('dp', 'mp'), may hold values from -0.15625 to 0.15625
- self_value: bfloat16 [1280, 1280], P('dp', 'mp'), may hold values from -0.15625 to 0.15625
- self_out: bfloat16 [1280, 1280], P('mp', 'dp'), may hold values from -1.25 to 1.25
- cross_query: bfloat16 [1280, 1280], P('dp', 'mp'), may hold values from -0.15625 to 0.15625
- cross_key: bfloat16 [2048, 1280], P('dp', 'mp'), may hold values from -0.125 to 0.125
- cross_value: bfloat16 [2048, 1280], P('dp', 'mp'), may hold values from -0.125 to 0.125
- cross_out: bfloat16 [1280, 1280], P('mp', 'dp'), may hold values from -0.75 to 0.75
- ff_value: bfloat16 [1280, 5120], P('dp', 'mp'), may hold values from -0.15625 to 0.15625
- ff_gate: bfloat16 [1280, 5120], P('dp', 'mp'), may hold values from -0.15625 to 0.15625
- ff_down: bfloat16 [5120, 1280], P('mp', 'dp'), may hold values from -0.125 to 0.125
- gn_in_gain: bfloat16 [1280], P('dp'), may hold values from 0.099609375 to 1.8984375
- gn_mid_gain: bfloat16 [1280], P('dp'), may hold values from 0.099609375 to 1.8984375
- self_gain: bfloat16 [1280], P('dp'), may hold values from 0.099609375 to 1.8984375
- cross_gain: bfloat16 [1280], P('dp'), may hold values from 0.099609375 to 1.8984375
- ff_gain: bfloat16 [1280], P('dp'), may hold values from 0.099609375 to 1.8984375
Outputs:
- output: bfloat16 [16, 256, 1280], P('dp', 'mp')
- latent_grad: bfloat16 [16, 256, 1280], P('dp', 'mp')
- conv_in_grad: float32 [3, 3, 1280, 1280], P(None, None, 'dp', 'mp')
- conv_out_grad: float32 [3, 3, 1280, 1280], P(None, None, 'mp', 'dp')
- time_weight_grad: float32 [1280, 1280], P('dp', 'mp')
- self_query_grad: float32 [1280, 1280], P('dp', 'mp')
- self_key_grad: float32 [1280, 1280], P('dp', 'mp')
- self_value_grad: float32 [1280, 1280], P('dp', 'mp')
- self_out_grad: float32 [1280, 1280], P('mp', 'dp')
- cross_query_grad: float32 [1280, 1280], P('dp', 'mp')
- cross_key_grad: float32 [2048, 1280], P('dp', 'mp')
- cross_value_grad: float32 [2048, 1280], P('dp', 'mp')
- cross_out_grad: float32 [1280, 1280], P('mp', 'dp')
- ff_value_grad: float32 [1280, 5120], P('dp', 'mp')
- ff_gate_grad: float32 [1280, 5120], P('dp', 'mp')
- ff_down_grad: float32 [5120, 1280], P('mp', 'dp')
- gn_in_gain_grad: float32 [1280], P('dp')
- gn_mid_gain_grad: float32 [1280], P('dp')
- self_gain_grad: float32 [1280], P('dp')
- cross_gain_grad: float32 [1280], P('dp')
- ff_gain_grad: float32 [1280], P('dp')
Inputs may be any that keep to these rules, and one draw needn't show every extreme that they name: `item_count`: A data group's items stand in its first slots; one group holds 2 items and another one item.
All inputs are finite; a program needn't handle non-finite values.
Results may differ from a plain program's by a relative error of at most 0.025.
Values may be sent and summed in bfloat16 or wider, within the bound.
No kernel may reach another device: no remote copies, remote signals or barrier semaphores. Data moves between devices by JAX's collectives and lax.ppermute only.
A program may use at most 384 MiB of HBM per device.

v0:
```python
from functools import partial
import math

import jax
import jax.numpy as jnp
from jax import lax
from jax.sharding import PartitionSpec as P

C = 1280
HEAD_DIM = 64
GN_GROUPS = 32
SIDE = 16


highest = lax.Precision.HIGHEST


def fetch_weights(
    conv_in,
    conv_out,
    time_weight,
    self_query,
    self_key,
    self_value,
    self_out,
    cross_query,
    cross_key,
    cross_value,
    cross_out,
    ff_value,
    ff_gate,
    ff_down,
    gn_in_gain,
    gn_mid_gain,
    self_gain,
    cross_gain,
    ff_gain,
):
    weights_held = (
        lax.all_gather(conv_in, "dp", axis=2, tiled=True),
        lax.all_gather(conv_out, "dp", axis=3, tiled=True),
        lax.all_gather(time_weight, "dp", axis=0, tiled=True),
        lax.all_gather(self_query, "dp", axis=0, tiled=True),
        lax.all_gather(self_key, "dp", axis=0, tiled=True),
        lax.all_gather(self_value, "dp", axis=0, tiled=True),
        lax.all_gather(self_out, "dp", axis=1, tiled=True),
        lax.all_gather(cross_query, "dp", axis=0, tiled=True),
        lax.all_gather(cross_key, "dp", axis=0, tiled=True),
        lax.all_gather(cross_value, "dp", axis=0, tiled=True),
        lax.all_gather(cross_out, "dp", axis=1, tiled=True),
        lax.all_gather(ff_value, "dp", axis=0, tiled=True),
        lax.all_gather(ff_gate, "dp", axis=0, tiled=True),
        lax.all_gather(ff_down, "dp", axis=1, tiled=True),
        lax.all_gather(gn_in_gain, "dp", axis=0, tiled=True),
        lax.all_gather(gn_mid_gain, "dp", axis=0, tiled=True),
        lax.all_gather(self_gain, "dp", axis=0, tiled=True),
        lax.all_gather(cross_gain, "dp", axis=0, tiled=True),
        lax.all_gather(ff_gain, "dp", axis=0, tiled=True),
    )
    whole_pair = (weights_held[6], weights_held[10])
    return (weights_held, whole_pair)


def gather_rows(values):
    return lax.all_gather(values, "mp", axis=1, tiled=True)


def sum_rows(values):
    return lax.psum_scatter(
        values.astype(jnp.bfloat16), "mp", scatter_dimension=1, tiled=True
    ).astype(jnp.float32)


def product(former, latter):
    return jnp.einsum("sna,ab->snb", former, latter, preferred_element_type=jnp.float32)


def product_back(former, latter):
    return jnp.einsum("snb,ab->sna", former, latter, preferred_element_type=jnp.float32)


def weight_grad(former, latter):
    return jnp.einsum("sna,snb->ab", former, latter, preferred_element_type=jnp.float32)


def step_embedding(steps):
    half_width = C // 2
    frequencies = jnp.exp(
        -math.log(10000.0) * jnp.arange(half_width, dtype=jnp.float32) / half_width
    )
    angles = steps.astype(jnp.float32)[:, None] * frequencies[None, :]
    return jnp.concatenate([jnp.cos(angles), jnp.sin(angles)], axis=1)


def pad_rows(values):
    return jnp.pad(values, ((0, 0), (2 * SIDE, 2 * SIDE), (0, 0)))


def tap_slices(padded, widths, row_step, column_step, item_rows):
    shift_start = 2 * SIDE + (row_step - 1) * widths + (column_step - 1)
    pieces = [
        lax.dynamic_slice_in_dim(padded[number], shift_start[number], item_rows, 0)
        for number in range(padded.shape[0])
    ]
    column = jnp.arange(item_rows, dtype=jnp.int32)[None, :] % widths[:, None] + (column_step - 1)
    usable = (column >= 0) & (column < widths[:, None])
    return jnp.where(usable[:, :, None], jnp.stack(pieces), jnp.zeros((), padded.dtype))


def convolve(values, kernel, widths):
    padded = pad_rows(values)
    summed = jnp.zeros(values.shape[:2] + (kernel.shape[3],), jnp.float32)
    for row_step in range(3):
        for column_step in range(3):
            summed = summed + product(
                tap_slices(padded, widths, row_step, column_step, values.shape[1]),
                kernel[row_step, column_step],
            )
    return summed


def kernel_grad(values, gradient, widths):
    padded = pad_rows(values)
    rows_of_taps = []
    for row_step in range(3):
        taps_here = [
            weight_grad(
                tap_slices(padded, widths, row_step, column_step, values.shape[1]), gradient
            )
            for column_step in range(3)
        ]
        rows_of_taps.append(jnp.stack(taps_here))
    return jnp.stack(rows_of_taps)


def convolve_back(gradient, kernel, widths):
    item_rows = gradient.shape[1]
    column = jnp.arange(item_rows, dtype=jnp.int32)[None, :] % widths[:, None]
    summed = jnp.zeros(gradient.shape[:2] + (kernel.shape[2],), jnp.float32)
    for column_step in range(3):
        usable = (column + column_step - 1 >= 0) & (column + column_step - 1 < widths[:, None])
        padded = pad_rows(jnp.where(usable[:, :, None], gradient, jnp.zeros((), gradient.dtype)))
        for row_step in range(3):
            back_start = 2 * SIDE - (row_step - 1) * widths - (column_step - 1)
            pieces = [
                lax.dynamic_slice_in_dim(padded[number], back_start[number], item_rows, 0)
                for number in range(gradient.shape[0])
            ]
            summed = summed + product_back(jnp.stack(pieces), kernel[row_step, column_step])
    return summed


def norm_rows(hidden, factor):
    center = hidden - jnp.mean(hidden, axis=-1, keepdims=True)
    scaling = lax.rsqrt(jnp.mean(center * center, axis=-1, keepdims=True) + 1e-05)
    normal = center * scaling
    return ((normal * factor).astype(jnp.bfloat16), normal, scaling)


def norm_rows_back(gradient, normal, scaling, factor):
    scaled = gradient * factor
    offset = jnp.mean(scaled, axis=-1, keepdims=True)
    slopes = jnp.mean(scaled * normal, axis=-1, keepdims=True)
    return (scaling * (scaled - offset - normal * slopes), jnp.sum(gradient * normal, axis=(0, 1)))


def group_view(values, per_group):
    return values.reshape(values.shape[0], values.shape[1], values.shape[2] // per_group, per_group)


def activation_back(gradient, standard, factor, row_mask):
    scaled = standard * factor
    activated, pullback = jax.vjp(jax.nn.silu, scaled)
    scaled_grad = pullback(gradient * row_mask[:, :, None])[0]
    return (scaled_grad * factor, jnp.sum(scaled_grad * standard, axis=(0, 1)))


def split_heads(values):
    return values.reshape(values.shape[0], values.shape[1], values.shape[2] // HEAD_DIM, HEAD_DIM)


def scores_of(query_heads, key_heads, key_valid):
    scores = jnp.einsum(
        "sqhd,skhd->shqk", query_heads, key_heads, preferred_element_type=jnp.float32
    ) * HEAD_DIM ** (-0.5)
    return jnp.where(key_valid[:, None, None, :], scores, -1e30)


def attend(query_rows, key_rows, value_rows, key_valid):
    scores = scores_of(split_heads(query_rows), split_heads(key_rows), key_valid)
    maximum = jnp.max(scores, axis=-1, keepdims=True)
    exponent = jnp.exp(scores - maximum)
    totals = jnp.sum(exponent, axis=-1, keepdims=True)
    shares = (exponent / totals).astype(jnp.bfloat16)
    mixture = jnp.einsum(
        "shqk,skhd->sqhd", shares, split_heads(value_rows), preferred_element_type=jnp.float32
    )
    return (
        mixture.reshape(query_rows.shape).astype(jnp.bfloat16),
        maximum[..., 0] + jnp.log(totals[..., 0]),
    )


def attend_back(query_rows, key_rows, value_rows, mixture_grad, logsum, key_valid):
    query_heads = split_heads(query_rows)
    key_heads = split_heads(key_rows)
    value_heads = split_heads(value_rows)
    scores = scores_of(query_heads, key_heads, key_valid)
    chances = jnp.exp(scores - logsum[..., None])
    grad_heads = split_heads(mixture_grad)
    value_grad = jnp.einsum(
        "shqk,sqhd->skhd",
        chances.astype(jnp.bfloat16),
        grad_heads,
        preferred_element_type=jnp.float32,
    )
    share_grad = jnp.einsum(
        "sqhd,skhd->shqk", grad_heads, value_heads, preferred_element_type=jnp.float32
    )
    inner_sum = jnp.sum(chances * share_grad, axis=-1, keepdims=True)
    score_grad = (chances * (share_grad - inner_sum)).astype(jnp.bfloat16)
    query_grad = jnp.einsum(
        "shqk,skhd->sqhd", score_grad, key_heads, preferred_element_type=jnp.float32
    ) * HEAD_DIM ** (-0.5)
    key_grad = jnp.einsum(
        "shqk,sqhd->skhd", score_grad, query_heads, preferred_element_type=jnp.float32
    ) * HEAD_DIM ** (-0.5)
    return (
        query_grad.reshape(query_rows.shape).astype(jnp.bfloat16),
        key_grad.reshape(key_rows.shape).astype(jnp.bfloat16),
        value_grad.reshape(value_rows.shape).astype(jnp.bfloat16),
    )


def out_project(mixture, out_rows):
    return (mixture, sum_rows(product(mixture, out_rows)))


def out_back(branch, mixture, out_rows):
    branch_all = gather_rows(branch)
    return (
        weight_grad(mixture, branch_all),
        product_back(branch_all, out_rows).astype(jnp.bfloat16),
    )


def body(
    latent,
    text_embeds,
    cotangent,
    item_count,
    bucket,
    timestep,
    conv_in,
    conv_out,
    time_weight,
    self_query,
    self_key,
    self_value,
    self_out,
    cross_query,
    cross_key,
    cross_value,
    cross_out,
    ff_value,
    ff_gate,
    ff_down,
    gn_in_gain,
    gn_mid_gain,
    self_gain,
    cross_gain,
    ff_gain,
):
    slot_count, local_rows, channels = latent.shape
    item_rows = local_rows * lax.axis_size("mp")
    per_group = channels // GN_GROUPS
    own_channels = conv_in.shape[3]
    is_live = (jnp.arange(slot_count, dtype=jnp.int32) < item_count[0]).astype(jnp.float32)
    widths = jnp.where(
        bucket == 0, SIDE, jnp.where(bucket == 1, 5 * SIDE // 4, 3 * SIDE // 2)
    ).astype(jnp.int32)
    heights = jnp.where(
        bucket == 0, SIDE, jnp.where(bucket == 1, 3 * SIDE // 4, 5 * SIDE // 8)
    ).astype(jnp.int32)
    filled = widths * heights
    position = lax.axis_index("mp") * local_rows + jnp.arange(local_rows, dtype=jnp.int32)
    row_mask = (position[None, :] < filled[:, None]).astype(jnp.float32) * is_live[:, None]
    key_valid = jnp.arange(item_rows, dtype=jnp.int32)[None, :] < filled[:, None]
    full_mask = key_valid.astype(jnp.float32) * is_live[:, None]
    every_token = jnp.ones((slot_count, text_embeds.shape[1]), dtype=jnp.bool_)
    counts = filled.astype(jnp.float32) * per_group
    time_act = jax.nn.silu(step_embedding(timestep)).astype(jnp.bfloat16)
    channel_start = lax.axis_index("mp") * own_channels
    weights_held, whole_pair = fetch_weights(
        conv_in,
        conv_out,
        time_weight,
        self_query,
        self_key,
        self_value,
        self_out,
        cross_query,
        cross_key,
        cross_value,
        cross_out,
        ff_value,
        ff_gate,
        ff_down,
        gn_in_gain,
        gn_mid_gain,
        self_gain,
        cross_gain,
        ff_gain,
    )
    (
        kernel_in,
        kernel_out,
        time_full,
        sq_full,
        sk_full,
        sv_full,
        so_full,
        cq_full,
        ck_full,
        cv_full,
        co_full,
        fv_full,
        fg_full,
        fd_full,
        gain_in,
        gain_mid,
        gain_self,
        gain_cross,
        gain_feed,
    ) = weights_held
    gain_in_f = gain_in.astype(jnp.float32)
    gain_self_f = gain_self.astype(jnp.float32)
    gain_cross_f = gain_cross.astype(jnp.float32)
    gain_feed_f = gain_feed.astype(jnp.float32)
    gain_mid_own = lax.dynamic_slice_in_dim(
        gain_mid.astype(jnp.float32), channel_start, own_channels
    )
    masked = latent.astype(jnp.float32) * row_mask[:, :, None]
    grouped = group_view(masked, per_group)
    average = lax.psum(jnp.sum(grouped, axis=(1, 3)), "mp") / counts[:, None]
    center = (grouped - average[:, None, :, None]) * row_mask[:, :, None, None]
    variance = lax.psum(jnp.sum(center * center, axis=(1, 3)), "mp") / counts[:, None]
    scaling_in = lax.rsqrt(variance + 1e-06)
    standard_in = ((grouped - average[:, None, :, None]) * scaling_in[:, None, :, None]).reshape(
        masked.shape
    )
    first_act = (jax.nn.silu(standard_in * gain_in_f) * row_mask[:, :, None]).astype(jnp.bfloat16)
    first_all = gather_rows(first_act)
    time_added = jnp.einsum("sa,ab->sb", time_act, time_full, preferred_element_type=jnp.float32)
    middle = (convolve(first_all, kernel_in, widths) + time_added[:, None, :]) * full_mask[
        :, :, None
    ]
    grouped_mid = group_view(middle, per_group)
    average_mid = jnp.sum(grouped_mid, axis=(1, 3)) / counts[:, None]
    center_mid = (grouped_mid - average_mid[:, None, :, None]) * full_mask[:, :, None, None]
    scaling_mid = lax.rsqrt(jnp.sum(center_mid * center_mid, axis=(1, 3)) / counts[:, None] + 1e-06)
    standard_mid = (
        (grouped_mid - average_mid[:, None, :, None]) * scaling_mid[:, None, :, None]
    ).reshape(middle.shape)
    second_act = (jax.nn.silu(standard_mid * gain_mid_own) * full_mask[:, :, None]).astype(
        jnp.bfloat16
    )
    resnet = (masked + sum_rows(convolve(second_act, kernel_out, widths))) * row_mask[:, :, None]
    attend_in, normal_self, scaling_self = norm_rows(resnet, gain_self_f)
    attend_all = gather_rows(attend_in)
    query_rows = product(attend_all, sq_full).astype(jnp.bfloat16)
    key_rows = product(attend_all, sk_full).astype(jnp.bfloat16)
    value_rows = product(attend_all, sv_full).astype(jnp.bfloat16)
    mixture, self_logsum = attend(query_rows, key_rows, value_rows, key_valid)
    self_kept, self_added = out_project(mixture, so_full)
    after_self = resnet + self_added
    cross_in, normal_cross, scaling_cross = norm_rows(after_self, gain_cross_f)
    cross_all = gather_rows(cross_in)
    cross_rows = product(cross_all, cq_full).astype(jnp.bfloat16)
    text_keys = product(text_embeds, ck_full).astype(jnp.bfloat16)
    text_values = product(text_embeds, cv_full).astype(jnp.bfloat16)
    cross_mix, cross_logsum = attend(cross_rows, text_keys, text_values, every_token)
    cross_kept, cross_added = out_project(cross_mix, co_full)
    after_cross = after_self + cross_added
    feed_in, normal_feed, scaling_feed = norm_rows(after_cross, gain_feed_f)
    feed_all = gather_rows(feed_in)
    value_part = product(feed_all, fv_full)
    gate_part = product(feed_all, fg_full)
    gelu_gate, gelu_pull = jax.vjp(partial(jax.nn.gelu, approximate=False), gate_part)
    hidden = (value_part * gelu_gate).astype(jnp.bfloat16)
    output = ((after_cross + sum_rows(product(hidden, fd_full))) * row_mask[:, :, None]).astype(
        jnp.bfloat16
    )
    weights_held, whole_pair = fetch_weights(
        conv_in,
        conv_out,
        time_weight,
        self_query,
        self_key,
        self_value,
        self_out,
        cross_query,
        cross_key,
        cross_value,
        cross_out,
        ff_value,
        ff_gate,
        ff_down,
        gn_in_gain,
        gn_mid_gain,
        self_gain,
        cross_gain,
        ff_gain,
    )
    (
        kernel_in,
        kernel_out,
        time_full,
        sq_full,
        sk_full,
        sv_full,
        so_full,
        cq_full,
        ck_full,
        cv_full,
        co_full,
        fv_full,
        fg_full,
        fd_full,
        gain_in,
        gain_mid,
        gain_self,
        gain_cross,
        gain_feed,
    ) = weights_held
    out_grad = cotangent.astype(jnp.float32) * row_mask[:, :, None]
    feed_branch = gather_rows(out_grad.astype(jnp.bfloat16))
    grad_down = weight_grad(hidden, feed_branch)
    hidden_grad = product_back(feed_branch, fd_full)
    value_grad = (hidden_grad * gelu_gate).astype(jnp.bfloat16)
    gate_grad = gelu_pull(hidden_grad * value_part)[0].astype(jnp.bfloat16)
    grad_ff_value = weight_grad(feed_all, value_grad)
    grad_ff_gate = weight_grad(feed_all, gate_grad)
    feed_back = sum_rows(product_back(value_grad, fv_full) + product_back(gate_grad, fg_full))
    feed_dv, grad_gain_feed = norm_rows_back(feed_back, normal_feed, scaling_feed, gain_feed_f)
    cross_grad = out_grad + feed_dv
    grad_cross_out, cross_mix_grad = out_back(cross_grad.astype(jnp.bfloat16), cross_mix, co_full)
    cross_dq, cross_dk, cross_dv = attend_back(
        cross_rows, text_keys, text_values, cross_mix_grad, cross_logsum, every_token
    )
    grad_cross_query = weight_grad(cross_all, cross_dq)
    grad_cross_key = weight_grad(text_embeds, cross_dk)
    grad_cross_value = weight_grad(text_embeds, cross_dv)
    cross_back = sum_rows(product_back(cross_dq, cq_full))
    cross_dv_rows, grad_gain_cross = norm_rows_back(
        cross_back, normal_cross, scaling_cross, gain_cross_f
    )
    self_grad = cross_grad + cross_dv_rows
    grad_self_out, mixture_grad = out_back(self_grad.astype(jnp.bfloat16), mixture, so_full)
    self_dq, self_dk, self_dv = attend_back(
        query_rows, key_rows, value_rows, mixture_grad, self_logsum, key_valid
    )
    grad_query = weight_grad(attend_all, self_dq)
    grad_key = weight_grad(attend_all, self_dk)
    grad_value = weight_grad(attend_all, self_dv)
    self_back = sum_rows(
        product_back(self_dq, sq_full)
        + product_back(self_dk, sk_full)
        + product_back(self_dv, sv_full)
    )
    self_dv_rows, grad_gain_self = norm_rows_back(self_back, normal_self, scaling_self, gain_self_f)
    resnet_grad = self_grad + self_dv_rows
    resnet_branch = gather_rows((resnet_grad * row_mask[:, :, None]).astype(jnp.bfloat16))
    grad_kernel_out = kernel_grad(second_act, resnet_branch, widths)
    second_grad = convolve_back(resnet_branch, kernel_out, widths)
    mid_hat, mid_gain_part = activation_back(second_grad, standard_mid, gain_mid_own, full_mask)
    hat_mid = group_view(mid_hat, per_group)
    standard_mid_grouped = group_view(standard_mid, per_group)
    mid_offset = jnp.sum(hat_mid, axis=(1, 3))
    mid_slope = jnp.sum(hat_mid * standard_mid_grouped, axis=(1, 3))
    middle_grad = scaling_mid[:, None, :, None] * (
        hat_mid
        - (mid_offset[:, None, :, None] + standard_mid_grouped * mid_slope[:, None, :, None])
        / counts[:, None, None, None]
    )
    middle_grad = (middle_grad.reshape(middle.shape) * full_mask[:, :, None]).astype(jnp.bfloat16)
    time_sum = jnp.sum(middle_grad.astype(jnp.float32), axis=1)
    grad_time = jnp.einsum(
        "sa,sb->ab",
        time_act.astype(jnp.float32),
        time_sum,
        precision=highest,
        preferred_element_type=jnp.float32,
    )
    grad_kernel_in = kernel_grad(first_all, middle_grad, widths)
    first_grad = sum_rows(convolve_back(middle_grad, kernel_in, widths))
    in_hat, in_gain_part = activation_back(first_grad, standard_in, gain_in_f, row_mask)
    hat_in = group_view(in_hat, per_group)
    standard_in_grouped = group_view(standard_in, per_group)
    mid_gain_whole = lax.dynamic_update_slice_in_dim(
        jnp.zeros((channels,), jnp.float32), mid_gain_part, channel_start, 0
    )
    (
        offset_sum,
        slope_sum,
        sum_gain_in,
        sum_gain_mid,
        sum_gain_self,
        sum_gain_cross,
        sum_gain_feed,
    ) = lax.psum(
        (
            jnp.sum(hat_in, axis=(1, 3)),
            jnp.sum(hat_in * standard_in_grouped, axis=(1, 3)),
            in_gain_part,
            mid_gain_whole,
            grad_gain_self,
            grad_gain_cross,
            grad_gain_feed,
        ),
        "mp",
    )
    grouped_grad = scaling_in[:, None, :, None] * (
        hat_in
        - (offset_sum[:, None, :, None] + standard_in_grouped * slope_sum[:, None, :, None])
        / counts[:, None, None, None]
    )
    latent_grad = (
        (resnet_grad * row_mask[:, :, None] + grouped_grad.reshape(masked.shape))
        * row_mask[:, :, None]
    ).astype(jnp.bfloat16)
    sums = (
        lax.psum_scatter(grad_kernel_in, "dp", scatter_dimension=2, tiled=True),
        lax.psum_scatter(grad_kernel_out, "dp", scatter_dimension=3, tiled=True),
        lax.psum_scatter(grad_time, "dp", scatter_dimension=0, tiled=True),
        lax.psum_scatter(grad_query, "dp", scatter_dimension=0, tiled=True),
        lax.psum_scatter(grad_key, "dp", scatter_dimension=0, tiled=True),
        lax.psum_scatter(grad_value, "dp", scatter_dimension=0, tiled=True),
        lax.psum_scatter(grad_self_out, "dp", scatter_dimension=1, tiled=True),
        lax.psum_scatter(grad_cross_query, "dp", scatter_dimension=0, tiled=True),
        lax.psum_scatter(grad_cross_key, "dp", scatter_dimension=0, tiled=True),
        lax.psum_scatter(grad_cross_value, "dp", scatter_dimension=0, tiled=True),
        lax.psum_scatter(grad_cross_out, "dp", scatter_dimension=1, tiled=True),
        lax.psum_scatter(grad_ff_value, "dp", scatter_dimension=0, tiled=True),
        lax.psum_scatter(grad_ff_gate, "dp", scatter_dimension=0, tiled=True),
        lax.psum_scatter(grad_down, "dp", scatter_dimension=1, tiled=True),
        lax.psum_scatter(sum_gain_in, "dp", scatter_dimension=0, tiled=True),
        lax.psum_scatter(sum_gain_mid, "dp", scatter_dimension=0, tiled=True),
        lax.psum_scatter(sum_gain_self, "dp", scatter_dimension=0, tiled=True),
        lax.psum_scatter(sum_gain_cross, "dp", scatter_dimension=0, tiled=True),
        lax.psum_scatter(sum_gain_feed, "dp", scatter_dimension=0, tiled=True),
    )
    return (
        output,
        latent_grad,
        sums[0],
        sums[1],
        sums[2],
        sums[3],
        sums[4],
        sums[5],
        sums[6],
        sums[7],
        sums[8],
        sums[9],
        sums[10],
        sums[11],
        sums[12],
        sums[13],
        sums[14],
        sums[15],
        sums[16],
        sums[17],
        sums[18],
    )


def solution(mesh):
    in_specs = (
        P("dp", "mp", None),
        P("dp", None, None),
        P("dp", "mp", None),
        P("dp"),
        P("dp"),
        P("dp"),
        P(None, None, "dp", "mp"),
        P(None, None, "mp", "dp"),
        P("dp", "mp"),
        P("dp", "mp"),
        P("dp", "mp"),
        P("dp", "mp"),
        P("mp", "dp"),
        P("dp", "mp"),
        P("dp", "mp"),
        P("dp", "mp"),
        P("mp", "dp"),
        P("dp", "mp"),
        P("dp", "mp"),
        P("mp", "dp"),
        P("dp"),
        P("dp"),
        P("dp"),
        P("dp"),
        P("dp"),
    )
    out_specs = (
        P("dp", "mp", None),
        P("dp", "mp", None),
        P(None, None, "dp", "mp"),
        P(None, None, "mp", "dp"),
        P("dp", "mp"),
        P("dp", "mp"),
        P("dp", "mp"),
        P("dp", "mp"),
        P("mp", "dp"),
        P("dp", "mp"),
        P("dp", "mp"),
        P("dp", "mp"),
        P("mp", "dp"),
        P("dp", "mp"),
        P("dp", "mp"),
        P("mp", "dp"),
        P("dp"),
        P("dp"),
        P("dp"),
        P("dp"),
        P("dp"),
    )
    return jax.shard_map(body, mesh=mesh, in_specs=in_specs, out_specs=out_specs, check_vma=False)
```

profile of v0, /device:TPU:0, one launch (start us, length us, event | category | flops | bytes accessed | tf_op | source)
XLA Modules:
  0.0 2797.5 jit_solution(7374803563149489693)
XLA Ops:
  16.1 38.8 %all-reduce.20 = (bf16[1280]{0:T(1024)(128)(2,1)S(1)}, bf16[1280]{0:T(1024)(128)(2,1)S(1)}, bf16[1280]{0:T(1024)(128)(2,1)S(1)}, bf16[1280]{0:T(1024)(128)(2,1)S(1)}, bf16[1280]{0:T(1024)(128)(2,1)S(1)}) all-reduce(bf16[1280]{0:T(1024)(128)(2,1)S(1)} %dynamic-update-slice.2, ...), channel_id=1, replica_groups=mesh['dp'=8,'mp'=4] {'dp'}, use_global_device_ids=true, to_apply=%add.10 | all-reduce | flops 6400 | bytes 25600
  56.8 5.6 psum.63
  64.1 6.6 psum.64
  101.6 36.0 %all_gather.95 = bf16[1280,320]{1,0:T(8,128)(2,1)S(1)} all-gather(bf16[160,320]{1,0:T(8,128)(2,1)S(1)} %copy-done.128), channel_id=1, replica_groups=mesh['dp'=8,'mp'=4] {'dp'}, dimensions={0}, use_global_device_ids=true | all-gather | bytes 921600 | tf_op jit(solution)/shard_map/all_gather | solution.py:42
  141.2 2.9 constant_dynamic-slice_fusion.36
  144.1 85.9 %all-gather.18.cloned.1.call-done = bf16[3,3,1280,320]{3,2,1,0:T(8,128)(2,1)} async-done(((bf16[3,3,160,320]{3,2,1,0:T(8,128)(2,1)}), bf16[3,3,1280,320]{3,2,1,0:T(8,128)(2,1)}) %all-gather.18.cloned.1.call-update) | async-done | bytes 7372816 | tf_op jit(solution)/shard_map/all_gather | solution.py:40
  245.1 116.2 %all-gather.20.cloned.1.call-done = bf16[3,3,320,1280]{2,3,1,0:T(8,128)(2,1)} async-done(((bf16[3,3,320,160]{2,3,1,0:T(8,128)(2,1)}), bf16[3,3,320,1280]{2,3,1,0:T(8,128)(2,1)}) %all-gather.20.cloned.1.call-update) | async-done | bytes 7372816 | tf_op jit(solution)/shard_map/all_gather | solution.py:41
  363.6 3.1 convolution_add_fusion.17
  374.8 24.8 reduce-scatter.27.cloned.1.call-done
  404.3 32.8 %all_gather.101 = bf16[1280,320]{1,0:T(8,128)(2,1)S(1)} all-gather(bf16[160,320]{1,0:T(8,128)(2,1)S(1)} %copy-done.129), channel_id=1, replica_groups=mesh['dp'=8,'mp'=4] {'dp'}, dimensions={0}, use_global_device_ids=true | all-gather | bytes 921600 | tf_op jit(solution)/shard_map/all_gather | solution.py:43
  437.1 32.5 %all_gather.102 = bf16[1280,320]{1,0:T(8,128)(2,1)S(1)} all-gather(bf16[160,320]{1,0:T(8,128)(2,1)S(1)} %copy-done.130), channel_id=1, replica_groups=mesh['dp'=8,'mp'=4] {'dp'}, dimensions={0}, use_global_device_ids=true | all-gather | bytes 921600 | tf_op jit(solution)/shard_map/all_gather | solution.py:44
  469.6 35.4 %all_gather.100 = bf16[1280,320]{1,0:T(8,128)(2,1)} all-gather(bf16[160,320]{1,0:T(8,128)(2,1)S(1)} %copy-done.131), channel_id=1, replica_groups=mesh['dp'=8,'mp'=4] {'dp'}, dimensions={0}, use_global_device_ids=true | all-gather | bytes 921600 | tf_op jit(solution)/shard_map/all_gather | solution.py:45
  505.0 34.1 %all_gather.103 = bf16[320,1280]{0,1:T(8,128)(2,1)} all-gather(bf16[320,160]{0,1:T(8,128)(2,1)S(1)} %copy-done.132), channel_id=1, replica_groups=mesh['dp'=8,'mp'=4] {'dp'}, dimensions={1}, use_global_device_ids=true | all-gather | bytes 921600 | tf_op jit(solution)/shard_map/all_gather | solution.py:46
  548.9 25.7 reduce-scatter.29.cloned.1.call-done
  578.5 36.0 %all_gather.107 = bf16[1280,320]{1,0:T(8,128)(2,1)} all-gather(bf16[160,320]{1,0:T(8,128)(2,1)S(1)} %copy-done.133), channel_id=1, replica_groups=mesh['dp'=8,'mp'=4] {'dp'}, dimensions={0}, use_global_device_ids=true | all-gather | bytes 921600 | tf_op jit(solution)/shard_map/all_gather | solution.py:47
  614.4 35.8 %all_gather.109 = bf16[320,1280]{0,1:T(8,128)(2,1)} all-gather(bf16[320,160]{0,1:T(8,128)(2,1)} %param.43), channel_id=1, replica_groups=mesh['dp'=8,'mp'=4] {'dp'}, dimensions={1}, use_global_device_ids=true | all-gather | bytes 921600 | tf_op jit(solution)/shard_map/all_gather | solution.py:50
  653.3 21.4 all-gather.28.cloned.1.call-done
  678.6 15.1 all-gather.26.cloned.1.call-done
  701.1 25.9 reduce-scatter.31.cloned.1.call-done
  732.0 59.4 %all-gather.32.cloned.1.call-done = bf16[1280,1280]{1,0:T(8,128)(2,1)} async-done(((bf16[160,1280]{1,0:T(8,128)(2,1)}), bf16[1280,1280]{1,0:T(8,128)(2,1)}) %all-gather.32.cloned.1.call-update) | async-done | bytes 3276816 | tf_op jit(solution)/shard_map/all_gather | solution.py:51
  791.4 18.9 all-gather.30.cloned.1.call-done
  810.3 5.7 fusion.11
  816.0 58.8 %all-gather.34.cloned.1.call-done = bf16[1280,1280]{1,0:T(8,128)(2,1)} async-done(((bf16[160,1280]{1,0:T(8,128)(2,1)}), bf16[1280,1280]{1,0:T(8,128)(2,1)}) %all-gather.34.cloned.1.call-update) | async-done | bytes 3276816 | tf_op jit(solution)/shard_map/all_gather | solution.py:52
  874.7 6.7 fusion.183
  881.4 56.2 %all-gather.36.cloned.1.call-done = bf16[1280,1280]{0,1:T(8,128)(2,1)} async-done(((bf16[1280,160]{0,1:T(8,128)(2,1)}), bf16[1280,1280]{0,1:T(8,128)(2,1)}) %all-gather.36.cloned.1.call-update) | async-done | bytes 3276816 | tf_op jit(solution)/shard_map/all_gather | solution.py:53
  937.6 18.9 all-gather.38.cloned.1.call-done
  956.5 11.3 add_convert_fusion
  972.7 3.0 fusion.19
  975.8 26.6 reduce-scatter.35.cloned.1.call-done
  1007.2 18.1 all-gather.40.cloned.1.call-done
  1031.9 5.3 fusion.13
  1037.3 21.2 reduce-scatter.37.cloned.1.call-done
  1060.6 27.7 reduce-scatter.33.cloned.1.call-done
  1088.3 3.3 fusion.320
  1091.8 18.3 all-gather.42.cloned.1.call-done
  1120.0 26.6 reduce-scatter.39.cloned.1.call-done
  1226.5 11.6 pad_maximum_fusion
  1238.0 24.7 copy.150
  1262.8 26.0 reshape.672
  1303.4 11.5 pad_maximum_fusion.1
  1314.9 24.9 copy.152
  1339.8 26.3 reshape.674
  1367.1 3.6 convolution_bitcast_fusion.3
  1387.3 6.0 convolution_bitcast_fusion.1
  1394.7 4.7 convolution_bitcast_fusion.2
  1401.0 4.6 convolution_bitcast_fusion
  1411.4 38.7 %all-reduce.18 = (f32[1280]{0:T(1024)S(1)}, f32[1280]{0:T(1024)S(1)}, f32[1280]{0:T(1024)S(1)}, f32[1280]{0:T(1024)S(1)}, f32[1280]{0:T(1024)S(1)}) all-reduce(f32[1280]{0:T(1024)S(1)} %get-tuple-element.108, f32[1280]{0:T(1024)S(1)} %dynamic_update_slice.3, f32[1280]{0:T(1024)S(1)} %copy-done.144, ...), channel_id=24, replica_groups=mesh['dp'=8,'mp'=4] {'dp'}, use_global_device_ids=true, to_apply=%region_63.65.clone | all-reduce | flops 6400 | bytes 51200
  1450.9 6.9 all-reduce.19
  1460.3 72.6 %reduce-scatter.67.cloned.1.call-done = f32[160,2880]{1,0:T(8,128)} async-done(((f32[1280,2880]{1,0:T(8,128)}), f32[160,2880]{1,0:T(8,128)}) %reduce-scatter.67.cloned.1.call-update) | async-done | bytes 1843216
  1532.9 3.3 reshape.673
  1537.8 239.9 %reduce-scatter.69.cloned.1.call-done = f32[160,2880]{1,0:T(8,128)} async-done(((f32[1280,2880]{1,0:T(8,128)}), f32[160,2880]{1,0:T(8,128)}) %reduce-scatter.69.cloned.1.call-update) | async-done | bytes 1843216
  1777.7 3.3 reshape.675
  1782.5 65.0 %reduce-scatter.59.cloned.1.call-done = f32[320,160]{0,1:T(8,128)} async-done(((f32[320,1280]{0,1:T(8,128)}), f32[320,160]{0,1:T(8,128)}) %reduce-scatter.59.cloned.1.call-update) | async-done | bytes 204816 | tf_op jit(solution)/shard_map/reduce_scatter | solution.py:543
  1847.5 70.3 %reduce-scatter.53.cloned.1.call-done = f32[160,320]{1,0:T(8,128)} async-done(((f32[1280,320]{1,0:T(8,128)}), f32[160,320]{1,0:T(8,128)}) %reduce-scatter.53.cloned.1.call-update) | async-done | bytes 204816 | tf_op jit(solution)/shard_map/reduce_scatter | solution.py:540
  1917.8 73.8 %reduce-scatter.55.cloned.1.call-done = f32[256,320]{0,1:T(8,128)} async-done(((f32[2048,320]{0,1:T(8,128)}), f32[256,320]{0,1:T(8,128)}) %reduce-scatter.55.cloned.1.call-update) | async-done | bytes 327696 | tf_op jit(solution)/shard_map/reduce_scatter | solution.py:541
  1991.7 73.8 %reduce-scatter.57.cloned.1.call-done = f32[256,320]{0,1:T(8,128)} async-done(((f32[2048,320]{0,1:T(8,128)}), f32[256,320]{0,1:T(8,128)}) %reduce-scatter.57.cloned.1.call-update) | async-done | bytes 327696 | tf_op jit(solution)/shard_map/reduce_scatter | solution.py:542
  2065.4 69.6 %reduce-scatter.51.cloned.1.call-done = f32[320,160]{0,1:T(8,128)} async-done(((f32[320,1280]{0,1:T(8,128)}), f32[320,160]{0,1:T(8,128)}) %reduce-scatter.51.cloned.1.call-update) | async-done | bytes 204816 | tf_op jit(solution)/shard_map/reduce_scatter | solution.py:539
  2135.1 70.3 %reduce-scatter.49.cloned.1.call-done = f32[160,320]{1,0:T(8,128)} async-done(((f32[1280,320]{1,0:T(8,128)}), f32[160,320]{1,0:T(8,128)}) %reduce-scatter.49.cloned.1.call-update) | async-done | bytes 204816 | tf_op jit(solution)/shard_map/reduce_scatter | solution.py:538
  2205.3 69.8 %reduce-scatter.47.cloned.1.call-done = f32[160,320]{1,0:T(8,128)} async-done(((f32[1280,320]{1,0:T(8,128)}), f32[160,320]{1,0:T(8,128)}) %reduce-scatter.47.cloned.1.call-update) | async-done | bytes 204816 | tf_op jit(solution)/shard_map/reduce_scatter | solution.py:537
  2275.1 70.1 %reduce-scatter.45.cloned.1.call-done = f32[160,320]{1,0:T(8,128)} async-done(((f32[1280,320]{1,0:T(8,128)}), f32[160,320]{1,0:T(8,128)}) %reduce-scatter.45.cloned.1.call-update) | async-done | bytes 204816 | tf_op jit(solution)/shard_map/reduce_scatter | solution.py:536
  2345.2 124.8 %reduce-scatter.63.cloned.1.call-done = f32[160,1280]{1,0:T(8,128)} async-done(((f32[1280,1280]{1,0:T(8,128)}), f32[160,1280]{1,0:T(8,128)}) %reduce-scatter.63.cloned.1.call-update) | async-done | bytes 819216 | tf_op jit(solution)/shard_map/reduce_scatter | solution.py:545
  2470.0 125.5 %reduce-scatter.61.cloned.1.call-done = f32[160,1280]{1,0:T(8,128)} async-done(((f32[1280,1280]{1,0:T(8,128)}), f32[160,1280]{1,0:T(8,128)}) %reduce-scatter.61.cloned.1.call-update) | async-done | bytes 819216 | tf_op jit(solution)/shard_map/reduce_scatter | solution.py:544
  2595.5 124.8 %reduce-scatter.65.cloned.1.call-done = f32[1280,160]{0,1:T(8,128)} async-done(((f32[1280,1280]{0,1:T(8,128)}), f32[1280,160]{0,1:T(8,128)}) %reduce-scatter.65.cloned.1.call-update) | async-done | bytes 819216 | tf_op jit(solution)/shard_map/reduce_scatter | solution.py:546
  2720.3 70.1 %reduce-scatter.43.cloned.1.call-done = f32[160,320]{1,0:T(8,128)} async-done(((f32[1280,320]{1,0:T(8,128)}), f32[160,320]{1,0:T(8,128)}) %reduce-scatter.43.cloned.1.call-update) | async-done | bytes 204816 | tf_op jit(solution)/shard_map/reduce_scatter | solution.py:535
  (702 shorter events, 214.5 us)
Async XLA Ops:
  7.2 94.4 %copy-start.128 = (bf16[160,320]{1,0:T(8,128)(2,1)S(1)}, bf16[160,320]{1,0:T(8,128)(2,1)}, u32[]{:S(2)}) copy-start(bf16[160,320]{1,0:T(8,128)(2,1)} %param.35) | copy-start | bytes 307204
  7.2 130.7 %all-gather.16.cloned.1.call-start = ((), (), s32[]{:S(2)}) async-start(), calls=%async_computation.22 | async-start | bytes 1638400 | tf_op jit(solution)/shard_map/all_gather | solution.py:65
  9.8 233.5 %copy-start.156 = (f32[2]{0:T(128)}, f32[2]{0:T(128)S(1)}, u32[]{:S(2)}) copy-start(f32[2]{0:T(128)S(1)} %get-tuple-element.151) | copy-start | bytes 28
  73.1 157.0 %all-gather.18.cloned.1.call-start = ((), (), s32[]{:S(2)}) async-start(), calls=%async_computation.23 | async-start | bytes 9953280 | tf_op jit(solution)/shard_map/all_gather | solution.py:40
  73.8 287.5 %all-gather.20.cloned.1.call-start = ((), (), s32[]{:S(2)}) async-start(), calls=%async_computation.24 | async-start | bytes 9953280 | tf_op jit(solution)/shard_map/all_gather | solution.py:41
  74.5 325.0 %reduce-scatter.27.cloned.1.call-start = ((), (), s32[]{:S(2)}) async-start(), calls=%async_computation.25 | async-start | bytes 1638400 | tf_op jit(solution)/shard_map/reduce_scatter | solution.py:69
  101.1 142.4 %copy-start.159 = (f32[320]{0:T(512)}, f32[320]{0:T(512)S(1)}, u32[]{:S(2)}) copy-start(f32[320]{0:T(512)S(1)} %dynamic-slice_convert_fusion) | copy-start | bytes 3844
  101.2 142.3 %copy-start.145 = (f32[2,256]{1,0:T(2,128)}, f32[2,256]{1,0:T(2,128)S(1)}, u32[]{:S(2)}) copy-start(f32[2,256]{1,0:T(2,128)S(1)} %broadcast_select_fusion.12) | copy-start | bytes 6148
  141.1 97.7 %copy-start.100 = (bf16[1,256,1280]{2,1,0:T(8,128)(2,1)}, bf16[1,256,1280]{2,1,0:T(8,128)(2,1)S(1)}, u32[]{:S(2)}) copy-start(bf16[1,256,1280]{2,1,0:T(8,128)(2,1)S(1)} %get-tuple-element.180) | copy-start | bytes 1966084
  141.1 98.8 %copy-start.98 = (bf16[1,256,1280]{2,1,0:T(8,128)(2,1)}, bf16[1,256,1280]{2,1,0:T(8,128)(2,1)S(1)}, u32[]{:S(2)}) copy-start(bf16[1,256,1280]{2,1,0:T(8,128)(2,1)S(1)} %get-tuple-element.179) | copy-start | bytes 1966084
  141.1 99.9 %copy-start.96 = (bf16[1,256,1280]{2,1,0:T(8,128)(2,1)}, bf16[1,256,1280]{2,1,0:T(8,128)(2,1)S(1)}, u32[]{:S(2)}) copy-start(bf16[1,256,1280]{2,1,0:T(8,128)(2,1)S(1)} %get-tuple-element.178) | copy-start | bytes 1966084
  243.9 125.8 %copy-start.5 = (bf16[2,256,320]{1,2,0:T(8,128)(2,1)}, bf16[2,256,320]{1,2,0:T(8,128)(2,1)S(1)}, u32[]{:S(2)}) copy-start(bf16[2,256,320]{1,2,0:T(8,128)(2,1)S(1)} %multiply_convert_fusion.10) | copy-start | bytes 983044
  244.5 119.0 %copy-start.51 = (bf16[1,256,320]{1,2,0:T(8,128)(2,1)}, bf16[1,256,320]{1,2,0:T(8,128)(2,1)S(1)}, u32[]{:S(2)}) copy-start(bf16[1,256,320]{1,2,0:T(8,128)(2,1)S(1)} %get-tuple-element.219) | copy-start | bytes 491524
  244.6 119.0 %copy-start.53 = (bf16[1,256,320]{1,2,0:T(8,128)(2,1)}, bf16[1,256,320]{1,2,0:T(8,128)(2,1)S(1)}, u32[]{:S(2)}) copy-start(bf16[1,256,320]{1,2,0:T(8,128)(2,1)S(1)} %get-tuple-element.218) | copy-start | bytes 491524
  244.6 122.1 %copy-start.55 = (bf16[1,256,320]{1,2,0:T(8,128)(2,1)}, bf16[1,256,320]{1,2,0:T(8,128)(2,1)S(1)}, u32[]{:S(2)}) copy-start(bf16[1,256,320]{1,2,0:T(8,128)(2,1)S(1)} %get-tuple-element.217) | copy-start | bytes 491524
  244.6 126.2 %copy-start.57 = (bf16[1,256,320]{1,2,0:T(8,128)(2,1)}, bf16[1,256,320]{1,2,0:T(8,128)(2,1)S(1)}, u32[]{:S(2)}) copy-start(bf16[1,256,320]{1,2,0:T(8,128)(2,1)S(1)} %get-tuple-element.216) | copy-start | bytes 491524
  244.6 127.2 %copy-start.47 = (bf16[1,256,320]{1,2,0:T(8,128)(2,1)}, bf16[1,256,320]{1,2,0:T(8,128)(2,1)S(1)}, u32[]{:S(2)}) copy-start(bf16[1,256,320]{1,2,0:T(8,128)(2,1)S(1)} %get-tuple-element.215) | copy-start | bytes 491524
  244.6 128.1 %copy-start.49 = (bf16[1,256,320]{1,2,0:T(8,128)(2,1)}, bf16[1,256,320]{1,2,0:T(8,128)(2,1)S(1)}, u32[]{:S(2)}) copy-start(bf16[1,256,320]{1,2,0:T(8,128)(2,1)S(1)} %get-tuple-element.214) | copy-start | bytes 491524
  245.0 121.6 %copy-start.63 = (bf16[1,256,320]{1,2,0:T(8,128)(2,1)}, bf16[1,256,320]{1,2,0:T(8,128)(2,1)S(1)}, u32[]{:S(2)}) copy-start(bf16[1,256,320]{1,2,0:T(8,128)(2,1)S(1)} %get-tuple-element.225) | copy-start | bytes 491524
  245.1 121.6 %copy-start.65 = (bf16[1,256,320]{1,2,0:T(8,128)(2,1)}, bf16[1,256,320]{1,2,0:T(8,128)(2,1)S(1)}, u32[]{:S(2)}) copy-start(bf16[1,256,320]{1,2,0:T(8,128)(2,1)S(1)} %get-tuple-element.224) | copy-start | bytes 491524
  245.1 121.6 %copy-start.67 = (bf16[1,256,320]{1,2,0:T(8,128)(2,1)}, bf16[1,256,320]{1,2,0:T(8,128)(2,1)S(1)}, u32[]{:S(2)}) copy-start(bf16[1,256,320]{1,2,0:T(8,128)(2,1)S(1)} %get-tuple-element.223) | copy-start | bytes 491524
  245.1 125.8 %copy-start.69 = (bf16[1,256,320]{1,2,0:T(8,128)(2,1)}, bf16[1,256,320]{1,2,0:T(8,128)(2,1)S(1)}, u32[]{:S(2)}) copy-start(bf16[1,256,320]{1,2,0:T(8,128)(2,1)S(1)} %get-tuple-element.222) | copy-start | bytes 491524
  245.1 126.7 %copy-start.59 = (bf16[1,256,320]{1,2,0:T(8,128)(2,1)}, bf16[1,256,320]{1,2,0:T(8,128)(2,1)S(1)}, u32[]{:S(2)}) copy-start(bf16[1,256,320]{1,2,0:T(8,128)(2,1)S(1)} %get-tuple-element.221) | copy-start | bytes 491524
  245.1 127.6 %copy-start.61 = (bf16[1,256,320]{1,2,0:T(8,128)(2,1)}, bf16[1,256,320]{1,2,0:T(8,128)(2,1)S(1)}, u32[]{:S(2)}) copy-start(bf16[1,256,320]{1,2,0:T(8,128)(2,1)S(1)} %get-tuple-element.220) | copy-start | bytes 491524
  374.7 94.9 %copy-start.131 = (bf16[160,320]{1,0:T(8,128)(2,1)S(1)}, bf16[160,320]{1,0:T(8,128)(2,1)}, u32[]{:S(2)}) copy-start(bf16[160,320]{1,0:T(8,128)(2,1)} %param.38) | copy-start | bytes 307204
  374.7 164.4 %all-gather.22.cloned.1.call-start = ((), (), s32[]{:S(2)}) async-start(), calls=%async_computation.26 | async-start | bytes 1638400 | tf_op jit(solution)/shard_map/all_gather | solution.py:65
  374.8 773.8 %copy-start.122 = (f32[1280]{0:T(1024)}, f32[1280]{0:T(1024)S(1)}, u32[]{:S(2)}) copy-start(f32[1280]{0:T(1024)S(1)} %convert_element_type.273) | copy-start | bytes 15364
  400.8 747.8 %copy-start.140 = (f32[2,64]{1,0:T(2,128)}, f32[2,64]{1,0:T(2,128)S(1)}, u32[]{:S(2)}) copy-start(f32[2,64]{1,0:T(2,128)S(1)} %broadcast_multiply_fusion.8) | copy-start | bytes 1540
  400.9 104.1 %copy-start.132 = (bf16[320,160]{0,1:T(8,128)(2,1)S(1)}, bf16[320,160]{0,1:T(8,128)(2,1)}, u32[]{:S(2)}) copy-start(bf16[320,160]{0,1:T(8,128)(2,1)} %param.39) | copy-start | bytes 307204
  402.2 136.9 %copy-start.149 = (f32[2,64]{1,0:T(2,128)}, f32[2,64]{1,0:T(2,128)S(1)}, u32[]{:S(2)}) copy-start(f32[2,64]{1,0:T(2,128)S(1)} %add_rsqrt_fusion.2) | copy-start | bytes 1540
  404.2 170.3 %reduce-scatter.29.cloned.1.call-start = ((), (), s32[]{:S(2)}) async-start(), calls=%async_computation.27 | async-start | bytes 1638400 | tf_op jit(solution)/shard_map/reduce_scatter | solution.py:69
  437.1 104.1 %copy-start.27 = (bf16[1280,320]{1,0:T(8,128)(2,1)}, bf16[1280,320]{1,0:T(8,128)(2,1)S(1)}, u32[]{:S(2)}) copy-start(bf16[1280,320]{1,0:T(8,128)(2,1)S(1)} %all_gather.101) | copy-start | bytes 2457604
  547.3 103.0 %all-gather.24.cloned.1.call-start = ((), (), s32[]{:S(2)}) async-start(), calls=%async_computation.28 | async-start | bytes 1474560 | tf_op jit(solution)/shard_map/all_gather | solution.py:49
  548.1 126.6 %all-gather.28.cloned.1.call-start = ((), (), s32[]{:S(2)}) async-start(), calls=%async_computation.30 | async-start | bytes 1474560 | tf_op jit(solution)/shard_map/all_gather | solution.py:48
  548.8 144.9 %all-gather.26.cloned.1.call-start = ((), (), s32[]{:S(2)}) async-start(), calls=%async_computation.29 | async-start | bytes 1638400 | tf_op jit(solution)/shard_map/all_gather | solution.py:65
  578.4 148.6 %reduce-scatter.31.cloned.1.call-start = ((), (), s32[]{:S(2)}) async-start(), calls=%async_computation.31 | async-start | bytes 1638400 | tf_op jit(solution)/shard_map/reduce_scatter | solution.py:69
  700.3 91.1 %all-gather.32.cloned.1.call-start = ((), (), s32[]{:S(2)}) async-start(), calls=%async_computation.33 | async-start | bytes 3686400 | tf_op jit(solution)/shard_map/all_gather | solution.py:51
  701.0 109.3 %all-gather.30.cloned.1.call-start = ((), (), s32[]{:S(2)}) async-start(), calls=%async_computation.32 | async-start | bytes 1638400 | tf_op jit(solution)/shard_map/all_gather | solution.py:65
  729.2 275.4 %copy-start.154 = (f32[2,64]{1,0:T(2,128)}, f32[2,64]{1,0:T(2,128)S(1)}, u32[]{:S(2)}) copy-start(f32[2,64]{1,0:T(2,128)S(1)} %add_rsqrt_fusion) | copy-start | bytes 1540
  730.1 144.7 %all-gather.34.cloned.1.call-start = ((), (), s32[]{:S(2)}) async-start(), calls=%async_computation.34 | async-start | bytes 3686400 | tf_op jit(solution)/shard_map/all_gather | solution.py:52
  730.8 206.8 %all-gather.36.cloned.1.call-start = ((), (), s32[]{:S(2)}) async-start(), calls=%async_computation.35 | async-start | bytes 3686400 | tf_op jit(solution)/shard_map/all_gather | solution.py:53
  731.4 225.1 %all-gather.38.cloned.1.call-start = ((), (), s32[]{:S(2)}) async-start(), calls=%async_computation.37 | async-start | bytes 1638400 | tf_op jit(solution)/shard_map/all_gather | solution.py:65
  732.0 270.4 %reduce-scatter.35.cloned.1.call-start = ((), (), s32[]{:S(2)}) async-start(), calls=%async_computation.38 | async-start | bytes 1638400 | tf_op jit(solution)/shard_map/reduce_scatter | solution.py:69
  975.7 49.5 %all-gather.40.cloned.1.call-start = ((), (), s32[]{:S(2)}) async-start(), calls=%async_computation.39 | async-start | bytes 1638400 | tf_op jit(solution)/shard_map/all_gather | solution.py:65
  1006.9 51.6 %reduce-scatter.37.cloned.1.call-start = ((), (), s32[]{:S(2)}) async-start(), calls=%async_computation.40 | async-start | bytes 1638400 | tf_op jit(solution)/shard_map/reduce_scatter | solution.py:69
  1031.8 56.5 %reduce-scatter.33.cloned.1.call-start = ((), (), s32[]{:S(2)}) async-start(), calls=%async_computation.36 | async-start | bytes 1638400 | tf_op jit(solution)/shard_map/reduce_scatter | solution.py:69
  1037.3 72.8 %all-gather.42.cloned.1.call-start = ((), (), s32[]{:S(2)}) async-start(), calls=%async_computation.41 | async-start | bytes 1638400 | tf_op jit(solution)/shard_map/all_gather | solution.py:65
  1091.7 54.9 %reduce-scatter.39.cloned.1.call-start = ((), (), s32[]{:S(2)}) async-start(), calls=%async_computation.42 | async-start | bytes 1638400 | tf_op jit(solution)/shard_map/reduce_scatter | solution.py:69
  1119.9 56.2 %all-gather.44.cloned.1.call-start = ((), (), s32[]{:S(2)}) async-start(), calls=%async_computation.43 | async-start | bytes 1638400 | tf_op jit(solution)/shard_map/all_gather | solution.py:65
  1150.8 259.0 %reduce-scatter.41.cloned.1.call-start = ((), (), s32[]{:S(2)}) async-start(), calls=%async_computation.44 | async-start | bytes 1638400 | tf_op jit(solution)/shard_map/reduce_scatter | solution.py:69
  1212.6 320.3 %reduce-scatter.67.cloned.1.call-start = ((), (), s32[]{:S(2)}) async-start(), calls=%async_computation.57 | async-start | bytes 16957440
  1288.8 488.8 %reduce-scatter.69.cloned.1.call-start = ((), (), s32[]{:S(2)}) async-start(), calls=%async_computation.58 | async-start | bytes 16957440
  1366.1 481.4 %reduce-scatter.59.cloned.1.call-start = ((), (), s32[]{:S(2)}) async-start(), calls=%async_computation.53 | async-start | bytes 2211840 | tf_op jit(solution)/shard_map/reduce_scatter | solution.py:543
  1370.7 547.1 %reduce-scatter.53.cloned.1.call-start = ((), (), s32[]{:S(2)}) async-start(), calls=%async_computation.50 | async-start | bytes 2211840 | tf_op jit(solution)/shard_map/reduce_scatter | solution.py:540
  1372.9 618.7 %reduce-scatter.55.cloned.1.call-start = ((), (), s32[]{:S(2)}) async-start(), calls=%async_computation.51 | async-start | bytes 2949120 | tf_op jit(solution)/shard_map/reduce_scatter | solution.py:541
  1375.4 690.0 %reduce-scatter.57.cloned.1.call-start = ((), (), s32[]{:S(2)}) async-start(), calls=%async_computation.52 | async-start | bytes 2949120 | tf_op jit(solution)/shard_map/reduce_scatter | solution.py:542
  1377.9 757.1 %reduce-scatter.51.cloned.1.call-start = ((), (), s32[]{:S(2)}) async-start(), calls=%async_computation.49 | async-start | bytes 2211840 | tf_op jit(solution)/shard_map/reduce_scatter | solution.py:539
  1380.3 825.1 %reduce-scatter.49.cloned.1.call-start = ((), (), s32[]{:S(2)}) async-start(), calls=%async_computation.48 | async-start | bytes 2211840 | tf_op jit(solution)/shard_map/reduce_scatter | solution.py:538
  1382.7 892.4 %reduce-scatter.47.cloned.1.call-start = ((), (), s32[]{:S(2)}) async-start(), calls=%async_computation.47 | async-start | bytes 2211840 | tf_op jit(solution)/shard_map/reduce_scatter | solution.py:537
  1385.0 960.2 %reduce-scatter.45.cloned.1.call-start = ((), (), s32[]{:S(2)}) async-start(), calls=%async_computation.46 | async-start | bytes 2211840 | tf_op jit(solution)/shard_map/reduce_scatter | solution.py:536
  1387.3 1082.8 %reduce-scatter.63.cloned.1.call-start = ((), (), s32[]{:S(2)}) async-start(), calls=%async_computation.55 | async-start | bytes 7372800 | tf_op jit(solution)/shard_map/reduce_scatter | solution.py:545
  1393.3 1202.2 %reduce-scatter.61.cloned.1.call-start = ((), (), s32[]{:S(2)}) async-start(), calls=%async_computation.54 | async-start | bytes 7372800 | tf_op jit(solution)/shard_map/reduce_scatter | solution.py:544
  1399.4 1321.0 %reduce-scatter.65.cloned.1.call-start = ((), (), s32[]{:S(2)}) async-start(), calls=%async_computation.56 | async-start | bytes 7372800 | tf_op jit(solution)/shard_map/reduce_scatter | solution.py:546
  1405.7 1384.7 %reduce-scatter.43.cloned.1.call-start = ((), (), s32[]{:S(2)}) async-start(), calls=%async_computation.45 | async-start | bytes 2211840 | tf_op jit(solution)/shard_map/reduce_scatter | solution.py:535
  (162 other events, 2337.1 us)
Sparse Core Ops, SparseCore 0:
  73.2 14.7 all-gather.15
  90.2 139.7 all-gather.17
  232.2 129.0 all-gather.19
  374.8 24.7 reduce-scatter.26
  404.3 18.1 all-gather.21
  547.4 27.0 reduce-scatter.28
  576.6 53.8 all-gather.23
  632.6 42.0 all-gather.27
  676.8 16.8 all-gather.25
  700.4 26.5 reduce-scatter.30
  729.4 61.9 all-gather.31
  793.5 16.7 all-gather.29
  812.7 61.9 all-gather.33
  877.0 60.5 all-gather.35
  939.6 16.7 all-gather.37
  975.8 26.5 reduce-scatter.34
  1007.0 18.1 all-gather.39
  1032.0 26.5 reduce-scatter.36
  1061.8 26.5 reduce-scatter.32
  1091.8 18.1 all-gather.41
  1120.0 26.5 reduce-scatter.38
  1150.9 18.2 all-gather.43
  1212.8 26.5 reduce-scatter.40
  1288.9 243.9 reduce-scatter.66
  1536.5 241.0 reduce-scatter.68
  1781.6 65.9 reduce-scatter.58
  1851.8 65.9 reduce-scatter.52
  1921.9 69.6 reduce-scatter.54
  1995.8 69.6 reduce-scatter.56
  2069.3 65.6 reduce-scatter.50
  2139.5 65.7 reduce-scatter.48
  2209.4 65.7 reduce-scatter.46
  2279.5 65.7 reduce-scatter.44
  2349.4 120.5 reduce-scatter.62
  2474.7 120.8 reduce-scatter.60
  2599.5 120.7 reduce-scatter.64
  2724.6 65.7 reduce-scatter.42
where the time goes:
time: 2800 us
  waiting for transfers between devices  1990 us (71%)
  blocking collectives  339 us (12%)
  matrix products  159 us (6%)
  local copies, waits for them, and re-layouts  158 us (6%)
  other arithmetic  81.7 us (3%)
  between operations  66.1 us (2%)
    unnamed x39, waiting for transfers between devices  318 us
    reduce_scatter x8, waiting for transfers between devices, sum_rows(): lax.psum_scatter(values.astype(jnp.bfloat16), 'mp', scatter_dimension=1,...  179 us
    unnamed x402, local copies, waits for them, and re-layouts  138 us
    reduce_scatter x1, waiting for transfers between devices, body(): lax.psum_scatter(grad_ff_value, 'dp', scatter_dimension=0, tiled=True)  125 us
    reduce_scatter x1, waiting for transfers between devices, body(): lax.psum_scatter(grad_down, 'dp', scatter_dimension=1, tiled=True)  125 us
    reduce_scatter x1, waiting for transfers between devices, body(): lax.psum_scatter(grad_ff_gate, 'dp', scatter_dimension=0, tiled=True)  125 us
    all_gather x1, waiting for transfers between devices, fetch_weights(): lax.all_gather(conv_out, 'dp', axis=3, tiled=True)  116 us
    all_gather x8, waiting for transfers between devices, gather_rows(): return lax.all_gather(values, 'mp', axis=1, tiled=True)  89.2 us
  transfers between devices with their start and end apart: 37, of which 32 were waited for; matrix products, arithmetic and copies ran while one was open for 9% of the time, Pallas kernels for 0%

commit v1 on v0

v1 whole, which is shorter than its diff:
```python
import math

import jax
import jax.numpy as jnp
from jax import lax
from jax.sharding import PartitionSpec as P

C = 1280
HEAD_DIM = 64
GN_GROUPS = 32
SIDE = 16
TAPS = 9

highest = lax.Precision.HIGHEST
f32 = jnp.float32
bf16 = jnp.bfloat16


def ring_order(size):
    return list(range(0, size, 2)) + list(range(size - 1, 0, -2))


def ring_pairs(size):
    order = ring_order(size)
    right = [(order[i], order[(i + 1) % size]) for i in range(size)]
    return right, [(b, a) for a, b in right]


def ring_place(size):
    order = ring_order(size)
    place = jnp.array([order.index(i) for i in range(size)], jnp.int32)
    return jnp.array(order, jnp.int32), place[lax.axis_index("dp")]


def ring_gather(block):
    size = lax.axis_size("dp")
    rows, columns = block.shape
    if size != 8:
        return lax.all_gather(block, "dp", axis=0, tiled=True)
    right, left = ring_pairs(size)
    order, place = ring_place(size)
    half = rows // 2
    zero = jnp.int32(0)

    def put(whole, part, away, start):
        owner = order[(place + away) % size]
        return lax.dynamic_update_slice(whole, part[None], (owner, jnp.int32(start), zero))

    whole = put(jnp.zeros((size, rows, columns), block.dtype), block, 0, 0)
    from_left = from_right = block
    for step in range(1, size // 2):
        from_left = lax.ppermute(from_left, "dp", right)
        from_right = lax.ppermute(from_right, "dp", left)
        whole = put(whole, from_left, size - step, 0)
        whole = put(whole, from_right, step, 0)
    from_left = lax.ppermute(from_left[:half], "dp", right)
    from_right = lax.ppermute(from_right[half:], "dp", left)
    whole = put(whole, from_left, size // 2, 0)
    whole = put(whole, from_right, size // 2, half)
    return whole.reshape(size * rows, columns)


def ring_scatter(grad):
    size = lax.axis_size("dp")
    rows, columns = grad.shape[0] // size, grad.shape[1]
    if size != 8:
        return lax.psum_scatter(grad, "dp", scatter_dimension=0, tiled=True).astype(f32)
    right, left = ring_pairs(size)
    order, place = ring_place(size)
    half = rows // 2
    blocks = grad.reshape(size, rows, columns)

    def own(away):
        return lax.dynamic_index_in_dim(blocks, order[(place + away) % size], 0, keepdims=False)

    far = own(size // 2)
    to_right = lax.ppermute(far[:half], "dp", right)
    to_left = lax.ppermute(far[half:], "dp", left)
    for step in range(size // 2 - 1, 0, -1):
        ahead, behind = own(step), own(size - step)
        if step == size // 2 - 1:
            ahead = jnp.concatenate([ahead[:half].astype(f32) + to_right, ahead[half:].astype(f32)])
            behind = jnp.concatenate([behind[:half].astype(f32), behind[half:].astype(f32) + to_left])
        else:
            ahead = ahead.astype(f32) + to_right
            behind = behind.astype(f32) + to_left
        to_right = lax.ppermute(ahead.astype(bf16), "dp", right)
        to_left = lax.ppermute(behind.astype(bf16), "dp", left)
    return own(0).astype(f32) + to_right.astype(f32) + to_left.astype(f32)


def share_small(values, axis):
    size = lax.axis_size(axis)
    return lax.all_to_all(
        jnp.broadcast_to(values[None], (size,) + values.shape), axis, 0, 0, tiled=True
    )


def mp_bits():
    me = lax.axis_index("mp")
    return me % 2, me // 2


NEAR = [(0, 1), (1, 0), (2, 3), (3, 2)]
FAR = [(0, 2), (2, 0), (1, 3), (3, 1)]


def gather_rows(values):
    near_bit, far_bit = mp_bits()
    far = lax.ppermute(values, "mp", FAR)
    near = lax.ppermute(values, "mp", NEAR)
    both = lax.ppermute(far, "mp", NEAR)

    def pair(mine, other, bit):
        return jnp.concatenate(
            [jnp.where(bit == 0, mine, other), jnp.where(bit == 0, other, mine)], axis=1
        )

    return pair(pair(values, near, near_bit), pair(far, both, near_bit), far_bit)


def sum_rows(values):
    near_bit, far_bit = mp_bits()
    items, rows, columns = values.shape
    parts = values.reshape(items, 2, 2, rows // 4, columns)

    def near_part(bit):
        return lax.dynamic_index_in_dim(parts, bit, 2, keepdims=False)

    got = lax.ppermute(near_part(1 - near_bit).astype(bf16), "mp", NEAR)
    held = near_part(near_bit).astype(f32) + got.astype(f32)

    def far_part(bit):
        return lax.dynamic_index_in_dim(held, bit, 1, keepdims=False)

    got = lax.ppermute(far_part(1 - far_bit).astype(bf16), "mp", FAR)
    return far_part(far_bit) + got.astype(f32)


def product(former, latter):
    return jnp.einsum("sna,ab->snb", former, latter, preferred_element_type=f32)


def product_back(former, latter):
    return jnp.einsum("snb,ab->sna", former, latter, preferred_element_type=f32)


def weight_grad(former, latter):
    return jnp.einsum("sna,snb->ab", former, latter, preferred_element_type=f32).astype(bf16)


def tap_matrices(widths, item_rows):
    row = jnp.arange(item_rows, dtype=jnp.int32)
    step = jnp.arange(TAPS, dtype=jnp.int32)
    row_step, column_step = step // 3 - 1, step % 3 - 1
    column = row[None, :] % widths[:, None]
    beside = column[:, None, :] + column_step[None, :, None]
    usable = (beside >= 0) & (beside < widths[:, None, None])
    source = (
        row[None, None, :]
        + row_step[None, :, None] * widths[:, None, None]
        + column_step[None, :, None]
    )
    source = jnp.where(usable, source, -1)
    return (source[:, :, :, None] == row[None, None, None, :]).astype(bf16)


def shift_stack(taps, values):
    stacked = jnp.einsum("strq,sqi->srti", taps, values, preferred_element_type=f32)
    return stacked.astype(bf16).reshape(values.shape[:2] + (TAPS * values.shape[2],))


def shift_stack_back(taps, values):
    stacked = jnp.einsum("strq,sro->sqto", taps, values, preferred_element_type=f32)
    return stacked.astype(bf16).reshape(values.shape[:2] + (TAPS * values.shape[2],))


def shift_sum(taps, values):
    parts = values.astype(bf16).reshape(values.shape[:2] + (TAPS, values.shape[2] // TAPS))
    return jnp.einsum("strq,sqto->sro", taps, parts, preferred_element_type=f32)


def shift_sum_back(taps, values):
    parts = values.astype(bf16).reshape(values.shape[:2] + (TAPS, values.shape[2] // TAPS))
    return jnp.einsum("strq,srti->sqi", taps, parts, preferred_element_type=f32)


def norm_rows(hidden, factor):
    center = hidden - jnp.mean(hidden, axis=-1, keepdims=True)
    scaling = lax.rsqrt(jnp.mean(center * center, axis=-1, keepdims=True) + 1e-05)
    normal = center * scaling
    return ((normal * factor).astype(bf16), normal, scaling)


def norm_rows_back(gradient, normal, scaling, factor):
    scaled = gradient * factor
    offset = jnp.mean(scaled, axis=-1, keepdims=True)
    slopes = jnp.mean(scaled * normal, axis=-1, keepdims=True)
    return (scaling * (scaled - offset - normal * slopes), jnp.sum(gradient * normal, axis=(0, 1)))


def group_sum(values, per_group):
    rows_summed = jnp.sum(values, axis=1)
    return rows_summed.reshape(values.shape[0], values.shape[2] // per_group, per_group).sum(-1)


def spread(values, per_group):
    return jnp.repeat(values, per_group, axis=-1)[:, None, :]


def silu_back(scaled, gradient):
    share = jax.nn.sigmoid(scaled)
    return gradient * share * (1.0 + scaled * (1.0 - share))


def split_heads(values):
    return values.reshape(values.shape[0], values.shape[1], values.shape[2] // HEAD_DIM, HEAD_DIM)


def attend(query_rows, key_rows, value_rows, key_valid):
    scores = jnp.einsum(
        "sqhd,skhd->shqk",
        split_heads(query_rows),
        split_heads(key_rows),
        preferred_element_type=f32,
    ) * HEAD_DIM ** (-0.5)
    if key_valid is not None:
        scores = jnp.where(key_valid[:, None, None, :], scores, -1e30)
    exponent = jnp.exp(scores - jnp.max(scores, axis=-1, keepdims=True))
    chances = exponent / jnp.sum(exponent, axis=-1, keepdims=True)
    mixture = jnp.einsum(
        "shqk,skhd->sqhd",
        chances.astype(bf16),
        split_heads(value_rows),
        preferred_element_type=f32,
    )
    return mixture.reshape(query_rows.shape).astype(bf16), chances


def attend_back(query_rows, key_rows, value_rows, mixture_grad, chances):
    query_heads = split_heads(query_rows)
    key_heads = split_heads(key_rows)
    value_heads = split_heads(value_rows)
    grad_heads = split_heads(mixture_grad)
    value_grad = jnp.einsum(
        "shqk,sqhd->skhd", chances.astype(bf16), grad_heads, preferred_element_type=f32
    )
    share_grad = jnp.einsum(
        "sqhd,skhd->shqk", grad_heads, value_heads, preferred_element_type=f32
    )
    inner_sum = jnp.sum(chances * share_grad, axis=-1, keepdims=True)
    score_grad = (chances * (share_grad - inner_sum)).astype(bf16)
    query_grad = jnp.einsum(
        "shqk,skhd->sqhd", score_grad, key_heads, preferred_element_type=f32
    ) * HEAD_DIM ** (-0.5)
    key_grad = jnp.einsum(
        "shqk,sqhd->skhd", score_grad, query_heads, preferred_element_type=f32
    ) * HEAD_DIM ** (-0.5)
    return (
        query_grad.reshape(query_rows.shape).astype(bf16),
        key_grad.reshape(key_rows.shape).astype(bf16),
        value_grad.reshape(value_rows.shape).astype(bf16),
    )


def body(
    latent,
    text_embeds,
    cotangent,
    item_count,
    bucket,
    timestep,
    conv_in,
    conv_out,
    time_weight,
    self_query,
    self_key,
    self_value,
    self_out,
    cross_query,
    cross_key,
    cross_value,
    cross_out,
    ff_value,
    ff_gate,
    ff_down,
    gn_in_gain,
    gn_mid_gain,
    self_gain,
    cross_gain,
    ff_gain,
):
    slot_count, local_rows, channels = latent.shape
    dp_size, mp_size = lax.axis_size("dp"), lax.axis_size("mp")
    item_rows = local_rows * mp_size
    per_group = channels // GN_GROUPS
    own_channels = conv_in.shape[3]
    share = conv_in.shape[2]
    dp_index, mp_index = lax.axis_index("dp"), lax.axis_index("mp")
    is_live = (jnp.arange(slot_count, dtype=jnp.int32) < item_count[0]).astype(f32)
    widths = jnp.where(
        bucket == 0, SIDE, jnp.where(bucket == 1, 5 * SIDE // 4, 3 * SIDE // 2)
    ).astype(jnp.int32)
    heights = jnp.where(
        bucket == 0, SIDE, jnp.where(bucket == 1, 3 * SIDE // 4, 5 * SIDE // 8)
    ).astype(jnp.int32)
    filled = widths * heights
    position = mp_index * local_rows + jnp.arange(local_rows, dtype=jnp.int32)
    row_mask = (position[None, :] < filled[:, None]).astype(f32) * is_live[:, None]
    key_valid = jnp.arange(item_rows, dtype=jnp.int32)[None, :] < filled[:, None]
    full_mask = key_valid.astype(f32) * is_live[:, None]
    keep = row_mask[:, :, None]
    keep_all = full_mask[:, :, None]
    counts = filled.astype(f32) * per_group
    channel_start = mp_index * own_channels
    taps = tap_matrices(widths, item_rows)

    gain_parts = jnp.stack([gn_in_gain, gn_mid_gain, self_gain, cross_gain, ff_gain]).astype(f32)
    small = jnp.concatenate([gain_parts.reshape(-1), timestep.astype(f32)])
    small_all = share_small(small, "dp")
    gains = small_all[:, : 5 * share].reshape(dp_size, 5, share)
    gains = jnp.swapaxes(gains, 0, 1).reshape(5, channels)
    gain_in_f, gain_self_f, gain_cross_f, gain_feed_f = gains[0], gains[2], gains[3], gains[4]
    gain_mid_own = lax.dynamic_slice_in_dim(gains[1], channel_start, own_channels)
    steps_all = small_all[:, 5 * share :].reshape(-1)

    w_in = ring_gather(
        jnp.swapaxes(conv_in.reshape(TAPS, share, own_channels), 0, 1).reshape(share, -1)
    )
    w_out = ring_gather(
        jnp.transpose(conv_out.reshape(TAPS, own_channels, share), (2, 0, 1)).reshape(share, -1)
    )
    w_self = ring_gather(
        jnp.concatenate([self_query, self_key, self_value, cross_query], axis=1)
    )
    w_outs = ring_gather(jnp.concatenate([self_out.T, cross_out.T], axis=1))
    w_text = ring_gather(jnp.concatenate([cross_key, cross_value], axis=1))
    w_feed = ring_gather(jnp.concatenate([ff_value, ff_gate], axis=1))
    w_down = ring_gather(ff_down.T)
    qkv_full, cq_full = w_self[:, : 3 * own_channels], w_self[:, 3 * own_channels :]
    so_full, co_full = w_outs[:, :own_channels], w_outs[:, own_channels:]
    hidden_own = ff_down.shape[0]

    half_width = C // 2
    wave = dp_index * share + jnp.arange(share, dtype=jnp.int32)
    frequency = jnp.exp(-math.log(10000.0) * (wave % half_width).astype(f32) / half_width)
    angles = steps_all[:, None] * frequency[None, :]
    time_act = jax.nn.silu(
        jnp.where(wave[None, :] < half_width, jnp.cos(angles), jnp.sin(angles))
    ).astype(bf16)
    time_part = jnp.dot(time_act, time_weight, preferred_element_type=f32)
    time_added = lax.all_to_all(
        time_part.reshape(dp_size, slot_count, own_channels), "dp", 0, 0, tiled=True
    ).sum(0)

    masked = latent.astype(f32) * keep
    all_positions = jnp.arange(item_rows, dtype=jnp.int32).reshape(mp_size, 1, local_rows)
    held = (all_positions < filled[None, :, None]).astype(f32).sum(-1) * is_live * per_group
    held_here = jnp.sum(row_mask, axis=1) * per_group
    local_sum = group_sum(masked, per_group)
    local_mean = local_sum / jnp.maximum(held_here, 1.0)[:, None]
    local_center = (masked - spread(local_mean, per_group)) * keep
    local_spread = group_sum(local_center * local_center, per_group)
    stats = share_small(jnp.stack([local_sum, local_spread]), "mp").reshape(
        mp_size, 2, slot_count, GN_GROUPS
    )
    average = jnp.sum(stats[:, 0], axis=0) / counts[:, None]
    means = stats[:, 0] / jnp.maximum(held, 1.0)[:, :, None]
    variance = (
        jnp.sum(stats[:, 1] + held[:, :, None] * (means - average) ** 2, axis=0) / counts[:, None]
    )
    scaling_in = spread(lax.rsqrt(variance + 1e-06), per_group)
    standard_in = (masked - spread(average, per_group)) * scaling_in
    first_act = (jax.nn.silu(standard_in * gain_in_f) * keep).astype(bf16)
    first_all = gather_rows(first_act)

    middle = (
        shift_sum(taps, product(first_all, w_in)) + time_added[:, None, :]
    ) * keep_all
    average_mid = group_sum(middle, per_group) / counts[:, None]
    apart_mid = middle - spread(average_mid, per_group)
    center_mid = apart_mid * keep_all
    scaling_mid = spread(
        lax.rsqrt(group_sum(center_mid * center_mid, per_group) / counts[:, None] + 1e-06),
        per_group,
    )
    standard_mid = apart_mid * scaling_mid
    second_act = (jax.nn.silu(standard_mid * gain_mid_own) * keep_all).astype(bf16)
    second_taps = shift_stack(taps, second_act)
    resnet = (masked + sum_rows(product_back(second_taps, w_out))) * keep

    attend_in, normal_self, scaling_self = norm_rows(resnet, gain_self_f)
    attend_all = gather_rows(attend_in)
    qkv = product(attend_all, qkv_full).astype(bf16)
    query_rows, key_rows, value_rows = jnp.split(qkv, 3, axis=2)
    mixture, self_chances = attend(query_rows, key_rows, value_rows, key_valid)
    after_self = resnet + sum_rows(product_back(mixture, so_full))

    text_pair = product(text_embeds, w_text).astype(bf16)
    text_keys, text_values = jnp.split(text_pair, 2, axis=2)
    cross_in, normal_cross, scaling_cross = norm_rows(after_self, gain_cross_f)
    cross_all = gather_rows(cross_in)
    cross_rows = product(cross_all, cq_full).astype(bf16)
    cross_mix, cross_chances = attend(cross_rows, text_keys, text_values, None)
    after_cross = after_self + sum_rows(product_back(cross_mix, co_full))

    feed_in, normal_feed, scaling_feed = norm_rows(after_cross, gain_feed_f)
    feed_all = gather_rows(feed_in)
    pair_part = product(feed_all, w_feed)
    value_part, gate_part = pair_part[:, :, :hidden_own], pair_part[:, :, hidden_own:]
    below = 0.5 * lax.erfc(-gate_part * math.sqrt(0.5))
    gelu_gate = gate_part * below
    gelu_slope = below + gate_part * jnp.exp(-0.5 * gate_part * gate_part) / math.sqrt(2 * math.pi)
    hidden = (value_part * gelu_gate).astype(bf16)
    output = ((after_cross + sum_rows(product_back(hidden, w_down))) * keep).astype(bf16)

    out_grad = cotangent.astype(f32) * keep
    feed_branch = gather_rows(out_grad.astype(bf16))
    sum_down = ring_scatter(weight_grad(feed_branch, hidden))
    hidden_grad = product(feed_branch, w_down)
    pair_grad = jnp.concatenate(
        [
            (hidden_grad * gelu_gate).astype(bf16),
            (hidden_grad * value_part * gelu_slope).astype(bf16),
        ],
        axis=2,
    )
    sum_feed = ring_scatter(weight_grad(feed_all, pair_grad))
    feed_back = sum_rows(product_back(pair_grad, w_feed))
    feed_dv, grad_gain_feed = norm_rows_back(feed_back, normal_feed, scaling_feed, gain_feed_f)
    cross_grad = out_grad + feed_dv

    cross_branch = gather_rows(cross_grad.astype(bf16))
    grad_cross_out = weight_grad(cross_branch, cross_mix)
    cross_mix_grad = product(cross_branch, co_full).astype(bf16)
    cross_dq, cross_dk, cross_dv = attend_back(
        cross_rows, text_keys, text_values, cross_mix_grad, cross_chances
    )
    grad_cross_query = weight_grad(cross_all, cross_dq)
    sum_text = ring_scatter(weight_grad(text_embeds, jnp.concatenate([cross_dk, cross_dv], axis=2)))
    cross_back = sum_rows(product_back(cross_dq, cq_full))
    cross_dv_rows, grad_gain_cross = norm_rows_back(
        cross_back, normal_cross, scaling_cross, gain_cross_f
    )
    self_grad = cross_grad + cross_dv_rows

    self_branch = gather_rows(self_grad.astype(bf16))
    grad_self_out = weight_grad(self_branch, mixture)
    mixture_grad = product(self_branch, so_full).astype(bf16)
    qkv_grad = jnp.concatenate(
        attend_back(query_rows, key_rows, value_rows, mixture_grad, self_chances), axis=2
    )
    sum_self = ring_scatter(
        jnp.concatenate([weight_grad(attend_all, qkv_grad), grad_cross_query], axis=1)
    )
    sum_outs = ring_scatter(jnp.concatenate([grad_self_out, grad_cross_out], axis=1))
    self_back = sum_rows(product_back(qkv_grad, qkv_full))
    self_dv_rows, grad_gain_self = norm_rows_back(self_back, normal_self, scaling_self, gain_self_f)
    resnet_grad = (self_grad + self_dv_rows) * keep

    resnet_branch = gather_rows(resnet_grad.astype(bf16))
    sum_out = ring_scatter(weight_grad(resnet_branch, second_taps))
    second_grad = shift_sum_back(taps, product(resnet_branch, w_out))
    mid_slope = silu_back(standard_mid * gain_mid_own, second_grad * keep_all)
    mid_gain_part = jnp.sum(mid_slope * standard_mid, axis=(0, 1))
    hat_mid = mid_slope * gain_mid_own
    mid_a = spread(group_sum(hat_mid, per_group) / counts[:, None], per_group)
    mid_b = spread(group_sum(hat_mid * standard_mid, per_group) / counts[:, None], per_group)
    middle_grad = (
        scaling_mid * (hat_mid - (mid_a + standard_mid * mid_b)) * keep_all
    ).astype(bf16)

    time_sum = jnp.sum(middle_grad.astype(f32), axis=1)
    time_sum_all = share_small(time_sum, "dp").reshape(-1, own_channels)
    grad_time = jnp.einsum(
        "sa,sb->ab",
        time_act.astype(f32),
        time_sum_all,
        precision=highest,
        preferred_element_type=f32,
    )

    middle_taps = shift_stack_back(taps, middle_grad)
    sum_in = ring_scatter(weight_grad(first_all, middle_taps))
    first_grad = sum_rows(product_back(middle_taps, w_in))
    in_slope = silu_back(standard_in * gain_in_f, first_grad * keep)
    in_gain_part = jnp.sum(in_slope * standard_in, axis=(0, 1))
    hat_in = in_slope * gain_in_f
    in_a, in_b = lax.psum(
        (group_sum(hat_in, per_group), group_sum(hat_in * standard_in, per_group)), "mp"
    )
    in_a = spread(in_a / counts[:, None], per_group)
    in_b = spread(in_b / counts[:, None], per_group)
    grouped_grad = scaling_in * (hat_in - (in_a + standard_in * in_b))
    latent_grad = ((resnet_grad + grouped_grad) * keep).astype(bf16)

    mid_gain_whole = lax.dynamic_update_slice_in_dim(
        jnp.zeros((channels,), f32), mid_gain_part, channel_start, 0
    )
    gain_parts = jnp.stack(
        [in_gain_part, mid_gain_whole, grad_gain_self, grad_gain_cross, grad_gain_feed]
    )
    gain_parts = jnp.swapaxes(gain_parts.reshape(5, dp_size, share), 0, 1)
    gain_parts = jnp.broadcast_to(gain_parts[:, None], (dp_size, mp_size, 5, share))
    gain_sums = lax.all_to_all(
        gain_parts.reshape(dp_size * mp_size, 5, share), ("dp", "mp"), 0, 0, tiled=True
    ).sum(0)

    return (
        output,
        latent_grad,
        jnp.swapaxes(sum_in.reshape(share, TAPS, own_channels), 0, 1).reshape(conv_in.shape),
        jnp.transpose(sum_out.reshape(share, TAPS, own_channels), (1, 2, 0)).reshape(
            conv_out.shape
        ),
        grad_time,
        sum_self[:, :own_channels],
        sum_self[:, own_channels : 2 * own_channels],
        sum_self[:, 2 * own_channels : 3 * own_channels],
        sum_outs[:, :own_channels].T,
        sum_self[:, 3 * own_channels :],
        sum_text[:, :own_channels],
        sum_text[:, own_channels:],
        sum_outs[:, own_channels:].T,
        sum_feed[:, :hidden_own],
        sum_feed[:, hidden_own:],
        sum_down.T,
        gain_sums[0],
        gain_sums[1],
        gain_sums[2],
        gain_sums[3],
        gain_sums[4],
    )


def solution(mesh):
    in_specs = (
        P("dp", "mp", None),
        P("dp", None, None),
        P("dp", "mp", None),
        P("dp"),
        P("dp"),
        P("dp"),
        P(None, None, "dp", "mp"),
        P(None, None, "mp", "dp"),
        P("dp", "mp"),
        P("dp", "mp"),
        P("dp", "mp"),
        P("dp", "mp"),
        P("mp", "dp"),
        P("dp", "mp"),
        P("dp", "mp"),
        P("dp", "mp"),
        P("mp", "dp"),
        P("dp", "mp"),
        P("dp", "mp"),
        P("mp", "dp"),
        P("dp"),
        P("dp"),
        P("dp"),
        P("dp"),
        P("dp"),
    )
    out_specs = (
        P("dp", "mp", None),
        P("dp", "mp", None),
        P(None, None, "dp", "mp"),
        P(None, None, "mp", "dp"),
        P("dp", "mp"),
        P("dp", "mp"),
        P("dp", "mp"),
        P("dp", "mp"),
        P("mp", "dp"),
        P("dp", "mp"),
        P("dp", "mp"),
        P("dp", "mp"),
        P("mp", "dp"),
        P("dp", "mp"),
        P("dp", "mp"),
        P("mp", "dp"),
        P("dp"),
        P("dp"),
        P("dp"),
        P("dp"),
        P("dp"),
    )
    return jax.shard_map(body, mesh=mesh, in_specs=in_specs, out_specs=out_specs, check_vma=False)
```

time: 2800 us -> 1130 us (0.40)
  waiting for transfers between devices: 1990 us -> 473 us
  blocking collectives: 339 us -> 7.57 us
  starting transfers between devices: 2.47 us -> 155 us
  local copies, waits for them, and re-layouts: 158 us -> 219 us
  between operations: 66.1 us -> 26.8 us
    reduce_scatter x20 -> x0, waiting for transfers between devices: 1190 us -> none  [the longest x8 179 us: sum_rows(): lax.psum_scatter(values.astype(jnp.bfloat16), 'mp', scatter_dimension=1,...]
    all_gather x15 -> x0, waiting for transfers between devices: 487 us -> none  [the longest x1 116 us: fetch_weights(): lax.all_gather(conv_out, 'dp', axis=3, tiled=True)]
    ppermute x0 -> x152, waiting for transfers between devices: none -> 462 us  [the longest x21 136 us: ring_scatter(): to_right = lax.ppermute(ahead.astype(bf16), 'dp', right)]
    unnamed x39 -> x0, waiting for transfers between devices: 318 us -> none
    all_gather x7 -> x0, blocking collectives: 243 us -> none  [the longest x1 36 us: fetch_weights(): lax.all_gather(time_weight, 'dp', axis=0, tiled=True)]
    ppermute x0 -> x152, starting transfers between devices: none -> 136 us  [the longest x21 28.4 us: ring_scatter(): to_right = lax.ppermute(ahead.astype(bf16), 'dp', right)]
    unnamed x402 -> x296, local copies, waits for them, and re-layouts: 138 us -> 17.9 us
    unnamed x2 -> x0, blocking collectives: 77.5 us -> none
  transfers between devices with their start and end apart: 37 -> 157, of which waited for: 32 -> 79; matrix products, arithmetic and copies ran while one was open for 9% -> 35% of each run, Pallas kernels for 0% -> 0%
where the time goes in v1:
time: 1130 us; the launch traced here: 1110 us
  waiting for transfers between devices  473 us (42%)
  local copies, waits for them, and re-layouts  219 us (19%)
  starting transfers between devices  155 us (14%)
  matrix products  148 us (13%)
  other arithmetic  85.7 us (8%)
  between operations  26.8 us (2%)
    ppermute x21, waiting for transfers between devices, ring_scatter(): to_right = lax.ppermute(ahead.astype(bf16), 'dp', right)  136 us
    ppermute x21, waiting for transfers between devices, ring_gather(): from_left = lax.ppermute(from_left, 'dp', right)  89.5 us
    dynamic_update_slice x63, local copies, waits for them, and re-layouts, put(): lax.dynamic_update_slice(whole, part[None], (owner, jnp.int32(start), zero))  76.1 us
    dot_general x8, matrix products, product_back(): return jnp.einsum('snb,ab->sna', former, latter, preferred_element_type=f32)  47.9 us
    dot_general x9, matrix products, product(): return jnp.einsum('sna,ab->snb', former, latter, preferred_element_type=f32)  47 us
    ppermute x21, waiting for transfers between devices, ring_gather(): from_right = lax.ppermute(from_right, 'dp', left)  42.1 us
    ppermute x7, waiting for transfers between devices, ring_gather(): from_left = lax.ppermute(from_left[:half], 'dp', right)  40.6 us
    ppermute x8, waiting for transfers between devices, sum_rows(): got = lax.ppermute(far_part(1 - far_bit).astype(bf16), 'mp', FAR)  38.3 us
  transfers between devices with their start and end apart: 157, of which 79 were waited for; matrix products, arithmetic and copies ran while one was open for 35% of the time, Pallas kernels for 0%

profile of v1, /device:TPU:0, one launch (start us, length us, event | category | flops | bytes accessed | tf_op | source)
XLA Modules:
  0.0 1114.6 jit_solution(13257733619527521712)
XLA Ops:
  75.4 4.7 all-to-all-start.1
  82.2 4.6 all-to-all-done.1
  93.7 5.3 all-to-all-done.2
  115.6 6.0 collective-permute-done.25
  135.7 6.6 collective-permute-done.36
  144.0 6.0 collective-permute-done.37
  161.5 5.3 collective-permute-done.38
  167.7 9.1 collective-permute-done.39
  184.8 19.9 %collective-permute-done.26 = bf16[160,1280]{1,0:T(8,128)(2,1)} collective-permute-done((bf16[160,1280]{1,0:T(8,128)(2,1)}, bf16[160,1280]{1,0:T(8,128)(2,1)}, u32[]{:S(2)}, u32[]{:S(2)}) %collective-permute-start.26) | collective-permute-done | bytes 409632 | tf_op jit(solution)/shard_map/ppermute | solution.py:52
  207.7 5.0 collective-permute-done.27
  215.3 5.5 collective-permute-done.68
  223.8 9.0 collective-permute-done.69
  248.7 15.2 %collective-permute-done.48 = bf16[128,640]{0,1:T(8,128)(2,1)S(1)} collective-permute-done((bf16[128,640]{0,1:T(8,128)(2,1)S(1)}, bf16[128,640]{0,1:T(8,128)(2,1)S(1)}, u32[]{:S(2)}, u32[]{:S(2)}) %collective-permute-start.48) | collective-permute-done | bytes 163872 | tf_op jit(solution)/shard_map/ppermute | solution.py:56
  288.6 9.9 collective-permute-done.30
  299.5 7.2 collective-permute-done.31
  312.4 17.7 %collective-permute-done.13 = bf16[160,2880]{1,0:T(8,128)(2,1)S(1)} collective-permute-done((bf16[160,2880]{1,0:T(8,128)(2,1)S(1)}, bf16[160,2880]{1,0:T(8,128)(2,1)S(1)}, u32[]{:S(2)}, u32[]{:S(2)}) %collective-permute-start.13) | collective-permute-done | bytes 921632 | tf_op jit(solution)/shard_map/ppermute | solution.py:52
  334.2 18.6 %collective-permute-done.7 = bf16[160,2880]{1,0:T(8,128)(2,1)S(1)} collective-permute-done((bf16[160,2880]{1,0:T(8,128)(2,1)S(1)}, bf16[160,2880]{1,0:T(8,128)(2,1)S(1)}, u32[]{:S(2)}, u32[]{:S(2)}) %collective-permute-start.7) | collective-permute-done | bytes 921632 | tf_op jit(solution)/shard_map/ppermute | solution.py:52
  357.4 14.1 %collective-permute-done.15 = bf16[160,2880]{1,0:T(8,128)(2,1)S(1)} collective-permute-done((bf16[160,2880]{1,0:T(8,128)(2,1)S(1)}, bf16[160,2880]{1,0:T(8,128)(2,1)S(1)}, u32[]{:S(2)}, u32[]{:S(2)}) %collective-permute-start.15) | collective-permute-done | bytes 921632 | tf_op jit(solution)/shard_map/ppermute | solution.py:52
  375.6 10.2 collective-permute-done.9
  386.6 7.8 collective-permute-done.10
  395.5 9.3 convolution_convert_fusion.1
  410.4 10.9 dot_general.144
  424.9 5.0 collective-permute-done.18
  430.7 12.4 %fusion.5 = f32[2,2,2,64,1280]{4,3,2,1,0:T(8,128)S(1)} fusion(bf16[1280,2880,1,1,1]{1,0,4,3,2:T(8,128)(2,1)} %bitcast.50, bf16[2,2,2,64,2880]{3,2,1,4,0:T(2,128)(2,1)} %dot_general.144), kind=kOutput, calls=%fused_computation.9 | convolution fusion | flops 3774873600 | bytes 12943360 | tf_op jit(solution)/shard_map/snb,ab->sna/dot_general | solution.py:145
  453.6 5.5 collective-permute-done.20
  468.9 4.6 collective-permute-done.63
  493.5 8.5 collective-permute-done.41
  506.6 6.7 collective-permute-done.51
  530.0 7.9 collective-permute-done.54
  540.2 8.5 collective-permute-done.56
  550.6 5.9 fusion.90
  556.6 8.8 multiply_convert_fusion.1
  566.7 4.4 bitcast_convert_fusion.2
  573.1 5.2 fusion.243
  578.6 6.4 fusion.244
  595.4 6.1 collective-permute-done.136
  615.9 7.3 collective-permute-done.80
  623.8 6.4 collective-permute-done.75
  632.4 7.7 collective-permute-done.146
  683.2 5.0 collective-permute-done.132
  701.4 22.2 %collective-permute-done.130 = bf16[256,640]{0,1:T(8,128)(2,1)S(1)} collective-permute-done((bf16[256,640]{0,1:T(8,128)(2,1)S(1)}, bf16[256,640]{0,1:T(8,128)(2,1)S(1)}, u32[]{:S(2)}, u32[]{:S(2)}) %collective-permute-start.130) | collective-permute-done | bytes 327712 | tf_op jit(solution)/shard_map/ppermute | solution.py:87
  765.2 5.8 copy.546
  793.4 7.2 collective-permute-done.122
  822.3 5.5 collective-permute-done.92
  835.2 9.7 convolution_convert_fusion
  851.1 10.9 dot_general.174
  862.0 12.5 %fusion.3 = f32[2,2,2,64,1280]{4,3,2,1,0:T(8,128)S(1)} fusion(bf16[1280,2880,1,1,1]{1,0,4,3,2:T(8,128)(2,1)} %bitcast.177, bf16[2,2,2,64,2880]{3,2,1,4,0:T(2,128)(2,1)} %dot_general.174), kind=kOutput, calls=%fused_computation.7 | convolution fusion | flops 3774873600 | bytes 12943360 | tf_op jit(solution)/shard_map/snb,ab->sna/dot_general | solution.py:145
  876.3 7.1 bitcast_convert_fusion.1
  883.4 10.5 copy.542
  898.6 7.0 bitcast_convert_fusion
  905.6 10.5 copy.544
  940.9 6.0 collective-permute-done.104
  950.7 16.4 %collective-permute-done.97 = bf16[160,2880]{1,0:T(8,128)(2,1)S(1)} collective-permute-done((bf16[160,2880]{1,0:T(8,128)(2,1)S(1)}, bf16[160,2880]{1,0:T(8,128)(2,1)S(1)}, u32[]{:S(2)}, u32[]{:S(2)}) %collective-permute-start.97) | collective-permute-done | bytes 921632 | tf_op jit(solution)/shard_map/ppermute | solution.py:87
  970.6 16.7 %collective-permute-done.105 = bf16[160,2880]{1,0:T(8,128)(2,1)S(1)} collective-permute-done((bf16[160,2880]{1,0:T(8,128)(2,1)S(1)}, bf16[160,2880]{1,0:T(8,128)(2,1)S(1)}, u32[]{:S(2)}, u32[]{:S(2)}) %collective-permute-start.105) | collective-permute-done | bytes 921632 | tf_op jit(solution)/shard_map/ppermute | solution.py:87
  991.5 16.0 %collective-permute-done.98 = bf16[160,2880]{1,0:T(8,128)(2,1)S(1)} collective-permute-done((bf16[160,2880]{1,0:T(8,128)(2,1)S(1)}, bf16[160,2880]{1,0:T(8,128)(2,1)S(1)}, u32[]{:S(2)}, u32[]{:S(2)}) %collective-permute-start.98) | collective-permute-done | bytes 921632 | tf_op jit(solution)/shard_map/ppermute | solution.py:87
  1012.8 14.2 %collective-permute-done.106 = bf16[160,2880]{1,0:T(8,128)(2,1)S(1)} collective-permute-done((bf16[160,2880]{1,0:T(8,128)(2,1)S(1)}, bf16[160,2880]{1,0:T(8,128)(2,1)S(1)}, u32[]{:S(2)}, u32[]{:S(2)}) %collective-permute-start.106) | collective-permute-done | bytes 921632 | tf_op jit(solution)/shard_map/ppermute | solution.py:87
  1032.1 4.7 all-to-all-start.4
  1037.1 7.6 all-reduce
  1061.0 7.8 collective-permute-done.99
  1068.8 17.3 %collective-permute-done.107 = bf16[160,2880]{1,0:T(8,128)(2,1)} collective-permute-done((bf16[160,2880]{1,0:T(8,128)(2,1)}, bf16[160,2880]{1,0:T(8,128)(2,1)}, u32[]{:S(2)}, u32[]{:S(2)}) %collective-permute-start.107) | collective-permute-done | bytes 921632 | tf_op jit(solution)/shard_map/ppermute | solution.py:87
  1086.2 9.0 collective-permute-done.111
  1095.2 4.5 fusion.41
  1102.9 4.5 copy.562
  1109.7 4.5 copy.563
  (960 shorter events, 519.7 us)
Async XLA Ops:
  4.6 230.0 %collective-permute-start.3 = (bf16[160,2880]{1,0:T(8,128)(2,1)}, bf16[160,2880]{1,0:T(8,128)(2,1)}, u32[]{:S(2)}, u32[]{:S(2)}) collective-permute-start(bf16[160,2880]{1,0:T(8,128)(2,1)} %copy.498), channel_id=1, source_target_pairs={{0,8},{8,16},{16,24},{24,28},{28,20},{20,12},{12,4},{4,0},{1,9},{9... | collective-permute-start | bytes 2764808 | tf_op jit(solution)/shard_map/ppermute | solution.py:52
  7.6 230.3 %collective-permute-start.4 = (bf16[160,2880]{1,0:T(8,128)(2,1)}, bf16[160,2880]{1,0:T(8,128)(2,1)}, u32[]{:S(2)}, u32[]{:S(2)}) collective-permute-start(bf16[160,2880]{1,0:T(8,128)(2,1)} %copy.498), channel_id=1, source_target_pairs={{8,0},{16,8},{24,16},{28,24},{20,28},{12,20},{4,12},{0,4},{9,1},{1... | collective-permute-start | bytes 2764808 | tf_op jit(solution)/shard_map/ppermute | solution.py:53
  19.6 80.0 %collective-permute-start.32 = (bf16[160,640]{1,0:T(8,128)(2,1)}, bf16[160,640]{1,0:T(8,128)(2,1)}, u32[]{:S(2)}, u32[]{:S(2)}) collective-permute-start(bf16[160,640]{1,0:T(8,128)(2,1)} %get-tuple-element.144), channel_id=1, source_target_pairs={{0,8},{8,16},{16,24},{24,28},{28,20},{20,12},{12,4},{4,0},{1,9},{9... | collective-permute-start | bytes 614408 | tf_op jit(solution)/shard_map/ppermute | solution.py:52
  21.6 80.0 %collective-permute-start.33 = (bf16[160,640]{1,0:T(8,128)(2,1)}, bf16[160,640]{1,0:T(8,128)(2,1)}, u32[]{:S(2)}, u32[]{:S(2)}) collective-permute-start(bf16[160,640]{1,0:T(8,128)(2,1)} %get-tuple-element.144), channel_id=1, source_target_pairs={{8,0},{16,8},{24,16},{28,24},{20,28},{12,20},{4,12},{0,4},{9,1},{1... | collective-permute-start | bytes 614408 | tf_op jit(solution)/shard_map/ppermute | solution.py:53
  24.2 50.5 %all-to-all-start = ((f32[4,1,128]{2,1,0:T(1,128)}), f32[4,1,128]{2,1,0:T(1,128)S(1)}, u32[]{:S(2)}, u32[]{:S(2)}) async-start(f32[4,1,128]{2,1,0:T(1,128)} %reshape.958), calls=%async_computation | async-start | bytes 4096 | tf_op jit(solution)/shard_map/all_to_all | solution.py:94
  28.5 83.6 %collective-permute-start.24 = (bf16[160,1280]{1,0:T(8,128)(2,1)}, bf16[160,1280]{1,0:T(8,128)(2,1)}, u32[]{:S(2)}, u32[]{:S(2)}) collective-permute-start(bf16[160,1280]{1,0:T(8,128)(2,1)} %concatenate.166), channel_id=1, source_target_pairs={{0,8},{8,16},{16,24},{24,28},{28,20},{20,12},{12,4},{4,0},{1,9},{9... | collective-permute-start | bytes 1228808 | tf_op jit(solution)/shard_map/ppermute | solution.py:52
  121.5 30.4 %collective-permute-start.1 = (bf16[2,64,1280]{2,1,0:T(8,128)(2,1)S(1)}, bf16[2,64,1280]{2,1,0:T(8,128)(2,1)S(1)}, u32[]{:S(2)}, u32[]{:S(2)}) collective-permute-start(bf16[2,64,1280]{2,1,0:T(8,128)(2,1)S(1)} %multiply_convert_fusion.10), channel_id=1, source_target_pairs={{0,2},{2,0},{1,3},{3,1},{4,6},{6,4},{5,7},{7,5},{8,10},{10,8},{9,1... | collective-permute-start | bytes 983048 | tf_op jit(solution)/shard_map/ppermute | solution.py:110
  130.3 22.5 %collective-permute-start.44 = (bf16[256,640]{0,1:T(8,128)(2,1)S(1)}, bf16[256,640]{0,1:T(8,128)(2,1)S(1)}, u32[]{:S(2)}, u32[]{:S(2)}) collective-permute-start(bf16[256,640]{0,1:T(8,128)(2,1)S(1)} %collective-permute-done.42), channel_id=1, source_target_pairs={{0,8},{8,16},{16,24},{24,28},{28,20},{20,12},{12,4},{4,0},{1,9},{9... | collective-permute-start | bytes 983048 | tf_op jit(solution)/shard_map/ppermute | solution.py:52
  151.9 26.2 %collective-permute-start.58 = (bf16[160,2560]{1,0:T(8,128)(2,1)S(1)}, bf16[160,2560]{1,0:T(8,128)(2,1)}, u32[]{:S(2)}, u32[]{:S(2)}) collective-permute-start(bf16[160,2560]{1,0:T(8,128)(2,1)S(1)} %copy-done.25), channel_id=1, source_target_pairs={{0,8},{8,16},{16,24},{24,28},{28,20},{20,12},{12,4},{4,0},{1,9},{9... | collective-permute-start | bytes 2457608 | tf_op jit(solution)/shard_map/ppermute | solution.py:52
  157.3 24.5 %collective-permute-start.59 = (bf16[160,2560]{1,0:T(8,128)(2,1)S(1)}, bf16[160,2560]{1,0:T(8,128)(2,1)}, u32[]{:S(2)}, u32[]{:S(2)}) collective-permute-start(bf16[160,2560]{1,0:T(8,128)(2,1)S(1)} %copy-done.25), channel_id=1, source_target_pairs={{8,0},{16,8},{24,16},{28,24},{20,28},{12,20},{4,12},{0,4},{9,1},{1... | collective-permute-start | bytes 2457608 | tf_op jit(solution)/shard_map/ppermute | solution.py:53
  176.8 64.2 %collective-permute-start.11 = (bf16[160,2880]{1,0:T(8,128)(2,1)S(1)}, bf16[160,2880]{1,0:T(8,128)(2,1)S(1)}, u32[]{:S(2)}, u32[]{:S(2)}) collective-permute-start(bf16[160,2880]{1,0:T(8,128)(2,1)S(1)} %copy.503), channel_id=1, source_target_pairs={{0,8},{8,16},{16,24},{24,28},{28,20},{20,12},{12,4},{4,0},{1,9},{9... | collective-permute-start | bytes 2764808 | tf_op jit(solution)/shard_map/ppermute | solution.py:52
  178.2 64.9 %collective-permute-start.12 = (bf16[160,2880]{1,0:T(8,128)(2,1)S(1)}, bf16[160,2880]{1,0:T(8,128)(2,1)S(1)}, u32[]{:S(2)}, u32[]{:S(2)}) collective-permute-start(bf16[160,2880]{1,0:T(8,128)(2,1)S(1)} %copy.503), channel_id=1, source_target_pairs={{8,0},{16,8},{24,16},{28,24},{20,28},{12,20},{4,12},{0,4},{9,1},{1... | collective-permute-start | bytes 2764808 | tf_op jit(solution)/shard_map/ppermute | solution.py:53
  181.9 22.8 %collective-permute-start.26 = (bf16[160,1280]{1,0:T(8,128)(2,1)}, bf16[160,1280]{1,0:T(8,128)(2,1)}, u32[]{:S(2)}, u32[]{:S(2)}) collective-permute-start(bf16[160,1280]{1,0:T(8,128)(2,1)} %collective-permute-done.24), channel_id=1, source_target_pairs={{0,8},{8,16},{16,24},{24,28},{28,20},{20,12},{12,4},{4,0},{1,9},{9... | collective-permute-start | bytes 1228808 | tf_op jit(solution)/shard_map/ppermute | solution.py:52
  237.9 38.4 %collective-permute-start.28 = (bf16[160,1280]{1,0:T(8,128)(2,1)}, bf16[160,1280]{1,0:T(8,128)(2,1)}, u32[]{:S(2)}, u32[]{:S(2)}) collective-permute-start(bf16[160,1280]{1,0:T(8,128)(2,1)} %collective-permute-done.26), channel_id=1, source_target_pairs={{0,8},{8,16},{16,24},{24,28},{28,20},{20,12},{12,4},{4,0},{1,9},{9... | collective-permute-start | bytes 1228808 | tf_op jit(solution)/shard_map/ppermute | solution.py:52
  241.0 39.3 %collective-permute-start.29 = (bf16[160,1280]{1,0:T(8,128)(2,1)}, bf16[160,1280]{1,0:T(8,128)(2,1)S(1)}, u32[]{:S(2)}, u32[]{:S(2)}) collective-permute-start(bf16[160,1280]{1,0:T(8,128)(2,1)} %collective-permute-done.27), channel_id=1, source_target_pairs={{8,0},{16,8},{24,16},{28,24},{20,28},{12,20},{4,12},{0,4},{9,1},{1... | collective-permute-start | bytes 1228808 | tf_op jit(solution)/shard_map/ppermute | solution.py:53
  243.1 203.4 %collective-permute-start.60 = (bf16[160,2560]{1,0:T(8,128)(2,1)}, bf16[160,2560]{1,0:T(8,128)(2,1)}, u32[]{:S(2)}, u32[]{:S(2)}) collective-permute-start(bf16[160,2560]{1,0:T(8,128)(2,1)} %collective-permute-done.58), channel_id=1, source_target_pairs={{0,8},{8,16},{16,24},{24,28},{28,20},{20,12},{12,4},{4,0},{1,9},{9... | collective-permute-start | bytes 2457608 | tf_op jit(solution)/shard_map/ppermute | solution.py:52
  245.1 208.1 %collective-permute-start.61 = (bf16[160,2560]{1,0:T(8,128)(2,1)}, bf16[160,2560]{1,0:T(8,128)(2,1)}, u32[]{:S(2)}, u32[]{:S(2)}) collective-permute-start(bf16[160,2560]{1,0:T(8,128)(2,1)} %collective-permute-done.59), channel_id=1, source_target_pairs={{8,0},{16,8},{24,16},{28,24},{20,28},{12,20},{4,12},{0,4},{9,1},{1... | collective-permute-start | bytes 2457608 | tf_op jit(solution)/shard_map/ppermute | solution.py:53
  280.3 28.1 %collective-permute-start.5 = (bf16[160,2880]{1,0:T(8,128)(2,1)}, bf16[160,2880]{1,0:T(8,128)(2,1)S(1)}, u32[]{:S(2)}, u32[]{:S(2)}) collective-permute-start(bf16[160,2880]{1,0:T(8,128)(2,1)} %collective-permute-done.3), channel_id=1, source_target_pairs={{0,8},{8,16},{16,24},{24,28},{28,20},{20,12},{12,4},{4,0},{1,9},{9... | collective-permute-start | bytes 2764808 | tf_op jit(solution)/shard_map/ppermute | solution.py:52
  283.6 26.8 %collective-permute-start.6 = (bf16[160,2880]{1,0:T(8,128)(2,1)}, bf16[160,2880]{1,0:T(8,128)(2,1)S(1)}, u32[]{:S(2)}, u32[]{:S(2)}) collective-permute-start(bf16[160,2880]{1,0:T(8,128)(2,1)} %collective-permute-done.4), channel_id=1, source_target_pairs={{8,0},{16,8},{24,16},{28,24},{20,28},{12,20},{4,12},{0,4},{9,1},{1... | collective-permute-start | bytes 2764808 | tf_op jit(solution)/shard_map/ppermute | solution.py:53
  306.7 23.4 %collective-permute-start.13 = (bf16[160,2880]{1,0:T(8,128)(2,1)S(1)}, bf16[160,2880]{1,0:T(8,128)(2,1)S(1)}, u32[]{:S(2)}, u32[]{:S(2)}) collective-permute-start(bf16[160,2880]{1,0:T(8,128)(2,1)S(1)} %collective-permute-done.11), channel_id=1, source_target_pairs={{0,8},{8,16},{16,24},{24,28},{28,20},{20,12},{12,4},{4,0},{1,9},{9... | collective-permute-start | bytes 2764808 | tf_op jit(solution)/shard_map/ppermute | solution.py:52
  308.4 23.4 %collective-permute-start.14 = (bf16[160,2880]{1,0:T(8,128)(2,1)S(1)}, bf16[160,2880]{1,0:T(8,128)(2,1)S(1)}, u32[]{:S(2)}, u32[]{:S(2)}) collective-permute-start(bf16[160,2880]{1,0:T(8,128)(2,1)S(1)} %copy-done.35), channel_id=1, source_target_pairs={{8,0},{16,8},{24,16},{28,24},{20,28},{12,20},{4,12},{0,4},{9,1},{1... | collective-permute-start | bytes 2764808 | tf_op jit(solution)/shard_map/ppermute | solution.py:53
  310.4 132.8 %collective-permute-start.72 = (bf16[80,1280]{1,0:T(8,128)(2,1)}, bf16[80,1280]{1,0:T(8,128)(2,1)}, u32[]{:S(2)}, u32[]{:S(2)}) collective-permute-start(bf16[80,1280]{1,0:T(8,128)(2,1)} %slice.461), channel_id=1, source_target_pairs={{0,8},{8,16},{16,24},{24,28},{28,20},{20,12},{12,4},{4,0},{1,9},{9... | collective-permute-start | bytes 614408 | tf_op jit(solution)/shard_map/ppermute | solution.py:56
  330.2 22.7 %collective-permute-start.7 = (bf16[160,2880]{1,0:T(8,128)(2,1)S(1)}, bf16[160,2880]{1,0:T(8,128)(2,1)S(1)}, u32[]{:S(2)}, u32[]{:S(2)}) collective-permute-start(bf16[160,2880]{1,0:T(8,128)(2,1)S(1)} %collective-permute-done.5), channel_id=1, source_target_pairs={{0,8},{8,16},{16,24},{24,28},{28,20},{20,12},{12,4},{4,0},{1,9},{9... | collective-permute-start | bytes 2764808 | tf_op jit(solution)/shard_map/ppermute | solution.py:52
  331.8 23.7 %collective-permute-start.8 = (bf16[160,2880]{1,0:T(8,128)(2,1)S(1)}, bf16[160,2880]{1,0:T(8,128)(2,1)S(1)}, u32[]{:S(2)}, u32[]{:S(2)}) collective-permute-start(bf16[160,2880]{1,0:T(8,128)(2,1)S(1)} %collective-permute-done.6), channel_id=1, source_target_pairs={{8,0},{16,8},{24,16},{28,24},{20,28},{12,20},{4,12},{0,4},{9,1},{1... | collective-permute-start | bytes 2764808 | tf_op jit(solution)/shard_map/ppermute | solution.py:53
  371.5 73.4 %collective-permute-start.73 = (bf16[80,1280]{1,0:T(8,128)(2,1)}, bf16[80,1280]{1,0:T(8,128)(2,1)}, u32[]{:S(2)}, u32[]{:S(2)}) collective-permute-start(bf16[80,1280]{1,0:T(8,128)(2,1)} %slice.462), channel_id=1, source_target_pairs={{8,0},{16,8},{24,16},{28,24},{20,28},{12,20},{4,12},{0,4},{9,1},{1... | collective-permute-start | bytes 614408 | tf_op jit(solution)/shard_map/ppermute | solution.py:57
  394.4 26.8 %collective-permute-start.17 = (bf16[80,2880]{1,0:T(8,128)(2,1)S(1)}, bf16[80,2880]{1,0:T(8,128)(2,1)}, u32[]{:S(2)}, u32[]{:S(2)}) collective-permute-start(bf16[80,2880]{1,0:T(8,128)(2,1)S(1)} %slice.442), channel_id=1, source_target_pairs={{0,8},{8,16},{16,24},{24,28},{28,20},{20,12},{12,4},{4,0},{1,9},{9... | collective-permute-start | bytes 1382408 | tf_op jit(solution)/shard_map/ppermute | solution.py:56
  468.2 34.8 %collective-permute-start.64 = (bf16[80,2560]{1,0:T(8,128)(2,1)}, bf16[80,2560]{1,0:T(8,128)(2,1)}, u32[]{:S(2)}, u32[]{:S(2)}) collective-permute-start(bf16[80,2560]{1,0:T(8,128)(2,1)} %slice.457), channel_id=1, source_target_pairs={{0,8},{8,16},{16,24},{24,28},{28,20},{20,12},{12,4},{4,0},{1,9},{9... | collective-permute-start | bytes 1228808 | tf_op jit(solution)/shard_map/ppermute | solution.py:56
  475.2 50.2 %collective-permute-start.65 = (bf16[80,2560]{1,0:T(8,128)(2,1)}, bf16[80,2560]{1,0:T(8,128)(2,1)}, u32[]{:S(2)}, u32[]{:S(2)}) collective-permute-start(bf16[80,2560]{1,0:T(8,128)(2,1)} %slice.458), channel_id=1, source_target_pairs={{8,0},{16,8},{24,16},{28,24},{20,28},{12,20},{4,12},{0,4},{9,1},{1... | collective-permute-start | bytes 1228808 | tf_op jit(solution)/shard_map/ppermute | solution.py:57
  504.8 22.7 %collective-permute-start.77 = (bf16[2,64,1280]{2,1,0:T(8,128)(2,1)}, bf16[2,64,1280]{2,1,0:T(8,128)(2,1)}, u32[]{:S(2)}, u32[]{:S(2)}) collective-permute-start(bf16[2,64,1280]{2,1,0:T(8,128)(2,1)} %get-tuple-element.283), channel_id=1, source_target_pairs={{0,2},{2,0},{1,3},{3,1},{4,6},{6,4},{5,7},{7,5},{8,10},{10,8},{9,1... | collective-permute-start | bytes 983048 | tf_op jit(solution)/shard_map/ppermute | solution.py:110
  578.3 37.0 %collective-permute-start.74 = (bf16[2,2,64,1280]{3,2,0,1:T(8,128)(2,1)S(1)}, bf16[2,2,64,1280]{3,2,0,1:T(8,128)(2,1)S(1)}, u32[]{:S(2)}, u32[]{:S(2)}) collective-permute-start(bf16[2,2,64,1280]{3,2,0,1:T(8,128)(2,1)S(1)} %fusion.111), channel_id=1, source_target_pairs={{0,1},{1,0},{2,3},{3,2},{4,5},{5,4},{6,7},{7,6},{8,9},{9,8},{10,11... | collective-permute-start | bytes 1966088 | tf_op jit(solution)/shard_map/ppermute | solution.py:130
  585.1 29.6 %collective-permute-start.79 = (bf16[2,2,64,1280]{3,2,0,1:T(8,128)(2,1)S(1)}, bf16[2,2,64,1280]{3,2,0,1:T(8,128)(2,1)S(1)}, u32[]{:S(2)}, u32[]{:S(2)}) collective-permute-start(bf16[2,2,64,1280]{3,2,0,1:T(8,128)(2,1)S(1)} %fusion.107), channel_id=1, source_target_pairs={{0,1},{1,0},{2,3},{3,2},{4,5},{5,4},{6,7},{7,6},{8,9},{9,8},{10,11... | collective-permute-start | bytes 1966088 | tf_op jit(solution)/shard_map/ppermute | solution.py:130
  595.0 37.1 %collective-permute-start.149 = (bf16[160,1280]{1,0:T(8,128)(2,1)}, bf16[160,1280]{1,0:T(8,128)(2,1)}, u32[]{:S(2)}, u32[]{:S(2)}) collective-permute-start(bf16[160,1280]{1,0:T(8,128)(2,1)} %pad_maximum_fusion.53), channel_id=1, source_target_pairs={{8,0},{16,8},{24,16},{28,24},{20,28},{12,20},{4,12},{0,4},{9,1},{1... | collective-permute-start | bytes 1228808 | tf_op jit(solution)/shard_map/ppermute | solution.py:88
  607.2 85.5 %collective-permute-start.141 = (bf16[160,2560]{1,0:T(8,128)(2,1)}, bf16[160,2560]{1,0:T(8,128)(2,1)}, u32[]{:S(2)}, u32[]{:S(2)}) collective-permute-start(bf16[160,2560]{1,0:T(8,128)(2,1)} %pad_maximum_fusion.33), channel_id=1, source_target_pairs={{8,0},{16,8},{24,16},{28,24},{20,28},{12,20},{4,12},{0,4},{9,1},{1... | collective-permute-start | bytes 2457608 | tf_op jit(solution)/shard_map/ppermute | solution.py:88
  612.3 30.3 %collective-permute-start.137 = (bf16[160,2560]{1,0:T(8,128)(2,1)}, bf16[160,2560]{1,0:T(8,128)(2,1)}, u32[]{:S(2)}, u32[]{:S(2)}) collective-permute-start(bf16[160,2560]{1,0:T(8,128)(2,1)} %pad_maximum_fusion.32), channel_id=1, source_target_pairs={{0,8},{8,16},{16,24},{24,28},{28,20},{20,12},{12,4},{4,0},{1,9},{9... | collective-permute-start | bytes 2457608 | tf_op jit(solution)/shard_map/ppermute | solution.py:87
  614.7 25.3 %collective-permute-start.146 = (bf16[160,1280]{1,0:T(8,128)(2,1)}, bf16[160,1280]{1,0:T(8,128)(2,1)}, u32[]{:S(2)}, u32[]{:S(2)}) collective-permute-start(bf16[160,1280]{1,0:T(8,128)(2,1)} %fusion.93), channel_id=1, source_target_pairs={{0,8},{8,16},{16,24},{24,28},{28,20},{20,12},{12,4},{4,0},{1,9},{9... | collective-permute-start | bytes 1228808 | tf_op jit(solution)/shard_map/ppermute | solution.py:87
  642.6 45.7 %collective-permute-start.147 = (bf16[160,1280]{1,0:T(8,128)(2,1)}, bf16[160,1280]{1,0:T(8,128)(2,1)}, u32[]{:S(2)}, u32[]{:S(2)}) collective-permute-start(bf16[160,1280]{1,0:T(8,128)(2,1)} %get-tuple-element.178), channel_id=1, source_target_pairs={{0,8},{8,16},{16,24},{24,28},{28,20},{20,12},{12,4},{4,0},{1,9},{9... | collective-permute-start | bytes 1228808 | tf_op jit(solution)/shard_map/ppermute | solution.py:87
  646.9 45.8 %collective-permute-start.138 = (bf16[160,2560]{1,0:T(8,128)(2,1)}, bf16[160,2560]{1,0:T(8,128)(2,1)}, u32[]{:S(2)}, u32[]{:S(2)}) collective-permute-start(bf16[160,2560]{1,0:T(8,128)(2,1)} %fusion.49), channel_id=1, source_target_pairs={{0,8},{8,16},{16,24},{24,28},{28,20},{20,12},{12,4},{4,0},{1,9},{9... | collective-permute-start | bytes 2457608 | tf_op jit(solution)/shard_map/ppermute | solution.py:87
  653.2 36.7 %collective-permute-start.151 = (bf16[160,1280]{1,0:T(8,128)(2,1)}, bf16[160,1280]{1,0:T(8,128)(2,1)}, u32[]{:S(2)}, u32[]{:S(2)}) collective-permute-start(bf16[160,1280]{1,0:T(8,128)(2,1)} %fusion.92), channel_id=1, source_target_pairs={{8,0},{16,8},{24,16},{28,24},{20,28},{12,20},{4,12},{0,4},{9,1},{1... | collective-permute-start | bytes 1228808 | tf_op jit(solution)/shard_map/ppermute | solution.py:88
  696.3 41.4 %collective-permute-start.142 = (bf16[160,2560]{1,0:T(8,128)(2,1)}, bf16[160,2560]{1,0:T(8,128)(2,1)}, u32[]{:S(2)}, u32[]{:S(2)}) collective-permute-start(bf16[160,2560]{1,0:T(8,128)(2,1)} %get-tuple-element.171), channel_id=1, source_target_pairs={{8,0},{16,8},{24,16},{28,24},{20,28},{12,20},{4,12},{0,4},{9,1},{1... | collective-permute-start | bytes 2457608 | tf_op jit(solution)/shard_map/ppermute | solution.py:88
  696.6 90.6 %collective-permute-start.139 = (bf16[160,2560]{1,0:T(8,128)(2,1)}, bf16[160,2560]{1,0:T(8,128)(2,1)}, u32[]{:S(2)}, u32[]{:S(2)}) collective-permute-start(bf16[160,2560]{1,0:T(8,128)(2,1)} %get-tuple-element.170), channel_id=1, source_target_pairs={{0,8},{8,16},{16,24},{24,28},{28,20},{20,12},{12,4},{4,0},{1,9},{9... | collective-permute-start | bytes 2457608 | tf_op jit(solution)/shard_map/ppermute | solution.py:87
  698.5 25.1 %collective-permute-start.130 = (bf16[256,640]{0,1:T(8,128)(2,1)S(1)}, bf16[256,640]{0,1:T(8,128)(2,1)S(1)}, u32[]{:S(2)}, u32[]{:S(2)}) collective-permute-start(bf16[256,640]{0,1:T(8,128)(2,1)S(1)} %fusion.114), channel_id=1, source_target_pairs={{0,8},{8,16},{16,24},{24,28},{28,20},{20,12},{12,4},{4,0},{1,9},{9... | collective-permute-start | bytes 983048 | tf_op jit(solution)/shard_map/ppermute | solution.py:87
  700.5 25.7 %collective-permute-start.134 = (bf16[256,640]{0,1:T(8,128)(2,1)S(1)}, bf16[256,640]{0,1:T(8,128)(2,1)S(1)}, u32[]{:S(2)}, u32[]{:S(2)}) collective-permute-start(bf16[256,640]{0,1:T(8,128)(2,1)S(1)} %fusion.112), channel_id=1, source_target_pairs={{8,0},{16,8},{24,16},{28,24},{20,28},{12,20},{4,12},{0,4},{9,1},{1... | collective-permute-start | bytes 983048 | tf_op jit(solution)/shard_map/ppermute | solution.py:88
  701.3 26.0 %collective-permute-start.85 = (bf16[2,64,1280]{2,1,0:T(8,128)(2,1)S(1)}, bf16[2,64,1280]{2,1,0:T(8,128)(2,1)S(1)}, u32[]{:S(2)}, u32[]{:S(2)}) collective-permute-start(bf16[2,64,1280]{2,1,0:T(8,128)(2,1)S(1)} %fusion.151), channel_id=1, source_target_pairs={{0,2},{2,0},{1,3},{3,1},{4,6},{6,4},{5,7},{7,5},{8,10},{10,8},{9,1... | collective-permute-start | bytes 983048 | tf_op jit(solution)/shard_map/ppermute | solution.py:136
  740.3 48.3 %collective-permute-start.143 = (bf16[160,2560]{1,0:T(8,128)(2,1)}, bf16[160,2560]{1,0:T(8,128)(2,1)}, u32[]{:S(2)}, u32[]{:S(2)}) collective-permute-start(bf16[160,2560]{1,0:T(8,128)(2,1)} %fusion.48), channel_id=1, source_target_pairs={{8,0},{16,8},{24,16},{28,24},{20,28},{12,20},{4,12},{0,4},{9,1},{1... | collective-permute-start | bytes 2457608 | tf_op jit(solution)/shard_map/ppermute | solution.py:88
  755.1 50.9 %collective-permute-start.89 = (bf16[2,2,64,1280]{3,2,0,1:T(8,128)(2,1)}, bf16[2,2,64,1280]{3,2,0,1:T(8,128)(2,1)}, u32[]{:S(2)}, u32[]{:S(2)}) collective-permute-start(bf16[2,2,64,1280]{3,2,0,1:T(8,128)(2,1)} %fusion.109), channel_id=1, source_target_pairs={{0,1},{1,0},{2,3},{3,2},{4,5},{5,4},{6,7},{7,6},{8,9},{9,8},{10,11... | collective-permute-start | bytes 1966088 | tf_op jit(solution)/shard_map/ppermute | solution.py:130
  786.3 31.6 %collective-permute-start.117 = (bf16[160,1280]{1,0:T(8,128)(2,1)}, bf16[160,1280]{1,0:T(8,128)(2,1)}, u32[]{:S(2)}, u32[]{:S(2)}) collective-permute-start(bf16[160,1280]{1,0:T(8,128)(2,1)} %pad_maximum_fusion.51), channel_id=1, source_target_pairs={{8,0},{16,8},{24,16},{28,24},{20,28},{12,20},{4,12},{0,4},{9,1},{1... | collective-permute-start | bytes 1228808 | tf_op jit(solution)/shard_map/ppermute | solution.py:88
  821.4 106.7 %collective-permute-start.115 = (bf16[160,1280]{1,0:T(8,128)(2,1)}, bf16[160,1280]{1,0:T(8,128)(2,1)}, u32[]{:S(2)}, u32[]{:S(2)}) collective-permute-start(bf16[160,1280]{1,0:T(8,128)(2,1)} %get-tuple-element.186), channel_id=1, source_target_pairs={{0,8},{8,16},{16,24},{24,28},{28,20},{20,12},{12,4},{4,0},{1,9},{9... | collective-permute-start | bytes 1228808 | tf_op jit(solution)/shard_map/ppermute | solution.py:87
  833.9 94.5 %collective-permute-start.119 = (bf16[160,1280]{1,0:T(8,128)(2,1)}, bf16[160,1280]{1,0:T(8,128)(2,1)}, u32[]{:S(2)}, u32[]{:S(2)}) collective-permute-start(bf16[160,1280]{1,0:T(8,128)(2,1)} %fusion.100), channel_id=1, source_target_pairs={{8,0},{16,8},{24,16},{28,24},{20,28},{12,20},{4,12},{0,4},{9,1},{1... | collective-permute-start | bytes 1228808 | tf_op jit(solution)/shard_map/ppermute | solution.py:88
  876.2 73.3 %collective-permute-start.94 = (bf16[2,2,64,1280]{3,2,0,1:T(8,128)(2,1)S(1)}, bf16[2,2,64,1280]{3,2,0,1:T(8,128)(2,1)}, u32[]{:S(2)}, u32[]{:S(2)}) collective-permute-start(bf16[2,2,64,1280]{3,2,0,1:T(8,128)(2,1)S(1)} %fusion.110), channel_id=1, source_target_pairs={{0,1},{1,0},{2,3},{3,2},{4,5},{5,4},{6,7},{7,6},{8,9},{9,8},{10,11... | collective-permute-start | bytes 1966088 | tf_op jit(solution)/shard_map/ppermute | solution.py:130
  896.6 35.9 %collective-permute-start.100 = (bf16[80,2880]{1,0:T(8,128)(2,1)}, bf16[80,2880]{1,0:T(8,128)(2,1)}, u32[]{:S(2)}, u32[]{:S(2)}) collective-permute-start(bf16[80,2880]{1,0:T(8,128)(2,1)} %get-tuple-element.168), channel_id=1, source_target_pairs={{8,0},{16,8},{24,16},{28,24},{20,28},{12,20},{4,12},{0,4},{9,1},{1... | collective-permute-start | bytes 1382408 | tf_op jit(solution)/shard_map/ppermute | solution.py:78
  938.7 52.8 %collective-permute-start.101 = (bf16[160,2880]{1,0:T(8,128)(2,1)S(1)}, bf16[160,2880]{1,0:T(8,128)(2,1)S(1)}, u32[]{:S(2)}, u32[]{:S(2)}) collective-permute-start(bf16[160,2880]{1,0:T(8,128)(2,1)S(1)} %pad_maximum_fusion.13), channel_id=1, source_target_pairs={{8,0},{16,8},{24,16},{28,24},{20,28},{12,20},{4,12},{0,4},{9,1},{1... | collective-permute-start | bytes 2764808 | tf_op jit(solution)/shard_map/ppermute | solution.py:88
  940.9 26.2 %collective-permute-start.97 = (bf16[160,2880]{1,0:T(8,128)(2,1)S(1)}, bf16[160,2880]{1,0:T(8,128)(2,1)S(1)}, u32[]{:S(2)}, u32[]{:S(2)}) collective-permute-start(bf16[160,2880]{1,0:T(8,128)(2,1)S(1)} %pad_maximum_fusion.12), channel_id=1, source_target_pairs={{0,8},{8,16},{16,24},{24,28},{28,20},{20,12},{12,4},{4,0},{1,9},{9... | collective-permute-start | bytes 2764808 | tf_op jit(solution)/shard_map/ppermute | solution.py:87
  947.3 65.6 %collective-permute-start.109 = (bf16[160,2880]{1,0:T(8,128)(2,1)S(1)}, bf16[160,2880]{1,0:T(8,128)(2,1)S(1)}, u32[]{:S(2)}, u32[]{:S(2)}) collective-permute-start(bf16[160,2880]{1,0:T(8,128)(2,1)S(1)} %pad_maximum_fusion.15), channel_id=1, source_target_pairs={{8,0},{16,8},{24,16},{28,24},{20,28},{12,20},{4,12},{0,4},{9,1},{1... | collective-permute-start | bytes 2764808 | tf_op jit(solution)/shard_map/ppermute | solution.py:88
  949.4 37.9 %collective-permute-start.105 = (bf16[160,2880]{1,0:T(8,128)(2,1)S(1)}, bf16[160,2880]{1,0:T(8,128)(2,1)S(1)}, u32[]{:S(2)}, u32[]{:S(2)}) collective-permute-start(bf16[160,2880]{1,0:T(8,128)(2,1)S(1)} %pad_maximum_fusion.14), channel_id=1, source_target_pairs={{0,8},{8,16},{16,24},{24,28},{28,20},{20,12},{12,4},{4,0},{1,9},{9... | collective-permute-start | bytes 2764808 | tf_op jit(solution)/shard_map/ppermute | solution.py:87
  968.5 39.0 %collective-permute-start.98 = (bf16[160,2880]{1,0:T(8,128)(2,1)S(1)}, bf16[160,2880]{1,0:T(8,128)(2,1)S(1)}, u32[]{:S(2)}, u32[]{:S(2)}) collective-permute-start(bf16[160,2880]{1,0:T(8,128)(2,1)S(1)} %fusion.44), channel_id=1, source_target_pairs={{0,8},{8,16},{16,24},{24,28},{28,20},{20,12},{12,4},{4,0},{1,9},{9... | collective-permute-start | bytes 2764808 | tf_op jit(solution)/shard_map/ppermute | solution.py:87
  987.5 39.5 %collective-permute-start.106 = (bf16[160,2880]{1,0:T(8,128)(2,1)S(1)}, bf16[160,2880]{1,0:T(8,128)(2,1)S(1)}, u32[]{:S(2)}, u32[]{:S(2)}) collective-permute-start(bf16[160,2880]{1,0:T(8,128)(2,1)S(1)} %fusion.39), channel_id=1, source_target_pairs={{0,8},{8,16},{16,24},{24,28},{28,20},{20,12},{12,4},{4,0},{1,9},{9... | collective-permute-start | bytes 2764808 | tf_op jit(solution)/shard_map/ppermute | solution.py:87
  989.7 40.7 %collective-permute-start.95 = (bf16[2,64,1280]{2,1,0:T(8,128)(2,1)S(1)}, bf16[2,64,1280]{2,1,0:T(8,128)(2,1)S(1)}, u32[]{:S(2)}, u32[]{:S(2)}) collective-permute-start(bf16[2,64,1280]{2,1,0:T(8,128)(2,1)S(1)} %fusion.153), channel_id=1, source_target_pairs={{0,2},{2,0},{1,3},{3,1},{4,6},{6,4},{5,7},{7,5},{8,10},{10,8},{9,1... | collective-permute-start | bytes 983048 | tf_op jit(solution)/shard_map/ppermute | solution.py:136
  1010.7 36.9 %collective-permute-start.102 = (bf16[160,2880]{1,0:T(8,128)(2,1)}, bf16[160,2880]{1,0:T(8,128)(2,1)S(1)}, u32[]{:S(2)}, u32[]{:S(2)}) collective-permute-start(bf16[160,2880]{1,0:T(8,128)(2,1)} %get-tuple-element.163), channel_id=1, source_target_pairs={{8,0},{16,8},{24,16},{28,24},{20,28},{12,20},{4,12},{0,4},{9,1},{1... | collective-permute-start | bytes 2764808 | tf_op jit(solution)/shard_map/ppermute | solution.py:88
  1028.8 26.3 %collective-permute-start.110 = (bf16[160,2880]{1,0:T(8,128)(2,1)}, bf16[160,2880]{1,0:T(8,128)(2,1)}, u32[]{:S(2)}, u32[]{:S(2)}) collective-permute-start(bf16[160,2880]{1,0:T(8,128)(2,1)} %get-tuple-element.155), channel_id=1, source_target_pairs={{8,0},{16,8},{24,16},{28,24},{20,28},{12,20},{4,12},{0,4},{9,1},{1... | collective-permute-start | bytes 2764808 | tf_op jit(solution)/shard_map/ppermute | solution.py:88
  1032.1 27.2 %all-to-all-start.4 = ((f32[32,1,800]{2,1,0:T(1,128)}), f32[32,1,800]{2,1,0:T(1,128)S(1)}, u32[]{:S(2)}, u32[]{:S(2)}) async-start(f32[32,1,800]{2,1,0:T(1,128)} %reshape.960), calls=%async_computation.4 | async-start | bytes 229376 | tf_op jit(solution)/shard_map/all_to_all | solution.py:505
  1044.7 24.2 %collective-permute-start.99 = (bf16[160,2880]{1,0:T(8,128)(2,1)}, bf16[160,2880]{1,0:T(8,128)(2,1)}, u32[]{:S(2)}, u32[]{:S(2)}) collective-permute-start(bf16[160,2880]{1,0:T(8,128)(2,1)} %get-tuple-element.162), channel_id=1, source_target_pairs={{0,8},{8,16},{16,24},{24,28},{28,20},{20,12},{12,4},{4,0},{1,9},{9... | collective-permute-start | bytes 2764808 | tf_op jit(solution)/shard_map/ppermute | solution.py:87
  1046.1 40.0 %collective-permute-start.107 = (bf16[160,2880]{1,0:T(8,128)(2,1)}, bf16[160,2880]{1,0:T(8,128)(2,1)}, u32[]{:S(2)}, u32[]{:S(2)}) collective-permute-start(bf16[160,2880]{1,0:T(8,128)(2,1)} %get-tuple-element.154), channel_id=1, source_target_pairs={{0,8},{8,16},{16,24},{24,28},{28,20},{20,12},{12,4},{4,0},{1,9},{9... | collective-permute-start | bytes 2764808 | tf_op jit(solution)/shard_map/ppermute | solution.py:87
  1050.1 36.1 %collective-permute-start.103 = (bf16[160,2880]{1,0:T(8,128)(2,1)}, bf16[160,2880]{1,0:T(8,128)(2,1)}, u32[]{:S(2)}, u32[]{:S(2)}) collective-permute-start(bf16[160,2880]{1,0:T(8,128)(2,1)} %fusion.43), channel_id=1, source_target_pairs={{8,0},{16,8},{24,16},{28,24},{20,28},{12,20},{4,12},{0,4},{9,1},{1... | collective-permute-start | bytes 2764808 | tf_op jit(solution)/shard_map/ppermute | solution.py:88
  1056.8 38.4 %collective-permute-start.111 = (bf16[160,2880]{1,0:T(8,128)(2,1)S(1)}, bf16[160,2880]{1,0:T(8,128)(2,1)}, u32[]{:S(2)}, u32[]{:S(2)}) collective-permute-start(bf16[160,2880]{1,0:T(8,128)(2,1)S(1)} %fusion.38), channel_id=1, source_target_pairs={{8,0},{16,8},{24,16},{28,24},{20,28},{12,20},{4,12},{0,4},{9,1},{1... | collective-permute-start | bytes 2764808 | tf_op jit(solution)/shard_map/ppermute | solution.py:88
  (234 other events, 4825.9 us)

commit v2 on v1

v2 whole, which is shorter than its diff:
```python
import math

import jax
import jax.numpy as jnp
from jax import lax
from jax.experimental.layout import Layout, with_layout_constraint
from jax.sharding import PartitionSpec as P

C = 1280
HEAD_DIM = 64
GN_GROUPS = 32
SIDE = 16
TAPS = 9

highest = lax.Precision.HIGHEST
f32 = jnp.float32
bf16 = jnp.bfloat16


def ring_order(size):
    return list(range(0, size, 2)) + list(range(size - 1, 0, -2))


def ring_pairs(size):
    order = ring_order(size)
    right = [(order[i], order[(i + 1) % size]) for i in range(size)]
    return right, [(b, a) for a, b in right]


def ring_place(size):
    order = ring_order(size)
    place = jnp.array([order.index(i) for i in range(size)], jnp.int32)
    return jnp.array(order, jnp.int32), place[lax.axis_index("dp")]


class Gathered:
    def __init__(self, ring, pack, *parts):
        self.ring, self.pack, self.parts, self.taken = ring, pack, parts, 0

    def put(self, part, away, start):
        place = (self.ring.owner(away), jnp.int32(start), jnp.int32(0))
        self.whole = lax.dynamic_update_slice(self.whole, part[None], place)

    def begin(self):
        ring = self.ring
        if not ring.whole:
            self.whole = lax.all_gather(self.pack(*self.parts), "dp", axis=0, tiled=True)
            return
        zero = jnp.zeros((), self.parts[0].dtype)
        parts = self.parts
        if ring.last:
            zero, *parts = ring.hold(zero, *parts)
        self.block = self.pack(*parts)
        self.whole = jnp.broadcast_to(zero, (ring.size,) + self.block.shape)
        self.put(self.block, 0, 0)
        self.from_left = self.from_right = self.block

    def step(self):
        ring = self.ring
        if not ring.whole:
            return
        self.taken += 1
        size = ring.size
        rows, columns = self.block.shape
        if self.taken < size // 2:
            self.from_left, self.from_right = ring.step(self.from_left, self.from_right)
            self.put(self.from_left, size - self.taken, 0)
            self.put(self.from_right, self.taken, 0)
        else:
            half = rows // 2
            first, second = ring.step(self.from_left[:half], self.from_right[half:])
            self.put(first, size // 2, 0)
            self.put(second, size // 2, half)
            self.whole = self.whole.reshape(size * rows, columns)


class Scattered:
    def __init__(self, ring, *grads):
        self.ring, self.taken = ring, 0
        if not ring.whole:
            parts = [lax.psum_scatter(g, "dp", scatter_dimension=0, tiled=True) for g in grads]
            self.part = jnp.concatenate(parts).astype(f32)
            return
        self.blocks = [g.reshape(ring.size, -1, g.shape[1]) for g in grads]

    def own(self, away):
        place = self.ring.owner(away)
        return jnp.concatenate(
            [lax.dynamic_index_in_dim(b, place, 0, keepdims=False) for b in self.blocks]
        )

    def step(self):
        ring = self.ring
        if not ring.whole:
            return
        size = ring.size
        half = sum(b.shape[1] for b in self.blocks) // 2
        away = size // 2 - self.taken
        self.taken += 1
        ahead, behind = self.own(away), self.own(size - away)
        if self.taken == 1:
            ahead, behind = ahead[:half], behind[half:]
        elif self.taken == 2:
            ahead = jnp.concatenate(
                [(ahead[:half].astype(f32) + self.from_left).astype(bf16), ahead[half:]]
            )
            behind = jnp.concatenate(
                [behind[:half], (behind[half:].astype(f32) + self.from_right).astype(bf16)]
            )
        else:
            ahead = (ahead.astype(f32) + self.from_left).astype(bf16)
            behind = (behind.astype(f32) + self.from_right).astype(bf16)
        self.from_left, self.from_right = ring.step(by_rows(ahead), by_rows(behind))
        if away == 1:
            self.part = (
                self.own(0).astype(f32)
                + self.from_left.astype(f32)
                + self.from_right.astype(f32)
            )


class Ring:
    def __init__(self):
        self.size = lax.axis_size("dp")
        self.whole = self.size == 8
        self.last = ()
        if self.whole:
            self.right, self.left = ring_pairs(self.size)
            self.order, self.place = ring_place(self.size)

    def step(self, to_right, to_left):
        if self.last:
            to_right = lax.optimization_barrier((to_right, self.last[0]))[0]
            to_left = lax.optimization_barrier((to_left, self.last[1]))[0]
        self.last = (
            lax.ppermute(to_right, "dp", self.right),
            lax.ppermute(to_left, "dp", self.left),
        )
        return self.last

    def hold(self, *values):
        held = lax.optimization_barrier(tuple(values) + self.last)[: len(values)]
        return held[0] if len(values) == 1 else held

    def owner(self, away):
        return self.order[(self.place + away) % self.size]


def share_small(values, axis):
    size = lax.axis_size(axis)
    return lax.all_to_all(
        jnp.broadcast_to(values[None], (size,) + values.shape), axis, 0, 0, tiled=True
    )


def mp_bits():
    me = lax.axis_index("mp")
    return me % 2, me // 2


NEAR = [(0, 1), (1, 0), (2, 3), (3, 2)]
FAR = [(0, 2), (2, 0), (1, 3), (3, 1)]


def gather_rows(values):
    near_bit, far_bit = mp_bits()
    far = lax.ppermute(values, "mp", FAR)
    near = lax.ppermute(values, "mp", NEAR)
    both = lax.ppermute(far, "mp", NEAR)

    def pair(mine, other, bit):
        return jnp.concatenate(
            [jnp.where(bit == 0, mine, other), jnp.where(bit == 0, other, mine)], axis=1
        )

    return pair(pair(values, near, near_bit), pair(far, both, near_bit), far_bit)


def sum_rows(values, items):
    near_bit, far_bit = mp_bits()
    columns = values.shape[-1]
    parts = values.reshape(items, 2, 2, -1, columns)

    def near_part(bit):
        return lax.dynamic_index_in_dim(parts, bit, 2, keepdims=False)

    got = lax.ppermute(near_part(1 - near_bit).astype(bf16), "mp", NEAR)
    held = near_part(near_bit).astype(f32) + got.astype(f32)

    def far_part(bit):
        return lax.dynamic_index_in_dim(held, bit, 1, keepdims=False)

    got = lax.ppermute(far_part(1 - far_bit).astype(bf16), "mp", FAR)
    return far_part(far_bit) + got.astype(f32)


def by_rows(values):
    return with_layout_constraint(values, Layout(major_to_minor=tuple(range(values.ndim))))


def flat(values):
    return values.reshape(-1, values.shape[-1])


def product(former, latter):
    return jnp.dot(former, latter, preferred_element_type=f32)


def product_back(former, latter):
    return lax.dot_general(former, latter, (((1,), (1,)), ((), ())), preferred_element_type=f32)


def product_down(former, latter):
    return lax.dot_general(former, latter, (((0,), (0,)), ((), ())), preferred_element_type=f32)


def weight_grad(former, latter):
    return by_rows(product_down(former, latter).astype(bf16))


def tap_sources(widths, item_rows):
    row = jnp.arange(item_rows, dtype=jnp.int32)
    step = jnp.arange(TAPS, dtype=jnp.int32)
    row_step, column_step = step // 3 - 1, step % 3 - 1
    column = row[None, :] % widths[:, None]
    beside = column[:, None, :] + column_step[None, :, None]
    usable = (beside >= 0) & (beside < widths[:, None, None])
    source = (
        row[None, None, :]
        + row_step[None, :, None] * widths[:, None, None]
        + column_step[None, :, None]
    )
    return jnp.where(usable, source, -1)


def tap_matrices(widths, item_rows):
    source = tap_sources(widths, item_rows)
    row = jnp.arange(item_rows, dtype=jnp.int32)
    tall = (source[:, :, :, None] == row).astype(bf16)
    tall = [by_rows(one.reshape(TAPS * item_rows, item_rows)) for one in tall]
    by_row = jnp.swapaxes(source, 1, 2)
    wide = (by_row[:, :, :, None] == row).astype(bf16)
    wide = [by_rows(one.reshape(item_rows, TAPS * item_rows)) for one in wide]
    return tall, wide


def items_of(values, count):
    rows = values.shape[0] // count
    return [values[i * rows : (i + 1) * rows] for i in range(count)]


def beside(stacked):
    rows = stacked.shape[0] // TAPS
    return jnp.concatenate([stacked[t * rows : (t + 1) * rows] for t in range(TAPS)], axis=1)


def below(values):
    columns = values.shape[1] // TAPS
    return jnp.concatenate(
        [values[:, t * columns : (t + 1) * columns] for t in range(TAPS)], axis=0
    )


def shift_stack(tall, values):
    return by_rows(
        jnp.concatenate(
            [
                beside(product(tap, item).astype(bf16))
                for tap, item in zip(tall, items_of(values, len(tall)))
            ]
        )
    )


def shift_stack_back(wide, values):
    return by_rows(
        jnp.concatenate(
            [
                beside(product_down(tap, item).astype(bf16))
                for tap, item in zip(wide, items_of(values, len(wide)))
            ]
        )
    )


def shift_sum(wide, values):
    return jnp.stack(
        [product(tap, below(item)) for tap, item in zip(wide, items_of(values, len(wide)))]
    )


def shift_sum_back(tall, values):
    return jnp.stack(
        [product_down(tap, below(item)) for tap, item in zip(tall, items_of(values, len(tall)))]
    )


def norm_rows(hidden, factor):
    center = hidden - jnp.mean(hidden, axis=-1, keepdims=True)
    scaling = lax.rsqrt(jnp.mean(center * center, axis=-1, keepdims=True) + 1e-05)
    normal = center * scaling
    return ((normal * factor).astype(bf16), normal, scaling)


def norm_rows_back(gradient, normal, scaling, factor):
    scaled = gradient * factor
    offset = jnp.mean(scaled, axis=-1, keepdims=True)
    slopes = jnp.mean(scaled * normal, axis=-1, keepdims=True)
    return (scaling * (scaled - offset - normal * slopes), jnp.sum(gradient * normal, axis=(0, 1)))


def group_sum(values, per_group):
    rows_summed = jnp.sum(values, axis=1)
    return rows_summed.reshape(values.shape[0], values.shape[2] // per_group, per_group).sum(-1)


def spread(values, per_group):
    return jnp.repeat(values, per_group, axis=-1)[:, None, :]


def silu_back(scaled, gradient):
    share = jax.nn.sigmoid(scaled)
    return gradient * share * (1.0 + scaled * (1.0 - share))


def split_heads(values):
    return values.reshape(values.shape[0], values.shape[1], values.shape[2] // HEAD_DIM, HEAD_DIM)


def attend(query_rows, key_rows, value_rows, key_valid):
    scores = jnp.einsum(
        "sqhd,skhd->shqk",
        split_heads(query_rows),
        split_heads(key_rows),
        preferred_element_type=f32,
    ) * HEAD_DIM ** (-0.5)
    if key_valid is not None:
        scores = jnp.where(key_valid[:, None, None, :], scores, -1e30)
    exponent = jnp.exp(scores - jnp.max(scores, axis=-1, keepdims=True))
    chances = exponent / jnp.sum(exponent, axis=-1, keepdims=True)
    mixture = jnp.einsum(
        "shqk,skhd->sqhd",
        chances.astype(bf16),
        split_heads(value_rows),
        preferred_element_type=f32,
    )
    return mixture.reshape(query_rows.shape).astype(bf16), chances


def attend_back(query_rows, key_rows, value_rows, mixture_grad, chances):
    query_heads = split_heads(query_rows)
    key_heads = split_heads(key_rows)
    value_heads = split_heads(value_rows)
    grad_heads = split_heads(mixture_grad)
    value_grad = jnp.einsum(
        "shqk,sqhd->skhd", chances.astype(bf16), grad_heads, preferred_element_type=f32
    )
    share_grad = jnp.einsum(
        "sqhd,skhd->shqk", grad_heads, value_heads, preferred_element_type=f32
    )
    inner_sum = jnp.sum(chances * share_grad, axis=-1, keepdims=True)
    score_grad = (chances * (share_grad - inner_sum)).astype(bf16)
    query_grad = jnp.einsum(
        "shqk,skhd->sqhd", score_grad, key_heads, preferred_element_type=f32
    ) * HEAD_DIM ** (-0.5)
    key_grad = jnp.einsum(
        "shqk,sqhd->skhd", score_grad, query_heads, preferred_element_type=f32
    ) * HEAD_DIM ** (-0.5)
    return (
        query_grad.reshape(query_rows.shape).astype(bf16),
        key_grad.reshape(key_rows.shape).astype(bf16),
        value_grad.reshape(value_rows.shape).astype(bf16),
    )


def body(
    latent,
    text_embeds,
    cotangent,
    item_count,
    bucket,
    timestep,
    conv_in,
    conv_out,
    time_weight,
    self_query,
    self_key,
    self_value,
    self_out,
    cross_query,
    cross_key,
    cross_value,
    cross_out,
    ff_value,
    ff_gate,
    ff_down,
    gn_in_gain,
    gn_mid_gain,
    self_gain,
    cross_gain,
    ff_gain,
):
    slot_count, local_rows, channels = latent.shape
    dp_size, mp_size = lax.axis_size("dp"), lax.axis_size("mp")
    item_rows = local_rows * mp_size
    per_group = channels // GN_GROUPS
    own_channels = conv_in.shape[3]
    share = conv_in.shape[2]
    dp_index, mp_index = lax.axis_index("dp"), lax.axis_index("mp")
    is_live = (jnp.arange(slot_count, dtype=jnp.int32) < item_count[0]).astype(f32)
    widths = jnp.where(
        bucket == 0, SIDE, jnp.where(bucket == 1, 5 * SIDE // 4, 3 * SIDE // 2)
    ).astype(jnp.int32)
    heights = jnp.where(
        bucket == 0, SIDE, jnp.where(bucket == 1, 3 * SIDE // 4, 5 * SIDE // 8)
    ).astype(jnp.int32)
    filled = widths * heights
    position = mp_index * local_rows + jnp.arange(local_rows, dtype=jnp.int32)
    row_mask = (position[None, :] < filled[:, None]).astype(f32) * is_live[:, None]
    key_valid = jnp.arange(item_rows, dtype=jnp.int32)[None, :] < filled[:, None]
    full_mask = key_valid.astype(f32) * is_live[:, None]
    keep = row_mask[:, :, None]
    keep_all = full_mask[:, :, None]
    counts = filled.astype(f32) * per_group
    channel_start = mp_index * own_channels
    ring = Ring()

    def rows3(values):
        return values.reshape(slot_count, item_rows, values.shape[-1])

    def own_sum(values):
        return sum_rows(values, slot_count)

    def across(*parts):
        return jnp.concatenate(parts, axis=1)

    g_in = Gathered(ring, lambda k: across(*[k[t // 3, t % 3] for t in range(TAPS)]), conv_in)
    g_out = Gathered(ring, lambda k: across(*[k[t // 3, t % 3].T for t in range(TAPS)]), conv_out)
    g_self = Gathered(
        ring,
        lambda q, k, v, c, s, o: across(q, k, v, c, s.T, o.T),
        self_query,
        self_key,
        self_value,
        cross_query,
        self_out,
        cross_out,
    )
    g_text = Gathered(ring, across, cross_key, cross_value)
    g_feed = Gathered(ring, across, ff_value, ff_gate)
    g_down = Gathered(ring, lambda down: down.T, ff_down)
    hidden_own = ff_down.shape[0]

    g_in.begin()
    g_in.step()
    gain_parts = jnp.stack([gn_in_gain, gn_mid_gain, self_gain, cross_gain, ff_gain]).astype(f32)
    small = jnp.concatenate([gain_parts.reshape(-1), timestep.astype(f32)])
    small_all = share_small(small, "dp")
    gains = small_all[:, : 5 * share].reshape(dp_size, 5, share)
    gains = jnp.swapaxes(gains, 0, 1).reshape(5, channels)
    gain_in_f, gain_self_f, gain_cross_f, gain_feed_f = gains[0], gains[2], gains[3], gains[4]
    gain_mid_own = lax.dynamic_slice_in_dim(gains[1], channel_start, own_channels)
    steps_all = small_all[:, 5 * share :].reshape(-1)
    latent, gain_in_f, shift_widths = ring.hold(latent, gain_in_f, widths)
    g_in.step()

    masked = latent.astype(f32) * keep
    all_positions = jnp.arange(item_rows, dtype=jnp.int32).reshape(mp_size, 1, local_rows)
    held = (all_positions < filled[None, :, None]).astype(f32).sum(-1) * is_live * per_group
    held_here = jnp.sum(row_mask, axis=1) * per_group
    local_sum = group_sum(masked, per_group)
    local_mean = local_sum / jnp.maximum(held_here, 1.0)[:, None]
    local_center = (masked - spread(local_mean, per_group)) * keep
    local_spread = group_sum(local_center * local_center, per_group)
    stats = share_small(jnp.stack([local_sum, local_spread]), "mp").reshape(
        mp_size, 2, slot_count, GN_GROUPS
    )
    stats, steps_all, cotangent, shift_widths = ring.hold(
        stats, steps_all, cotangent, shift_widths
    )
    g_in.step()
    average = jnp.sum(stats[:, 0], axis=0) / counts[:, None]
    means = stats[:, 0] / jnp.maximum(held, 1.0)[:, :, None]
    variance = (
        jnp.sum(stats[:, 1] + held[:, :, None] * (means - average) ** 2, axis=0) / counts[:, None]
    )
    scaling_in = spread(lax.rsqrt(variance + 1e-06), per_group)
    standard_in = (masked - spread(average, per_group)) * scaling_in
    first_act = (jax.nn.silu(standard_in * gain_in_f) * keep).astype(bf16)
    first_all = flat(gather_rows(first_act))
    first_all, steps_all, cotangent, shift_widths = ring.hold(
        first_all, steps_all, cotangent, shift_widths
    )
    tall, wide = tap_matrices(shift_widths, item_rows)
    g_out.begin()
    g_in.step()

    half_width = C // 2
    wave = dp_index * share + jnp.arange(share, dtype=jnp.int32)
    frequency = jnp.exp(-math.log(10000.0) * (wave % half_width).astype(f32) / half_width)
    angles = steps_all[:, None] * frequency[None, :]
    time_act = jax.nn.silu(
        jnp.where(wave[None, :] < half_width, jnp.cos(angles), jnp.sin(angles))
    ).astype(bf16)
    time_part = jnp.dot(time_act, time_weight, preferred_element_type=f32)
    time_added = lax.all_to_all(
        time_part.reshape(dp_size, slot_count, own_channels), "dp", 0, 0, tiled=True
    ).sum(0)
    w_in = g_in.whole

    g_out.step()
    first_taps = product(first_all, w_in).astype(bf16)
    first_taps, time_added, cotangent, text_embeds = ring.hold(
        first_taps, time_added, cotangent, text_embeds
    )
    g_out.step()
    middle = (shift_sum(wide, first_taps) + time_added[:, None, :]) * keep_all
    average_mid = group_sum(middle, per_group) / counts[:, None]
    apart_mid = middle - spread(average_mid, per_group)
    center_mid = apart_mid * keep_all
    scaling_mid = spread(
        lax.rsqrt(group_sum(center_mid * center_mid, per_group) / counts[:, None] + 1e-06),
        per_group,
    )
    standard_mid = apart_mid * scaling_mid
    standard_mid, cotangent, text_embeds = ring.hold(standard_mid, cotangent, text_embeds)
    g_out.step()
    second_act = (jax.nn.silu(standard_mid * gain_mid_own) * keep_all).astype(bf16)
    second_taps = shift_stack(tall, flat(second_act))
    second_taps, cotangent, text_embeds = ring.hold(second_taps, cotangent, text_embeds)
    g_self.begin()
    g_out.step()
    out_grad = cotangent.astype(f32) * keep
    feed_branch = flat(gather_rows(out_grad.astype(bf16)))
    w_out = g_out.whole
    g_self.step()
    second_out = product_back(second_taps, w_out)
    second_out, text_embeds = ring.hold(second_out, text_embeds)
    g_self.step()
    resnet = (masked + own_sum(second_out)) * keep

    attend_in, normal_self, scaling_self = norm_rows(resnet, gain_self_f)
    attend_in = ring.hold(attend_in)
    g_self.step()
    attend_all = flat(gather_rows(attend_in))
    attend_all = ring.hold(attend_all)
    g_text.begin()
    g_self.step()
    w_self = g_self.whole
    qkv_full = w_self[:, : 3 * own_channels]
    cq_full = w_self[:, 3 * own_channels : 4 * own_channels]
    so_full = w_self[:, 4 * own_channels : 5 * own_channels]
    co_full = w_self[:, 5 * own_channels :]
    g_text.step()
    qkv = product(attend_all, qkv_full).astype(bf16)
    qkv = rows3(ring.hold(qkv))
    g_text.step()
    query_rows, key_rows, value_rows = jnp.split(qkv, 3, axis=2)
    mixture, self_chances = attend(query_rows, key_rows, value_rows, key_valid)
    self_part = product_back(flat(mixture), so_full)
    self_part = ring.hold(self_part)
    g_text.step()
    g_feed.begin()
    g_text.step()
    w_text = g_text.whole
    after_self = resnet + own_sum(self_part)
    g_feed.step()

    text_rows = flat(text_embeds)
    text_pair = product(text_rows, w_text).astype(bf16).reshape(slot_count, -1, 2 * own_channels)
    text_keys, text_values = jnp.split(text_pair, 2, axis=2)
    cross_in, normal_cross, scaling_cross = norm_rows(after_self, gain_cross_f)
    cross_all = flat(gather_rows(cross_in))
    cross_all = ring.hold(cross_all)
    g_feed.step()
    cross_rows = rows3(product(cross_all, cq_full).astype(bf16))
    cross_mix, cross_chances = attend(cross_rows, text_keys, text_values, None)
    cross_part = product_back(flat(cross_mix), co_full)
    cross_part = ring.hold(cross_part)
    g_feed.step()
    after_cross = after_self + own_sum(cross_part)

    feed_in, normal_feed, scaling_feed = norm_rows(after_cross, gain_feed_f)
    feed_in = ring.hold(feed_in)
    g_down.begin()
    g_feed.step()
    feed_all = flat(gather_rows(feed_in))
    w_feed = g_feed.whole
    g_down.step()
    pair_part = product(feed_all, w_feed)
    pair_part = ring.hold(pair_part)
    g_down.step()
    value_part, gate_part = pair_part[:, :hidden_own], pair_part[:, hidden_own:]
    lower = 0.5 * lax.erfc(-gate_part * math.sqrt(0.5))
    gelu_gate = gate_part * lower
    gelu_slope = lower + gate_part * jnp.exp(-0.5 * gate_part * gate_part) / math.sqrt(2 * math.pi)
    hidden = (value_part * gelu_gate).astype(bf16)
    hidden = ring.hold(hidden)
    g_down.step()
    s_down = Scattered(ring, weight_grad(feed_branch, hidden))
    g_down.step()
    w_down = g_down.whole

    s_down.step()
    hidden_grad = product(feed_branch, w_down)
    pair_grad = jnp.concatenate(
        [
            (hidden_grad * gelu_gate).astype(bf16),
            (hidden_grad * value_part * gelu_slope).astype(bf16),
        ],
        axis=1,
    )
    pair_grad = ring.hold(pair_grad)
    s_down.step()
    feed_part = product_back(pair_grad, w_feed)
    feed_part = ring.hold(feed_part)
    s_down.step()
    s_feed = Scattered(ring, weight_grad(feed_all, pair_grad))
    feed_back = own_sum(feed_part)
    feed_back = ring.hold(feed_back)
    s_down.step()
    feed_dv, grad_gain_feed = norm_rows_back(feed_back, normal_feed, scaling_feed, gain_feed_f)
    cross_grad = out_grad + feed_dv
    cross_branch = flat(gather_rows(cross_grad.astype(bf16)))
    cross_branch = ring.hold(cross_branch)
    s_feed.step()

    cross_mix_grad = rows3(product(cross_branch, co_full).astype(bf16))
    cross_dq, cross_dk, cross_dv = attend_back(
        cross_rows, text_keys, text_values, cross_mix_grad, cross_chances
    )
    cross_dq = flat(cross_dq)
    cross_dq, cross_dk, cross_dv = ring.hold(cross_dq, cross_dk, cross_dv)
    s_feed.step()
    cross_back = own_sum(product_back(cross_dq, cq_full))
    grad_cross_out = weight_grad(cross_branch, flat(cross_mix))
    grad_cross_query = weight_grad(cross_all, cross_dq)
    s_cross = Scattered(
        ring,
        weight_grad(text_rows, flat(jnp.concatenate([cross_dk, cross_dv], axis=2))),
        jnp.concatenate([grad_cross_query, grad_cross_out], axis=1),
    )
    cross_back = ring.hold(cross_back)
    s_feed.step()
    cross_dv_rows, grad_gain_cross = norm_rows_back(
        cross_back, normal_cross, scaling_cross, gain_cross_f
    )
    self_grad = cross_grad + cross_dv_rows

    self_branch = flat(gather_rows(self_grad.astype(bf16)))
    mixture_grad = product(self_branch, so_full).astype(bf16)
    mixture_grad = rows3(ring.hold(mixture_grad))
    s_feed.step()
    qkv_grad = flat(
        jnp.concatenate(
            attend_back(query_rows, key_rows, value_rows, mixture_grad, self_chances), axis=2
        )
    )
    self_back = own_sum(product_back(qkv_grad, qkv_full))
    self_back = ring.hold(self_back)
    s_cross.step()
    self_dv_rows, grad_gain_self = norm_rows_back(self_back, normal_self, scaling_self, gain_self_f)
    resnet_grad = (self_grad + self_dv_rows) * keep
    resnet_grad = ring.hold(resnet_grad)
    s_cross.step()
    resnet_branch = flat(gather_rows(resnet_grad.astype(bf16)))
    resnet_branch = ring.hold(resnet_branch)
    s_cross.step()

    second_parts = product(resnet_branch, w_out).astype(bf16)
    second_parts = ring.hold(second_parts)
    s_cross.step()
    grad_self_out = weight_grad(self_branch, flat(mixture))
    s_self = Scattered(
        ring, jnp.concatenate([weight_grad(attend_all, qkv_grad), grad_self_out], axis=1)
    )
    second_grad = shift_sum_back(tall, second_parts)
    second_grad = ring.hold(second_grad)
    s_self.step()
    s_out = Scattered(ring, weight_grad(resnet_branch, second_taps))
    mid_slope = silu_back(standard_mid * gain_mid_own, second_grad * keep_all)
    mid_gain_part = jnp.sum(mid_slope * standard_mid, axis=(0, 1))
    hat_mid = mid_slope * gain_mid_own
    mid_a = spread(group_sum(hat_mid, per_group) / counts[:, None], per_group)
    mid_b = spread(group_sum(hat_mid * standard_mid, per_group) / counts[:, None], per_group)
    middle_grad = (
        scaling_mid * (hat_mid - (mid_a + standard_mid * mid_b)) * keep_all
    ).astype(bf16)
    middle_grad = ring.hold(middle_grad)
    s_self.step()
    middle_taps = shift_stack_back(wide, flat(middle_grad))
    middle_taps = ring.hold(middle_taps)
    s_self.step()
    first_part = product_back(middle_taps, w_in)
    first_part = ring.hold(first_part)
    s_self.step()
    s_in = Scattered(ring, weight_grad(first_all, middle_taps))
    first_grad = own_sum(first_part)
    first_grad, hidden = ring.hold(first_grad, hidden)
    s_out.step()

    time_sum = jnp.sum(middle_grad.astype(f32), axis=1)
    time_sum_all = share_small(time_sum, "dp").reshape(-1, own_channels)
    grad_time = jnp.einsum(
        "sa,sb->ab",
        time_act.astype(f32),
        time_sum_all,
        precision=highest,
        preferred_element_type=f32,
    )

    in_slope = silu_back(standard_in * gain_in_f, first_grad * keep)
    in_gain_part = jnp.sum(in_slope * standard_in, axis=(0, 1))
    hat_in = in_slope * gain_in_f
    in_a, in_b = lax.psum(
        (group_sum(hat_in, per_group), group_sum(hat_in * standard_in, per_group)), "mp"
    )
    in_a, in_b, grad_time = ring.hold(in_a, in_b, grad_time)
    s_out.step()
    in_a = spread(in_a / counts[:, None], per_group)
    in_b = spread(in_b / counts[:, None], per_group)
    grouped_grad = scaling_in * (hat_in - (in_a + standard_in * in_b))
    latent_grad = ((resnet_grad + grouped_grad) * keep).astype(bf16)
    latent_grad, hidden = ring.hold(latent_grad, hidden)
    s_out.step()
    output = ((after_cross + own_sum(product_back(hidden, w_down))) * keep).astype(bf16)
    output = ring.hold(output)
    s_out.step()
    s_in.step()

    mid_gain_whole = lax.dynamic_update_slice_in_dim(
        jnp.zeros((channels,), f32), mid_gain_part, channel_start, 0
    )
    gain_parts = jnp.stack(
        [in_gain_part, mid_gain_whole, grad_gain_self, grad_gain_cross, grad_gain_feed]
    )
    gain_parts = jnp.swapaxes(gain_parts.reshape(5, dp_size, share), 0, 1)
    gain_parts = jnp.broadcast_to(gain_parts[:, None], (dp_size, mp_size, 5, share))
    gain_sums = lax.all_to_all(
        gain_parts.reshape(dp_size * mp_size, 5, share), ("dp", "mp"), 0, 0, tiled=True
    ).sum(0)
    gain_sums = ring.hold(gain_sums)
    s_in.step()
    s_in.step()
    s_in.step()
    sum_in, sum_out, sum_self = s_in.part, s_out.part, s_self.part
    sum_feed, sum_down = s_feed.part, s_down.part
    text_share = cross_key.shape[0]
    sum_text, sum_cross = s_cross.part[:text_share], s_cross.part[text_share:]

    def tap_part(values, tap):
        return values[:, tap * own_channels : (tap + 1) * own_channels]

    def column_part(values, part):
        return values[:, part * own_channels : (part + 1) * own_channels]

    return (
        output,
        latent_grad,
        jnp.stack([tap_part(sum_in, t) for t in range(TAPS)]).reshape(conv_in.shape),
        jnp.stack([tap_part(sum_out, t).T for t in range(TAPS)]).reshape(conv_out.shape),
        grad_time,
        column_part(sum_self, 0),
        column_part(sum_self, 1),
        column_part(sum_self, 2),
        column_part(sum_self, 3).T,
        column_part(sum_cross, 0),
        column_part(sum_text, 0),
        column_part(sum_text, 1),
        column_part(sum_cross, 1).T,
        sum_feed[:, :hidden_own],
        sum_feed[:, hidden_own:],
        sum_down.T,
        gain_sums[0],
        gain_sums[1],
        gain_sums[2],
        gain_sums[3],
        gain_sums[4],
    )


def solution(mesh):
    in_specs = (
        P("dp", "mp", None),
        P("dp", None, None),
        P("dp", "mp", None),
        P("dp"),
        P("dp"),
        P("dp"),
        P(None, None, "dp", "mp"),
        P(None, None, "mp", "dp"),
        P("dp", "mp"),
        P("dp", "mp"),
        P("dp", "mp"),
        P("dp", "mp"),
        P("mp", "dp"),
        P("dp", "mp"),
        P("dp", "mp"),
        P("dp", "mp"),
        P("mp", "dp"),
        P("dp", "mp"),
        P("dp", "mp"),
        P("mp", "dp"),
        P("dp"),
        P("dp"),
        P("dp"),
        P("dp"),
        P("dp"),
    )
    out_specs = (
        P("dp", "mp", None),
        P("dp", "mp", None),
        P(None, None, "dp", "mp"),
        P(None, None, "mp", "dp"),
        P("dp", "mp"),
        P("dp", "mp"),
        P("dp", "mp"),
        P("dp", "mp"),
        P("mp", "dp"),
        P("dp", "mp"),
        P("dp", "mp"),
        P("dp", "mp"),
        P("mp", "dp"),
        P("dp", "mp"),
        P("dp", "mp"),
        P("mp", "dp"),
        P("dp"),
        P("dp"),
        P("dp"),
        P("dp"),
        P("dp"),
    )
    return jax.shard_map(body, mesh=mesh, in_specs=in_specs, out_specs=out_specs, check_vma=False)
```

time: 1130 us -> 878 us (0.78)
  waiting for transfers between devices: 473 us -> 323 us
  local copies, waits for them, and re-layouts: 219 us -> 152 us
  matrix products: 148 us -> 114 us
  other arithmetic: 85.7 us -> 102 us
  starting transfers between devices: 155 us -> 143 us
    ppermute x112 -> x96, waiting for transfers between devices: 395 us -> 294 us  [the longest x48 244 us: step(): lax.ppermute(to_right, 'dp', self.right)]
    dot_general x30 -> x34, matrix products: 132 us -> 96.3 us  [the longest x13 37.3 us: product(): return jnp.dot(former, latter, preferred_element_type=f32)]
    dynamic_update_slice x63 -> x53, local copies, waits for them, and re-layouts: 76.1 us -> 50 us  [put(): self.whole = lax.dynamic_update_slice(self.whole, part[None], place)]
    ppermute x8, waiting for transfers between devices: 38.3 us -> 15 us  [sum_rows(): got = lax.ppermute(far_part(1 - far_bit).astype(bf16), 'mp', FAR)]
    dot_general x2 -> x0, local copies, waits for them, and re-layouts: 21.8 us -> none  [product_back(): return jnp.einsum('snb,ab->sna', former, latter, preferred_element_type=f32)]
    convert_element_type x2 -> x0, local copies, waits for them, and re-layouts: 21 us -> none  [weight_grad(): jnp.einsum('sna,snb->ab', former, latter, preferred_element_type=f32)]
    ppermute x112 -> x96, starting transfers between devices: 119 us -> 103 us  [the longest x48 52.2 us: step(): lax.ppermute(to_right, 'dp', self.right)]
    ppermute x8, waiting for transfers between devices: 20.8 us -> 7.46 us  [gather_rows(): far = lax.ppermute(values, 'mp', FAR)]
  transfers between devices with their start and end apart: 157 -> 141, of which waited for: 79 -> 74; matrix products, arithmetic and copies ran while one was open for 35% -> 37% of each run, Pallas kernels for 0% -> 0%
where the time goes in v2:
time: 878 us; the launch traced here: 867 us
  waiting for transfers between devices  323 us (37%)
  local copies, waits for them, and re-layouts  152 us (17%)
  starting transfers between devices  143 us (16%)
  matrix products  114 us (13%)
  other arithmetic  102 us (12%)
  between operations  27.6 us (3%)
    ppermute x48, waiting for transfers between devices, step(): lax.ppermute(to_right, 'dp', self.right)  244 us
    ppermute x48, starting transfers between devices, step(): lax.ppermute(to_right, 'dp', self.right)  52.2 us
    ppermute x48, starting transfers between devices, step(): lax.ppermute(to_left, 'dp', self.left)  51.2 us
    dynamic_update_slice x53, local copies, waits for them, and re-layouts, put(): self.whole = lax.dynamic_update_slice(self.whole, part[None], place)  50 us
    ppermute x48, waiting for transfers between devices, step(): lax.ppermute(to_left, 'dp', self.left)  49.9 us
    dot_general x13, matrix products, product(): return jnp.dot(former, latter, preferred_element_type=f32)  37.3 us
    dot_general x8, matrix products, product_back(): lax.dot_general(former, latter, (((1,), (1,)), ((), ())), preferred_eleme...  29.6 us
    dot_general x13, matrix products, product_down(): lax.dot_general(former, latter, (((0,), (0,)), ((), ())), preferred_eleme...  29.5 us
  transfers between devices with their start and end apart: 141, of which 74 were waited for; matrix products, arithmetic and copies ran while one was open for 37% of the time, Pallas kernels for 0%

profile of v2, /device:TPU:0, one launch (start us, length us, event | category | flops | bytes accessed | tf_op | source)
XLA Modules:
  0.0 867.1 jit_solution(9390063107338121400)
XLA Ops:
  2.9 3.1 collective-permute-start
  6.9 6.2 all-to-all-start
  24.9 3.6 broadcast_in_dim.355
  46.5 3.2 all-to-all-start.1
  55.4 18.0 %collective-permute-done.2 = bf16[160,2880]{1,0:T(8,128)(2,1)} collective-permute-done((bf16[160,2880]{1,0:T(8,128)(2,1)S(1)}, bf16[160,2880]{1,0:T(8,128)(2,1)}, u32[]{:S(2)}, u32[]{:S(2)}) %collective-permute-start.2) | collective-permute-done | bytes 921632 | tf_op jit(solution)/shard_map/ppermute | solution.py:136
  87.9 13.2 %collective-permute-done.7 = bf16[160,2880]{1,0:T(8,128)(2,1)S(1)} collective-permute-done((bf16[160,2880]{1,0:T(8,128)(2,1)}, bf16[160,2880]{1,0:T(8,128)(2,1)S(1)}, u32[]{:S(2)}, u32[]{:S(2)}) %collective-permute-start.7) | collective-permute-done | bytes 921632 | tf_op jit(solution)/shard_map/ppermute | solution.py:136
  110.2 4.0 all-to-all-start.2
  131.2 7.6 convolution_convert_fusion.5
  138.8 8.1 collective-permute-done.11
  158.0 14.8 %collective-permute-done.13 = bf16[160,2880]{1,0:T(8,128)(2,1)} collective-permute-done((bf16[160,2880]{1,0:T(8,128)(2,1)}, bf16[160,2880]{1,0:T(8,128)(2,1)}, u32[]{:S(2)}, u32[]{:S(2)}) %collective-permute-start.13) | collective-permute-done | bytes 921632 | tf_op jit(solution)/shard_map/ppermute | solution.py:136
  191.8 6.0 collective-permute-done.15
  216.6 6.7 fusion.242
  229.7 11.3 %collective-permute-done.23 = bf16[160,1920]{1,0:T(8,128)(2,1)} collective-permute-done((bf16[160,1920]{1,0:T(8,128)(2,1)S(1)}, bf16[160,1920]{1,0:T(8,128)(2,1)}, u32[]{:S(2)}, u32[]{:S(2)}) %collective-permute-start.23) | collective-permute-done | bytes 614432 | tf_op jit(solution)/shard_map/ppermute | solution.py:136
  249.1 6.4 collective-permute-done.22
  267.4 3.8 collective-permute-done.52
  278.2 3.7 fusion.40
  299.7 7.9 collective-permute-done.38
  319.0 4.7 collective-permute-done.37
  325.7 9.9 %collective-permute-done.45 = bf16[160,2560]{1,0:T(8,128)(2,1)} collective-permute-done((bf16[160,2560]{1,0:T(8,128)(2,1)}, bf16[160,2560]{1,0:T(8,128)(2,1)}, u32[]{:S(2)}, u32[]{:S(2)}) %collective-permute-start.45) | collective-permute-done | bytes 819232 | tf_op jit(solution)/shard_map/ppermute | solution.py:136
  361.2 13.8 %collective-permute-done.54 = bf16[160,2560]{1,0:T(8,128)(2,1)S(1)} collective-permute-done((bf16[160,2560]{1,0:T(8,128)(2,1)}, bf16[160,2560]{1,0:T(8,128)(2,1)S(1)}, u32[]{:S(2)}, u32[]{:S(2)}) %collective-permute-start.54) | collective-permute-done | bytes 819232 | tf_op jit(solution)/shard_map/ppermute | solution.py:136
  381.7 4.4 collective-permute-done.56
  388.8 7.4 collective-permute-done.57
  398.8 3.5 fusion.243
  402.4 5.7 multiply_convert_fusion.1
  412.3 5.5 collective-permute-done.62
  420.0 5.7 collective-permute-done.64
  432.2 3.6 fusion.244
  438.1 3.8 convolution_convert_fusion.2
  441.9 6.1 collective-permute-done.71
  452.2 6.0 collective-permute-done.75
  462.6 7.0 collective-permute-done.80
  490.7 3.0 convolution_convert_fusion.15
  500.8 3.2 convolution_convert_fusion.11
  521.2 3.4 fusion.38
  533.0 12.2 %collective-permute-done.91 = bf16[160,2560]{1,0:T(8,128)(2,1)} collective-permute-done((bf16[160,2560]{1,0:T(8,128)(2,1)}, bf16[160,2560]{1,0:T(8,128)(2,1)}, u32[]{:S(2)}, u32[]{:S(2)}) %collective-permute-start.91) | collective-permute-done | bytes 819232 | tf_op jit(solution)/shard_map/ppermute | solution.py:136
  546.9 3.4 fusion.36
  556.5 3.2 fusion.55
  576.1 3.7 fusion.13
  601.2 8.2 collective-permute-done.102
  616.0 9.4 %convolution_convert_fusion.4 = bf16[512,2880]{0,1:T(8,128)(2,1)S(1)} fusion(bf16[512,1280]{1,0:T(8,128)(2,1)S(1)} %bitcast.873, bf16[1280,2880]{1,0:T(8,128)(2,1)} %bitcast.830), kind=kOutput, calls=%fused_computation.11 | convolution fusion | flops 3776348160 | bytes 11632640 | tf_op jit(solution)/shard_map/dot_general | solution.py:206
  625.4 4.5 convolution_convert_fusion.1
  636.4 9.4 %collective-permute-done.106 = bf16[416,640]{1,0:T(8,128)(2,1)S(1)} collective-permute-done((bf16[416,640]{1,0:T(8,128)(2,1)S(1)}, bf16[416,640]{1,0:T(8,128)(2,1)S(1)}, u32[]{:S(2)}, u32[]{:S(2)}) %collective-permute-start.106) | collective-permute-done | bytes 532512 | tf_op jit(solution)/shard_map/ppermute | solution.py:136
  650.9 3.8 collective-permute-done.108
  674.2 4.3 collective-permute-done.112
  685.3 3.3 all-to-all-start.3
  698.5 4.5 collective-permute-done.118
  707.7 3.7 concatenate.257
  713.9 3.6 concatenate.256
  717.5 3.7 pad_maximum_fusion.2
  728.8 6.7 fusion.245
  735.7 7.0 collective-permute-done.124
  749.3 4.5 convolution_convert_fusion
  754.0 13.6 %collective-permute-done.126 = bf16[160,2880]{1,0:T(8,128)(2,1)S(1)} collective-permute-done((bf16[160,2880]{1,0:T(8,128)(2,1)S(1)}, bf16[160,2880]{1,0:T(8,128)(2,1)S(1)}, u32[]{:S(2)}, u32[]{:S(2)}) %collective-permute-start.126) | collective-permute-done | bytes 921632 | tf_op jit(solution)/shard_map/ppermute | solution.py:136
  770.5 8.6 collective-permute-done.127
  782.8 6.2 all-reduce
  792.2 5.1 collective-permute-done.128
  802.1 10.7 %collective-permute-done.133 = bf16[160,2880]{1,0:T(8,128)(2,1)S(1)} collective-permute-done((bf16[160,2880]{1,0:T(8,128)(2,1)S(1)}, bf16[160,2880]{1,0:T(8,128)(2,1)S(1)}, u32[]{:S(2)}, u32[]{:S(2)}) %collective-permute-start.133) | collective-permute-done | bytes 921632 | tf_op jit(solution)/shard_map/ppermute | solution.py:137
  812.8 3.8 collective-permute-done.129
  816.7 3.3 fusion.31
  823.6 3.0 all-to-all-start.4
  831.7 7.0 collective-permute-done.134
  848.1 5.4 collective-permute-done.130
  853.4 6.8 collective-permute-done.135
  860.3 3.2 fusion.25
  (1049 shorter events, 439.5 us)
Async XLA Ops:
  2.9 41.8 %collective-permute-start = (bf16[160,2880]{1,0:T(8,128)(2,1)S(1)}, bf16[160,2880]{1,0:T(8,128)(2,1)S(1)}, u32[]{:S(2)}, u32[]{:S(2)}) collective-permute-start(bf16[160,2880]{1,0:T(8,128)(2,1)S(1)} %concatenate.201), channel_id=1, source_target_pairs={{0,8},{8,16},{16,24},{24,28},{28,20},{20,12},{12,4},{4,0},{1,9},{9... | collective-permute-start | bytes 2764808 | tf_op jit(solution)/shard_map/ppermute | solution.py:136
  5.9 38.8 %collective-permute-start.1 = (bf16[160,2880]{1,0:T(8,128)(2,1)S(1)}, bf16[160,2880]{1,0:T(8,128)(2,1)S(1)}, u32[]{:S(2)}, u32[]{:S(2)}) collective-permute-start(bf16[160,2880]{1,0:T(8,128)(2,1)S(1)} %concatenate.201), channel_id=1, source_target_pairs={{8,0},{16,8},{24,16},{28,24},{20,28},{12,20},{4,12},{0,4},{9,1},{1... | collective-permute-start | bytes 2764808 | tf_op jit(solution)/shard_map/ppermute | solution.py:137
  6.9 36.4 %all-to-all-start = ((f32[8,1,802]{2,1,0:T(1,128)}), f32[8,1,802]{2,1,0:T(1,128)S(1)}, u32[]{:S(2)}, u32[]{:S(2)}) async-start(f32[8,1,802]{2,1,0:T(1,128)} %broadcast_in_dim.343), calls=%async_computation | async-start | bytes 57344 | tf_op jit(solution)/shard_map/all_to_all | solution.py:151
  49.7 23.7 %collective-permute-start.2 = (bf16[160,2880]{1,0:T(8,128)(2,1)S(1)}, bf16[160,2880]{1,0:T(8,128)(2,1)}, u32[]{:S(2)}, u32[]{:S(2)}) collective-permute-start(bf16[160,2880]{1,0:T(8,128)(2,1)S(1)} %collective-permute-done), channel_id=1, source_target_pairs={{0,8},{8,16},{16,24},{24,28},{28,20},{20,12},{12,4},{4,0},{1,9},{9... | collective-permute-start | bytes 2764808 | tf_op jit(solution)/shard_map/ppermute | solution.py:136
  51.8 23.0 %collective-permute-start.3 = (bf16[160,2880]{1,0:T(8,128)(2,1)S(1)}, bf16[160,2880]{1,0:T(8,128)(2,1)}, u32[]{:S(2)}, u32[]{:S(2)}) collective-permute-start(bf16[160,2880]{1,0:T(8,128)(2,1)S(1)} %collective-permute-done.1), channel_id=1, source_target_pairs={{8,0},{16,8},{24,16},{28,24},{20,28},{12,20},{4,12},{0,4},{9,1},{1... | collective-permute-start | bytes 2764808 | tf_op jit(solution)/shard_map/ppermute | solution.py:137
  77.5 23.5 %collective-permute-start.7 = (bf16[160,2880]{1,0:T(8,128)(2,1)}, bf16[160,2880]{1,0:T(8,128)(2,1)S(1)}, u32[]{:S(2)}, u32[]{:S(2)}) collective-permute-start(bf16[160,2880]{1,0:T(8,128)(2,1)} %collective-permute-done.2), channel_id=1, source_target_pairs={{0,8},{8,16},{16,24},{24,28},{28,20},{20,12},{12,4},{4,0},{1,9},{9... | collective-permute-start | bytes 2764808 | tf_op jit(solution)/shard_map/ppermute | solution.py:136
  79.0 23.2 %collective-permute-start.8 = (bf16[160,2880]{1,0:T(8,128)(2,1)}, bf16[160,2880]{1,0:T(8,128)(2,1)S(1)}, u32[]{:S(2)}, u32[]{:S(2)}) collective-permute-start(bf16[160,2880]{1,0:T(8,128)(2,1)} %collective-permute-done.3), channel_id=1, source_target_pairs={{8,0},{16,8},{24,16},{28,24},{20,28},{12,20},{4,12},{0,4},{9,1},{1... | collective-permute-start | bytes 2764808 | tf_op jit(solution)/shard_map/ppermute | solution.py:137
  106.4 18.6 %collective-permute-start.9 = (bf16[80,2880]{1,0:T(8,128)(2,1)}, bf16[80,2880]{1,0:T(8,128)(2,1)}, u32[]{:S(2)}, u32[]{:S(2)}) collective-permute-start(bf16[80,2880]{1,0:T(8,128)(2,1)} %slice.931), channel_id=1, source_target_pairs={{0,8},{8,16},{16,24},{24,28},{28,20},{20,12},{12,4},{4,0},{1,9},{9... | collective-permute-start | bytes 1382408 | tf_op jit(solution)/shard_map/ppermute | solution.py:136
  108.7 18.3 %collective-permute-start.10 = (bf16[80,2880]{1,0:T(8,128)(2,1)}, bf16[80,2880]{1,0:T(8,128)(2,1)}, u32[]{:S(2)}, u32[]{:S(2)}) collective-permute-start(bf16[80,2880]{1,0:T(8,128)(2,1)} %slice.932), channel_id=1, source_target_pairs={{8,0},{16,8},{24,16},{28,24},{20,28},{12,20},{4,12},{0,4},{9,1},{1... | collective-permute-start | bytes 1382408 | tf_op jit(solution)/shard_map/ppermute | solution.py:137
  110.2 14.1 %all-to-all-start.2 = ((f32[8,2,320]{2,1,0:T(2,128)}), f32[8,2,320]{2,1,0:T(2,128)}, u32[]{:S(2)}, u32[]{:S(2)}) async-start(f32[8,2,320]{2,1,0:T(2,128)} %reshape.806), calls=%async_computation.2 | async-start | bytes 49152 | tf_op jit(solution)/shard_map/all_to_all | solution.py:506
  125.0 21.9 %collective-permute-start.11 = (bf16[160,2880]{1,0:T(8,128)(2,1)}, bf16[160,2880]{1,0:T(8,128)(2,1)S(1)}, u32[]{:S(2)}, u32[]{:S(2)}) collective-permute-start(bf16[160,2880]{1,0:T(8,128)(2,1)} %copy-done.26), channel_id=1, source_target_pairs={{0,8},{8,16},{16,24},{24,28},{28,20},{20,12},{12,4},{4,0},{1,9},{9... | collective-permute-start | bytes 2764808 | tf_op jit(solution)/shard_map/ppermute | solution.py:136
  127.0 21.7 %collective-permute-start.12 = (bf16[160,2880]{1,0:T(8,128)(2,1)}, bf16[160,2880]{1,0:T(8,128)(2,1)S(1)}, u32[]{:S(2)}, u32[]{:S(2)}) collective-permute-start(bf16[160,2880]{1,0:T(8,128)(2,1)} %copy-done.26), channel_id=1, source_target_pairs={{8,0},{16,8},{24,16},{28,24},{20,28},{12,20},{4,12},{0,4},{9,1},{1... | collective-permute-start | bytes 2764808 | tf_op jit(solution)/shard_map/ppermute | solution.py:137
  152.4 20.5 %collective-permute-start.13 = (bf16[160,2880]{1,0:T(8,128)(2,1)}, bf16[160,2880]{1,0:T(8,128)(2,1)}, u32[]{:S(2)}, u32[]{:S(2)}) collective-permute-start(bf16[160,2880]{1,0:T(8,128)(2,1)} %copy-done.75), channel_id=1, source_target_pairs={{0,8},{8,16},{16,24},{24,28},{28,20},{20,12},{12,4},{4,0},{1,9},{9... | collective-permute-start | bytes 2764808 | tf_op jit(solution)/shard_map/ppermute | solution.py:136
  153.9 20.2 %collective-permute-start.14 = (bf16[160,2880]{1,0:T(8,128)(2,1)}, bf16[160,2880]{1,0:T(8,128)(2,1)}, u32[]{:S(2)}, u32[]{:S(2)}) collective-permute-start(bf16[160,2880]{1,0:T(8,128)(2,1)} %copy-done.76), channel_id=1, source_target_pairs={{8,0},{16,8},{24,16},{28,24},{20,28},{12,20},{4,12},{0,4},{9,1},{1... | collective-permute-start | bytes 2764808 | tf_op jit(solution)/shard_map/ppermute | solution.py:137
  178.5 19.3 %collective-permute-start.15 = (bf16[160,2880]{1,0:T(8,128)(2,1)}, bf16[160,2880]{1,0:T(8,128)(2,1)}, u32[]{:S(2)}, u32[]{:S(2)}) collective-permute-start(bf16[160,2880]{1,0:T(8,128)(2,1)} %collective-permute-done.13), channel_id=1, source_target_pairs={{0,8},{8,16},{16,24},{24,28},{28,20},{20,12},{12,4},{4,0},{1,9},{9... | collective-permute-start | bytes 2764808 | tf_op jit(solution)/shard_map/ppermute | solution.py:136
  180.0 19.0 %collective-permute-start.16 = (bf16[160,2880]{1,0:T(8,128)(2,1)}, bf16[160,2880]{1,0:T(8,128)(2,1)}, u32[]{:S(2)}, u32[]{:S(2)}) collective-permute-start(bf16[160,2880]{1,0:T(8,128)(2,1)} %collective-permute-done.14), channel_id=1, source_target_pairs={{8,0},{16,8},{24,16},{28,24},{20,28},{12,20},{4,12},{0,4},{9,1},{1... | collective-permute-start | bytes 2764808 | tf_op jit(solution)/shard_map/ppermute | solution.py:137
  224.6 20.4 %collective-permute-start.21 = (bf16[2,2,64,1280]{3,2,0,1:T(8,128)(2,1)S(1)}, bf16[2,2,64,1280]{3,2,0,1:T(8,128)(2,1)}, u32[]{:S(2)}, u32[]{:S(2)}) collective-permute-start(bf16[2,2,64,1280]{3,2,0,1:T(8,128)(2,1)S(1)} %fusion.95), channel_id=1, source_target_pairs={{0,1},{1,0},{2,3},{3,2},{4,5},{5,4},{6,7},{7,6},{8,9},{9,8},{10,11... | collective-permute-start | bytes 1966088 | tf_op jit(solution)/shard_map/ppermute | solution.py:187
  224.7 16.4 %collective-permute-start.23 = (bf16[160,1920]{1,0:T(8,128)(2,1)S(1)}, bf16[160,1920]{1,0:T(8,128)(2,1)}, u32[]{:S(2)}, u32[]{:S(2)}) collective-permute-start(bf16[160,1920]{1,0:T(8,128)(2,1)S(1)} %collective-permute-done.19), channel_id=1, source_target_pairs={{0,8},{8,16},{16,24},{24,28},{28,20},{20,12},{12,4},{4,0},{1,9},{9... | collective-permute-start | bytes 1843208 | tf_op jit(solution)/shard_map/ppermute | solution.py:136
  225.8 16.3 %collective-permute-start.24 = (bf16[160,1920]{1,0:T(8,128)(2,1)S(1)}, bf16[160,1920]{1,0:T(8,128)(2,1)}, u32[]{:S(2)}, u32[]{:S(2)}) collective-permute-start(bf16[160,1920]{1,0:T(8,128)(2,1)S(1)} %collective-permute-done.20), channel_id=1, source_target_pairs={{8,0},{16,8},{24,16},{28,24},{20,28},{12,20},{4,12},{0,4},{9,1},{1... | collective-permute-start | bytes 1843208 | tf_op jit(solution)/shard_map/ppermute | solution.py:137
  241.0 17.3 %collective-permute-start.28 = (bf16[160,1920]{1,0:T(8,128)(2,1)}, bf16[160,1920]{1,0:T(8,128)(2,1)S(1)}, u32[]{:S(2)}, u32[]{:S(2)}) collective-permute-start(bf16[160,1920]{1,0:T(8,128)(2,1)} %collective-permute-done.23), channel_id=1, source_target_pairs={{0,8},{8,16},{16,24},{24,28},{28,20},{20,12},{12,4},{4,0},{1,9},{9... | collective-permute-start | bytes 1843208 | tf_op jit(solution)/shard_map/ppermute | solution.py:136
  242.1 17.2 %collective-permute-start.29 = (bf16[160,1920]{1,0:T(8,128)(2,1)}, bf16[160,1920]{1,0:T(8,128)(2,1)S(1)}, u32[]{:S(2)}, u32[]{:S(2)}) collective-permute-start(bf16[160,1920]{1,0:T(8,128)(2,1)} %collective-permute-done.24), channel_id=1, source_target_pairs={{8,0},{16,8},{24,16},{28,24},{20,28},{12,20},{4,12},{0,4},{9,1},{1... | collective-permute-start | bytes 1843208 | tf_op jit(solution)/shard_map/ppermute | solution.py:137
  256.7 14.5 %collective-permute-start.52 = (bf16[2,64,1280]{2,1,0:T(8,128)(2,1)S(1)}, bf16[2,64,1280]{2,1,0:T(8,128)(2,1)}, u32[]{:S(2)}, u32[]{:S(2)}) collective-permute-start(bf16[2,64,1280]{2,1,0:T(8,128)(2,1)S(1)} %get-tuple-element.736), channel_id=1, source_target_pairs={{0,2},{2,0},{1,3},{3,1},{4,6},{6,4},{5,7},{7,5},{8,10},{10,8},{9,1... | collective-permute-start | bytes 983048 | tf_op jit(solution)/shard_map/ppermute | solution.py:167
  258.3 13.9 %collective-permute-start.51 = (bf16[2,64,1280]{2,1,0:T(8,128)(2,1)S(1)}, bf16[2,64,1280]{2,1,0:T(8,128)(2,1)}, u32[]{:S(2)}, u32[]{:S(2)}) collective-permute-start(bf16[2,64,1280]{2,1,0:T(8,128)(2,1)S(1)} %get-tuple-element.736), channel_id=1, source_target_pairs={{0,1},{1,0},{2,3},{3,2},{4,5},{5,4},{6,7},{7,6},{8,9},{9,8},{10,11... | collective-permute-start | bytes 983048 | tf_op jit(solution)/shard_map/ppermute | solution.py:168
  259.3 14.0 %collective-permute-start.30 = (bf16[80,1920]{1,0:T(8,128)(2,1)}, bf16[80,1920]{1,0:T(8,128)(2,1)}, u32[]{:S(2)}, u32[]{:S(2)}) collective-permute-start(bf16[80,1920]{1,0:T(8,128)(2,1)} %slice.957), channel_id=1, source_target_pairs={{0,8},{8,16},{16,24},{24,28},{28,20},{20,12},{12,4},{4,0},{1,9},{9... | collective-permute-start | bytes 921608 | tf_op jit(solution)/shard_map/ppermute | solution.py:136
  297.1 17.3 %collective-permute-start.36 = (bf16[2,2,64,1280]{3,2,0,1:T(8,128)(2,1)S(1)}, bf16[2,2,64,1280]{3,2,0,1:T(8,128)(2,1)S(1)}, u32[]{:S(2)}, u32[]{:S(2)}) collective-permute-start(bf16[2,2,64,1280]{3,2,0,1:T(8,128)(2,1)S(1)} %fusion.96), channel_id=1, source_target_pairs={{0,1},{1,0},{2,3},{3,2},{4,5},{5,4},{6,7},{7,6},{8,9},{9,8},{10,11... | collective-permute-start | bytes 1966088 | tf_op jit(solution)/shard_map/ppermute | solution.py:187
  316.9 18.7 %collective-permute-start.45 = (bf16[160,2560]{1,0:T(8,128)(2,1)}, bf16[160,2560]{1,0:T(8,128)(2,1)}, u32[]{:S(2)}, u32[]{:S(2)}) collective-permute-start(bf16[160,2560]{1,0:T(8,128)(2,1)} %copy-done.44), channel_id=1, source_target_pairs={{0,8},{8,16},{16,24},{24,28},{28,20},{20,12},{12,4},{4,0},{1,9},{9... | collective-permute-start | bytes 2457608 | tf_op jit(solution)/shard_map/ppermute | solution.py:136
  317.6 18.8 %collective-permute-start.46 = (bf16[160,2560]{1,0:T(8,128)(2,1)}, bf16[160,2560]{1,0:T(8,128)(2,1)}, u32[]{:S(2)}, u32[]{:S(2)}) collective-permute-start(bf16[160,2560]{1,0:T(8,128)(2,1)} %copy-done.44), channel_id=1, source_target_pairs={{8,0},{16,8},{24,16},{28,24},{20,28},{12,20},{4,12},{0,4},{9,1},{1... | collective-permute-start | bytes 2457608 | tf_op jit(solution)/shard_map/ppermute | solution.py:137
  325.3 16.6 %collective-permute-start.43 = (bf16[2,64,1280]{2,1,0:T(8,128)(2,1)S(1)}, bf16[2,64,1280]{2,1,0:T(8,128)(2,1)S(1)}, u32[]{:S(2)}, u32[]{:S(2)}) collective-permute-start(bf16[2,64,1280]{2,1,0:T(8,128)(2,1)S(1)} %multiply_convert_fusion.7), channel_id=1, source_target_pairs={{0,2},{2,0},{1,3},{3,1},{4,6},{6,4},{5,7},{7,5},{8,10},{10,8},{9,1... | collective-permute-start | bytes 983048 | tf_op jit(solution)/shard_map/ppermute | solution.py:167
  325.7 16.1 %collective-permute-start.42 = (bf16[2,64,1280]{2,1,0:T(8,128)(2,1)S(1)}, bf16[2,64,1280]{2,1,0:T(8,128)(2,1)S(1)}, u32[]{:S(2)}, u32[]{:S(2)}) collective-permute-start(bf16[2,64,1280]{2,1,0:T(8,128)(2,1)S(1)} %multiply_convert_fusion.7), channel_id=1, source_target_pairs={{0,1},{1,0},{2,3},{3,2},{4,5},{5,4},{6,7},{7,6},{8,9},{9,8},{10,11... | collective-permute-start | bytes 983048 | tf_op jit(solution)/shard_map/ppermute | solution.py:168
  335.6 17.7 %collective-permute-start.47 = (bf16[160,2560]{1,0:T(8,128)(2,1)}, bf16[160,2560]{1,0:T(8,128)(2,1)}, u32[]{:S(2)}, u32[]{:S(2)}) collective-permute-start(bf16[160,2560]{1,0:T(8,128)(2,1)} %collective-permute-done.45), channel_id=1, source_target_pairs={{0,8},{8,16},{16,24},{24,28},{28,20},{20,12},{12,4},{4,0},{1,9},{9... | collective-permute-start | bytes 2457608 | tf_op jit(solution)/shard_map/ppermute | solution.py:136
  336.4 17.5 %collective-permute-start.48 = (bf16[160,2560]{1,0:T(8,128)(2,1)}, bf16[160,2560]{1,0:T(8,128)(2,1)S(1)}, u32[]{:S(2)}, u32[]{:S(2)}) collective-permute-start(bf16[160,2560]{1,0:T(8,128)(2,1)} %collective-permute-done.46), channel_id=1, source_target_pairs={{8,0},{16,8},{24,16},{28,24},{20,28},{12,20},{4,12},{0,4},{9,1},{1... | collective-permute-start | bytes 2457608 | tf_op jit(solution)/shard_map/ppermute | solution.py:137
  354.1 20.9 %collective-permute-start.54 = (bf16[160,2560]{1,0:T(8,128)(2,1)}, bf16[160,2560]{1,0:T(8,128)(2,1)S(1)}, u32[]{:S(2)}, u32[]{:S(2)}) collective-permute-start(bf16[160,2560]{1,0:T(8,128)(2,1)} %collective-permute-done.47), channel_id=1, source_target_pairs={{0,8},{8,16},{16,24},{24,28},{28,20},{20,12},{12,4},{4,0},{1,9},{9... | collective-permute-start | bytes 2457608 | tf_op jit(solution)/shard_map/ppermute | solution.py:136
  354.8 20.9 %collective-permute-start.55 = (bf16[160,2560]{1,0:T(8,128)(2,1)S(1)}, bf16[160,2560]{1,0:T(8,128)(2,1)S(1)}, u32[]{:S(2)}, u32[]{:S(2)}) collective-permute-start(bf16[160,2560]{1,0:T(8,128)(2,1)S(1)} %collective-permute-done.48), channel_id=1, source_target_pairs={{8,0},{16,8},{24,16},{28,24},{20,28},{12,20},{4,12},{0,4},{9,1},{1... | collective-permute-start | bytes 2457608 | tf_op jit(solution)/shard_map/ppermute | solution.py:137
  359.4 19.9 %collective-permute-start.50 = (bf16[2,64,1280]{2,1,0:T(8,128)(2,1)S(1)}, bf16[2,64,1280]{2,1,0:T(8,128)(2,1)S(1)}, u32[]{:S(2)}, u32[]{:S(2)}) collective-permute-start(bf16[2,64,1280]{2,1,0:T(8,128)(2,1)S(1)} %fusion.124), channel_id=1, source_target_pairs={{0,2},{2,0},{1,3},{3,1},{4,6},{6,4},{5,7},{7,5},{8,10},{10,8},{9,1... | collective-permute-start | bytes 983048 | tf_op jit(solution)/shard_map/ppermute | solution.py:193
  483.1 38.1 %collective-permute-start.86 = (bf16[160,2560]{1,0:T(8,128)(2,1)}, bf16[160,2560]{1,0:T(8,128)(2,1)}, u32[]{:S(2)}, u32[]{:S(2)}) collective-permute-start(bf16[160,2560]{1,0:T(8,128)(2,1)} %pad_maximum_fusion.17), channel_id=1, source_target_pairs={{0,8},{8,16},{16,24},{24,28},{28,20},{20,12},{12,4},{4,0},{1,9},{9... | collective-permute-start | bytes 2457608 | tf_op jit(solution)/shard_map/ppermute | solution.py:136
  486.0 35.2 %collective-permute-start.87 = (bf16[160,2560]{1,0:T(8,128)(2,1)}, bf16[160,2560]{1,0:T(8,128)(2,1)}, u32[]{:S(2)}, u32[]{:S(2)}) collective-permute-start(bf16[160,2560]{1,0:T(8,128)(2,1)} %pad_maximum_fusion.18), channel_id=1, source_target_pairs={{8,0},{16,8},{24,16},{28,24},{20,28},{12,20},{4,12},{0,4},{9,1},{1... | collective-permute-start | bytes 2457608 | tf_op jit(solution)/shard_map/ppermute | solution.py:137
  524.6 20.6 %collective-permute-start.91 = (bf16[160,2560]{1,0:T(8,128)(2,1)}, bf16[160,2560]{1,0:T(8,128)(2,1)}, u32[]{:S(2)}, u32[]{:S(2)}) collective-permute-start(bf16[160,2560]{1,0:T(8,128)(2,1)} %get-tuple-element.303), channel_id=1, source_target_pairs={{0,8},{8,16},{16,24},{24,28},{28,20},{20,12},{12,4},{4,0},{1,9},{9... | collective-permute-start | bytes 2457608 | tf_op jit(solution)/shard_map/ppermute | solution.py:136
  526.6 20.3 %collective-permute-start.92 = (bf16[160,2560]{1,0:T(8,128)(2,1)}, bf16[160,2560]{1,0:T(8,128)(2,1)}, u32[]{:S(2)}, u32[]{:S(2)}) collective-permute-start(bf16[160,2560]{1,0:T(8,128)(2,1)} %get-tuple-element.304), channel_id=1, source_target_pairs={{8,0},{16,8},{24,16},{28,24},{20,28},{12,20},{4,12},{0,4},{9,1},{1... | collective-permute-start | bytes 2457608 | tf_op jit(solution)/shard_map/ppermute | solution.py:137
  531.3 21.2 %collective-permute-start.89 = (bf16[2,64,1280]{2,1,0:T(8,128)(2,1)S(1)}, bf16[2,64,1280]{2,1,0:T(8,128)(2,1)S(1)}, u32[]{:S(2)}, u32[]{:S(2)}) collective-permute-start(bf16[2,64,1280]{2,1,0:T(8,128)(2,1)S(1)} %get-tuple-element.488), channel_id=1, source_target_pairs={{0,2},{2,0},{1,3},{3,1},{4,6},{6,4},{5,7},{7,5},{8,10},{10,8},{9,1... | collective-permute-start | bytes 983048 | tf_op jit(solution)/shard_map/ppermute | solution.py:167
  532.9 19.5 %collective-permute-start.88 = (bf16[2,64,1280]{2,1,0:T(8,128)(2,1)S(1)}, bf16[2,64,1280]{2,1,0:T(8,128)(2,1)S(1)}, u32[]{:S(2)}, u32[]{:S(2)}) collective-permute-start(bf16[2,64,1280]{2,1,0:T(8,128)(2,1)S(1)} %get-tuple-element.488), channel_id=1, source_target_pairs={{0,1},{1,0},{2,3},{3,2},{4,5},{5,4},{6,7},{7,6},{8,9},{9,8},{10,11... | collective-permute-start | bytes 983048 | tf_op jit(solution)/shard_map/ppermute | solution.py:168
  550.3 34.7 %collective-permute-start.95 = (bf16[160,2560]{1,0:T(8,128)(2,1)}, bf16[160,2560]{1,0:T(8,128)(2,1)}, u32[]{:S(2)}, u32[]{:S(2)}) collective-permute-start(bf16[160,2560]{1,0:T(8,128)(2,1)} %get-tuple-element.306), channel_id=1, source_target_pairs={{0,8},{8,16},{16,24},{24,28},{28,20},{20,12},{12,4},{4,0},{1,9},{9... | collective-permute-start | bytes 2457608 | tf_op jit(solution)/shard_map/ppermute | solution.py:136
  551.3 34.7 %collective-permute-start.96 = (bf16[160,2560]{1,0:T(8,128)(2,1)}, bf16[160,2560]{1,0:T(8,128)(2,1)}, u32[]{:S(2)}, u32[]{:S(2)}) collective-permute-start(bf16[160,2560]{1,0:T(8,128)(2,1)} %get-tuple-element.307), channel_id=1, source_target_pairs={{8,0},{16,8},{24,16},{28,24},{20,28},{12,20},{4,12},{0,4},{9,1},{1... | collective-permute-start | bytes 2457608 | tf_op jit(solution)/shard_map/ppermute | solution.py:137
  597.6 14.2 %collective-permute-start.103 = (bf16[416,640]{1,0:T(8,128)(2,1)}, bf16[416,640]{1,0:T(8,128)(2,1)}, u32[]{:S(2)}, u32[]{:S(2)}) collective-permute-start(bf16[416,640]{1,0:T(8,128)(2,1)} %pad_maximum_fusion.36), channel_id=1, source_target_pairs={{8,0},{16,8},{24,16},{28,24},{20,28},{12,20},{4,12},{0,4},{9,1},{1... | collective-permute-start | bytes 1597448 | tf_op jit(solution)/shard_map/ppermute | solution.py:137
  610.6 20.6 %collective-permute-start.104 = (bf16[416,640]{1,0:T(8,128)(2,1)S(1)}, bf16[416,640]{1,0:T(8,128)(2,1)S(1)}, u32[]{:S(2)}, u32[]{:S(2)}) collective-permute-start(bf16[416,640]{1,0:T(8,128)(2,1)S(1)} %add_convert_fusion.3), channel_id=1, source_target_pairs={{0,8},{8,16},{16,24},{24,28},{28,20},{20,12},{12,4},{4,0},{1,9},{9... | collective-permute-start | bytes 1597448 | tf_op jit(solution)/shard_map/ppermute | solution.py:136
  612.9 18.3 %collective-permute-start.105 = (bf16[416,640]{1,0:T(8,128)(2,1)S(1)}, bf16[416,640]{1,0:T(8,128)(2,1)S(1)}, u32[]{:S(2)}, u32[]{:S(2)}) collective-permute-start(bf16[416,640]{1,0:T(8,128)(2,1)S(1)} %add_convert_fusion.2), channel_id=1, source_target_pairs={{8,0},{16,8},{24,16},{28,24},{20,28},{12,20},{4,12},{0,4},{9,1},{1... | collective-permute-start | bytes 1597448 | tf_op jit(solution)/shard_map/ppermute | solution.py:137
  631.5 14.2 %collective-permute-start.106 = (bf16[416,640]{1,0:T(8,128)(2,1)S(1)}, bf16[416,640]{1,0:T(8,128)(2,1)S(1)}, u32[]{:S(2)}, u32[]{:S(2)}) collective-permute-start(bf16[416,640]{1,0:T(8,128)(2,1)S(1)} %add_convert_fusion.1), channel_id=1, source_target_pairs={{0,8},{8,16},{16,24},{24,28},{28,20},{20,12},{12,4},{4,0},{1,9},{9... | collective-permute-start | bytes 1597448 | tf_op jit(solution)/shard_map/ppermute | solution.py:136
  632.7 14.0 %collective-permute-start.107 = (bf16[416,640]{1,0:T(8,128)(2,1)S(1)}, bf16[416,640]{1,0:T(8,128)(2,1)}, u32[]{:S(2)}, u32[]{:S(2)}) collective-permute-start(bf16[416,640]{1,0:T(8,128)(2,1)S(1)} %add_convert_fusion), channel_id=1, source_target_pairs={{8,0},{16,8},{24,16},{28,24},{20,28},{12,20},{4,12},{0,4},{9,1},{1... | collective-permute-start | bytes 1597448 | tf_op jit(solution)/shard_map/ppermute | solution.py:137
  685.3 35.9 %all-to-all-start.3 = ((f32[8,2,320]{2,1,0:T(2,128)}), f32[8,2,320]{2,1,0:T(2,128)S(1)}, u32[]{:S(2)}, u32[]{:S(2)}) async-start(f32[8,2,320]{2,1,0:T(2,128)} %broadcast_in_dim.422), calls=%async_computation.3 | async-start | bytes 49152 | tf_op jit(solution)/shard_map/all_to_all | solution.py:151
  704.6 18.3 %collective-permute-start.120 = (bf16[160,2880]{1,0:T(8,128)(2,1)S(1)}, bf16[160,2880]{1,0:T(8,128)(2,1)}, u32[]{:S(2)}, u32[]{:S(2)}) collective-permute-start(bf16[160,2880]{1,0:T(8,128)(2,1)S(1)} %pad_maximum_fusion.13), channel_id=1, source_target_pairs={{0,8},{8,16},{16,24},{24,28},{28,20},{20,12},{12,4},{4,0},{1,9},{9... | collective-permute-start | bytes 2764808 | tf_op jit(solution)/shard_map/ppermute | solution.py:136
  705.7 18.6 %collective-permute-start.121 = (bf16[160,2880]{1,0:T(8,128)(2,1)}, bf16[160,2880]{1,0:T(8,128)(2,1)}, u32[]{:S(2)}, u32[]{:S(2)}) collective-permute-start(bf16[160,2880]{1,0:T(8,128)(2,1)} %pad_maximum_fusion.14), channel_id=1, source_target_pairs={{8,0},{16,8},{24,16},{28,24},{20,28},{12,20},{4,12},{0,4},{9,1},{1... | collective-permute-start | bytes 2764808 | tf_op jit(solution)/shard_map/ppermute | solution.py:137
  726.8 15.9 %collective-permute-start.124 = (bf16[160,2880]{1,0:T(8,128)(2,1)S(1)}, bf16[160,2880]{1,0:T(8,128)(2,1)S(1)}, u32[]{:S(2)}, u32[]{:S(2)}) collective-permute-start(bf16[160,2880]{1,0:T(8,128)(2,1)S(1)} %get-tuple-element.343), channel_id=1, source_target_pairs={{0,8},{8,16},{16,24},{24,28},{28,20},{20,12},{12,4},{4,0},{1,9},{9... | collective-permute-start | bytes 2764808 | tf_op jit(solution)/shard_map/ppermute | solution.py:136
  726.8 18.4 %collective-permute-start.125 = (bf16[160,2880]{1,0:T(8,128)(2,1)S(1)}, bf16[160,2880]{1,0:T(8,128)(2,1)S(1)}, u32[]{:S(2)}, u32[]{:S(2)}) collective-permute-start(bf16[160,2880]{1,0:T(8,128)(2,1)S(1)} %get-tuple-element.344), channel_id=1, source_target_pairs={{8,0},{16,8},{24,16},{28,24},{20,28},{12,20},{4,12},{0,4},{9,1},{1... | collective-permute-start | bytes 2764808 | tf_op jit(solution)/shard_map/ppermute | solution.py:137
  735.6 34.2 %collective-permute-start.114 = (bf16[2,2,64,1280]{3,2,0,1:T(8,128)(2,1)S(1)}, bf16[2,2,64,1280]{3,2,0,1:T(8,128)(2,1)S(1)}, u32[]{:S(2)}, u32[]{:S(2)}) collective-permute-start(bf16[2,2,64,1280]{3,2,0,1:T(8,128)(2,1)S(1)} %fusion.100), channel_id=1, source_target_pairs={{0,1},{1,0},{2,3},{3,2},{4,5},{5,4},{6,7},{7,6},{8,9},{9,8},{10,11... | collective-permute-start | bytes 1966088 | tf_op jit(solution)/shard_map/ppermute | solution.py:187
  747.2 21.1 %collective-permute-start.131 = (bf16[160,2880]{1,0:T(8,128)(2,1)S(1)}, bf16[160,2880]{1,0:T(8,128)(2,1)S(1)}, u32[]{:S(2)}, u32[]{:S(2)}) collective-permute-start(bf16[160,2880]{1,0:T(8,128)(2,1)S(1)} %get-tuple-element.352), channel_id=1, source_target_pairs={{8,0},{16,8},{24,16},{28,24},{20,28},{12,20},{4,12},{0,4},{9,1},{1... | collective-permute-start | bytes 2764808 | tf_op jit(solution)/shard_map/ppermute | solution.py:137
  749.0 18.7 %collective-permute-start.126 = (bf16[160,2880]{1,0:T(8,128)(2,1)S(1)}, bf16[160,2880]{1,0:T(8,128)(2,1)S(1)}, u32[]{:S(2)}, u32[]{:S(2)}) collective-permute-start(bf16[160,2880]{1,0:T(8,128)(2,1)S(1)} %get-tuple-element.347), channel_id=1, source_target_pairs={{0,8},{8,16},{16,24},{24,28},{28,20},{20,12},{12,4},{4,0},{1,9},{9... | collective-permute-start | bytes 2764808 | tf_op jit(solution)/shard_map/ppermute | solution.py:136
  781.3 16.0 %collective-permute-start.128 = (bf16[160,2880]{1,0:T(8,128)(2,1)}, bf16[160,2880]{1,0:T(8,128)(2,1)}, u32[]{:S(2)}, u32[]{:S(2)}) collective-permute-start(bf16[160,2880]{1,0:T(8,128)(2,1)} %pad_maximum_fusion.15), channel_id=1, source_target_pairs={{0,8},{8,16},{16,24},{24,28},{28,20},{20,12},{12,4},{4,0},{1,9},{9... | collective-permute-start | bytes 2764808 | tf_op jit(solution)/shard_map/ppermute | solution.py:136
  790.6 22.3 %collective-permute-start.133 = (bf16[160,2880]{1,0:T(8,128)(2,1)S(1)}, bf16[160,2880]{1,0:T(8,128)(2,1)S(1)}, u32[]{:S(2)}, u32[]{:S(2)}) collective-permute-start(bf16[160,2880]{1,0:T(8,128)(2,1)S(1)} %pad_maximum_fusion.16), channel_id=1, source_target_pairs={{8,0},{16,8},{24,16},{28,24},{20,28},{12,20},{4,12},{0,4},{9,1},{1... | collective-permute-start | bytes 2764808 | tf_op jit(solution)/shard_map/ppermute | solution.py:137
  799.0 17.7 %collective-permute-start.129 = (bf16[160,2880]{1,0:T(8,128)(2,1)S(1)}, bf16[160,2880]{1,0:T(8,128)(2,1)S(1)}, u32[]{:S(2)}, u32[]{:S(2)}) collective-permute-start(bf16[160,2880]{1,0:T(8,128)(2,1)S(1)} %fusion.30), channel_id=1, source_target_pairs={{0,8},{8,16},{16,24},{24,28},{28,20},{20,12},{12,4},{4,0},{1,9},{9... | collective-permute-start | bytes 2764808 | tf_op jit(solution)/shard_map/ppermute | solution.py:136
  802.1 24.6 %collective-permute-start.122 = (bf16[2,2,64,1280]{3,2,0,1:T(8,128)(2,1)S(1)}, bf16[2,2,64,1280]{3,2,0,1:T(8,128)(2,1)}, u32[]{:S(2)}, u32[]{:S(2)}) collective-permute-start(bf16[2,2,64,1280]{3,2,0,1:T(8,128)(2,1)S(1)} %fusion.101), channel_id=1, source_target_pairs={{0,1},{1,0},{2,3},{3,2},{4,5},{5,4},{6,7},{7,6},{8,9},{9,8},{10,11... | collective-permute-start | bytes 1966088 | tf_op jit(solution)/shard_map/ppermute | solution.py:187
  819.9 18.7 %collective-permute-start.134 = (bf16[160,2880]{1,0:T(8,128)(2,1)}, bf16[160,2880]{1,0:T(8,128)(2,1)}, u32[]{:S(2)}, u32[]{:S(2)}) collective-permute-start(bf16[160,2880]{1,0:T(8,128)(2,1)} %get-tuple-element.355), channel_id=1, source_target_pairs={{8,0},{16,8},{24,16},{28,24},{20,28},{12,20},{4,12},{0,4},{9,1},{1... | collective-permute-start | bytes 2764808 | tf_op jit(solution)/shard_map/ppermute | solution.py:137
  823.6 20.9 %all-to-all-start.4 = ((f32[32,1,800]{2,1,0:T(1,128)}), f32[32,1,800]{2,1,0:T(1,128)S(1)}, u32[]{:S(2)}, u32[]{:S(2)}) async-start(f32[32,1,800]{2,1,0:T(1,128)} %reshape.902), calls=%async_computation.4 | async-start | bytes 229376 | tf_op jit(solution)/shard_map/all_to_all | solution.py:739
  828.4 17.2 %collective-permute-start.123 = (bf16[2,64,1280]{2,1,0:T(8,128)(2,1)S(1)}, bf16[2,64,1280]{2,1,0:T(8,128)(2,1)}, u32[]{:S(2)}, u32[]{:S(2)}) collective-permute-start(bf16[2,64,1280]{2,1,0:T(8,128)(2,1)S(1)} %fusion.129), channel_id=1, source_target_pairs={{0,2},{2,0},{1,3},{3,1},{4,6},{6,4},{5,7},{7,5},{8,10},{10,8},{9,1... | collective-permute-start | bytes 983048 | tf_op jit(solution)/shard_map/ppermute | solution.py:193
  830.2 23.2 %collective-permute-start.130 = (bf16[160,2880]{1,0:T(8,128)(2,1)}, bf16[160,2880]{1,0:T(8,128)(2,1)}, u32[]{:S(2)}, u32[]{:S(2)}) collective-permute-start(bf16[160,2880]{1,0:T(8,128)(2,1)} %get-tuple-element.351), channel_id=1, source_target_pairs={{0,8},{8,16},{16,24},{24,28},{28,20},{20,12},{12,4},{4,0},{1,9},{9... | collective-permute-start | bytes 2764808 | tf_op jit(solution)/shard_map/ppermute | solution.py:136
  841.3 19.0 %collective-permute-start.135 = (bf16[160,2880]{1,0:T(8,128)(2,1)}, bf16[160,2880]{1,0:T(8,128)(2,1)}, u32[]{:S(2)}, u32[]{:S(2)}) collective-permute-start(bf16[160,2880]{1,0:T(8,128)(2,1)} %fusion.28), channel_id=1, source_target_pairs={{8,0},{16,8},{24,16},{28,24},{20,28},{12,20},{4,12},{0,4},{9,1},{1... | collective-permute-start | bytes 2764808 | tf_op jit(solution)/shard_map/ppermute | solution.py:137
  (247 other events, 2682.0 us)

commit v3 on v2

--- a/solution.py
+++ b/solution.py
@@ -27,10 +27,15 @@
     return right, [(b, a) for a, b in right]
 
 
-def ring_place(size):
+def ring_owners(size):
     order = ring_order(size)
-    place = jnp.array([order.index(i) for i in range(size)], jnp.int32)
-    return jnp.array(order, jnp.int32), place[lax.axis_index("dp")]
+    table = [[order[(order.index(i) + away) % size] for away in range(size)] for i in range(size)]
+    row = lax.dynamic_slice(
+        jnp.array(table, jnp.uint32),
+        (lax.axis_index("dp").astype(jnp.uint32), jnp.uint32(0)),
+        (1, size),
+    )
+    return [jnp.minimum(row[0, away], jnp.uint32(size - 1)) for away in range(size)]
 
 
 class Gathered:
@@ -38,7 +43,7 @@
         self.ring, self.pack, self.parts, self.taken = ring, pack, parts, 0
 
     def put(self, part, away, start):
-        place = (self.ring.owner(away), jnp.int32(start), jnp.int32(0))
+        place = (self.ring.owner(away), jnp.uint32(start), jnp.uint32(0))
         self.whole = lax.dynamic_update_slice(self.whole, part[None], place)
 
     def begin(self):
@@ -85,8 +90,12 @@
 
     def own(self, away):
         place = self.ring.owner(away)
+        zero = jnp.uint32(0)
         return jnp.concatenate(
-            [lax.dynamic_index_in_dim(b, place, 0, keepdims=False) for b in self.blocks]
+            [
+                lax.dynamic_slice(b, (place, zero, zero), (1,) + b.shape[1:])[0]
+                for b in self.blocks
+            ]
         )
 
     def step(self):
@@ -126,12 +135,11 @@
         self.last = ()
         if self.whole:
             self.right, self.left = ring_pairs(self.size)
-            self.order, self.place = ring_place(self.size)
+            self.owners = ring_owners(self.size)
 
     def step(self, to_right, to_left):
         if self.last:
-            to_right = lax.optimization_barrier((to_right, self.last[0]))[0]
-            to_left = lax.optimization_barrier((to_left, self.last[1]))[0]
+            to_right, to_left = lax.optimization_barrier((to_right, to_left, self.last))[:2]
         self.last = (
             lax.ppermute(to_right, "dp", self.right),
             lax.ppermute(to_left, "dp", self.left),
@@ -139,11 +147,11 @@
         return self.last
 
     def hold(self, *values):
-        held = lax.optimization_barrier(tuple(values) + self.last)[: len(values)]
+        held = lax.optimization_barrier((values, self.last))[0]
         return held[0] if len(values) == 1 else held
 
     def owner(self, away):
-        return self.order[(self.place + away) % self.size]
+        return self.owners[away % self.size]
 
 
 def share_small(values, axis):
@@ -154,8 +162,8 @@
 
 
 def mp_bits():
-    me = lax.axis_index("mp")
-    return me % 2, me // 2
+    me = lax.axis_index("mp").astype(jnp.uint32)
+    return me & 1, me >> 1
 
 
 NEAR = [(0, 1), (1, 0), (2, 3), (3, 2)]
@@ -176,19 +184,26 @@
     return pair(pair(values, near, near_bit), pair(far, both, near_bit), far_bit)
 
 
-def sum_rows(values, items):
-    near_bit, far_bit = mp_bits()
-    columns = values.shape[-1]
-    parts = values.reshape(items, 2, 2, -1, columns)
+def sum_near(values, items):
+    near_bit, _ = mp_bits()
+    parts = values.reshape(items, 2, 2, -1, values.shape[-1])
 
     def near_part(bit):
-        return lax.dynamic_index_in_dim(parts, bit, 2, keepdims=False)
+        zero = jnp.uint32(0)
+        sizes = parts.shape[:2] + (1,) + parts.shape[3:]
+        return lax.dynamic_slice(parts, (zero, zero, bit, zero, zero), sizes)[:, :, 0]
 
     got = lax.ppermute(near_part(1 - near_bit).astype(bf16), "mp", NEAR)
-    held = near_part(near_bit).astype(f32) + got.astype(f32)
+    return near_part(near_bit).astype(f32) + got.astype(f32)
+
+
+def sum_far(held):
+    _, far_bit = mp_bits()
 
     def far_part(bit):
-        return lax.dynamic_index_in_dim(held, bit, 1, keepdims=False)
+        zero = jnp.uint32(0)
+        sizes = held.shape[:1] + (1,) + held.shape[2:]
+        return lax.dynamic_slice(held, (zero, bit, zero, zero), sizes)[:, 0]
 
     got = lax.ppermute(far_part(1 - far_bit).astype(bf16), "mp", FAR)
     return far_part(far_bit) + got.astype(f32)
@@ -407,6 +422,39 @@
     own_channels = conv_in.shape[3]
     share = conv_in.shape[2]
     dp_index, mp_index = lax.axis_index("dp"), lax.axis_index("mp")
+    ring = Ring()
+
+    def across(*parts):
+        return jnp.concatenate(parts, axis=1)
+
+    g_in = Gathered(ring, lambda k: across(*[k[t // 3, t % 3] for t in range(TAPS)]), conv_in)
+    g_out = Gathered(ring, lambda k: across(*[k[t // 3, t % 3].T for t in range(TAPS)]), conv_out)
+    g_self = Gathered(
+        ring,
+        lambda q, k, v, c, s, o: across(q, k, v, c, s.T, o.T),
+        self_query,
+        self_key,
+        self_value,
+        cross_query,
+        self_out,
+        cross_out,
+    )
+    g_text = Gathered(ring, across, cross_key, cross_value)
+    g_feed = Gathered(ring, across, ff_value, ff_gate)
+    g_down = Gathered(ring, lambda down: down.T, ff_down)
+    hidden_own = ff_down.shape[0]
+
+    g_in.begin()
+    g_out.begin()
+    g_in.step()
+    gain_parts = jnp.stack([gn_in_gain, gn_mid_gain, self_gain, cross_gain, ff_gain]).astype(f32)
+    small = jnp.concatenate([gain_parts.reshape(-1), timestep.astype(f32)])
+    small_all = share_small(small, "dp")
+    latent, item_count, bucket, later = ring.hold(
+        latent, item_count, bucket, (cotangent, text_embeds)
+    )
+    g_in.step()
+
     is_live = (jnp.arange(slot_count, dtype=jnp.int32) < item_count[0]).astype(f32)
     widths = jnp.where(
         bucket == 0, SIDE, jnp.where(bucket == 1, 5 * SIDE // 4, 3 * SIDE // 2)
@@ -423,46 +471,12 @@
     keep_all = full_mask[:, :, None]
     counts = filled.astype(f32) * per_group
     channel_start = mp_index * own_channels
-    ring = Ring()
 
     def rows3(values):
         return values.reshape(slot_count, item_rows, values.shape[-1])
 
     def own_sum(values):
-        return sum_rows(values, slot_count)
-
-    def across(*parts):
-        return jnp.concatenate(parts, axis=1)
-
-    g_in = Gathered(ring, lambda k: across(*[k[t // 3, t % 3] for t in range(TAPS)]), conv_in)
-    g_out = Gathered(ring, lambda k: across(*[k[t // 3, t % 3].T for t in range(TAPS)]), conv_out)
-    g_self = Gathered(
-        ring,
-        lambda q, k, v, c, s, o: across(q, k, v, c, s.T, o.T),
-        self_query,
-        self_key,
-        self_value,
-        cross_query,
-        self_out,
-        cross_out,
-    )
-    g_text = Gathered(ring, across, cross_key, cross_value)
-    g_feed = Gathered(ring, across, ff_value, ff_gate)
-    g_down = Gathered(ring, lambda down: down.T, ff_down)
-    hidden_own = ff_down.shape[0]
-
-    g_in.begin()
-    g_in.step()
-    gain_parts = jnp.stack([gn_in_gain, gn_mid_gain, self_gain, cross_gain, ff_gain]).astype(f32)
-    small = jnp.concatenate([gain_parts.reshape(-1), timestep.astype(f32)])
-    small_all = share_small(small, "dp")
-    gains = small_all[:, : 5 * share].reshape(dp_size, 5, share)
-    gains = jnp.swapaxes(gains, 0, 1).reshape(5, channels)
-    gain_in_f, gain_self_f, gain_cross_f, gain_feed_f = gains[0], gains[2], gains[3], gains[4]
-    gain_mid_own = lax.dynamic_slice_in_dim(gains[1], channel_start, own_channels)
-    steps_all = small_all[:, 5 * share :].reshape(-1)
-    latent, gain_in_f, shift_widths = ring.hold(latent, gain_in_f, widths)
-    g_in.step()
+        return sum_far(sum_near(values, slot_count))
 
     masked = latent.astype(f32) * keep
     all_positions = jnp.arange(item_rows, dtype=jnp.int32).reshape(mp_size, 1, local_rows)
@@ -475,10 +489,13 @@
     stats = share_small(jnp.stack([local_sum, local_spread]), "mp").reshape(
         mp_size, 2, slot_count, GN_GROUPS
     )
-    stats, steps_all, cotangent, shift_widths = ring.hold(
-        stats, steps_all, cotangent, shift_widths
-    )
+    stats, small_all, later = ring.hold(stats, small_all, later)
     g_in.step()
+    gains = small_all[:, : 5 * share].reshape(dp_size, 5, share)
+    gains = jnp.swapaxes(gains, 0, 1).reshape(5, channels)
+    gain_in_f, gain_self_f, gain_cross_f, gain_feed_f = gains[0], gains[2], gains[3], gains[4]
+    gain_mid_own = lax.dynamic_slice_in_dim(gains[1], channel_start, own_channels)
+    steps_all = small_all[:, 5 * share :].reshape(-1)
     average = jnp.sum(stats[:, 0], axis=0) / counts[:, None]
     means = stats[:, 0] / jnp.maximum(held, 1.0)[:, :, None]
     variance = (
@@ -488,12 +505,6 @@
     standard_in = (masked - spread(average, per_group)) * scaling_in
     first_act = (jax.nn.silu(standard_in * gain_in_f) * keep).astype(bf16)
     first_all = flat(gather_rows(first_act))
-    first_all, steps_all, cotangent, shift_widths = ring.hold(
-        first_all, steps_all, cotangent, shift_widths
-    )
-    tall, wide = tap_matrices(shift_widths, item_rows)
-    g_out.begin()
-    g_in.step()
 
     half_width = C // 2
     wave = dp_index * share + jnp.arange(share, dtype=jnp.int32)
@@ -503,18 +514,26 @@
         jnp.where(wave[None, :] < half_width, jnp.cos(angles), jnp.sin(angles))
     ).astype(bf16)
     time_part = jnp.dot(time_act, time_weight, preferred_element_type=f32)
+    first_all, time_part, later = ring.hold(first_all, time_part, later)
+    g_in.step()
+    first_all, time_part, shift_widths, later = ring.hold(first_all, time_part, widths, later)
+    w_in = g_in.whole
+
+    g_out.step()
+    first_taps = product(first_all, w_in).astype(bf16)
+    cotangent, text_embeds = later
+    tall, wide = tap_matrices(shift_widths, item_rows)
+
     time_added = lax.all_to_all(
         time_part.reshape(dp_size, slot_count, own_channels), "dp", 0, 0, tiled=True
     ).sum(0)
-    w_in = g_in.whole
-
-    g_out.step()
-    first_taps = product(first_all, w_in).astype(bf16)
     first_taps, time_added, cotangent, text_embeds = ring.hold(
         first_taps, time_added, cotangent, text_embeds
     )
     g_out.step()
     middle = (shift_sum(wide, first_taps) + time_added[:, None, :]) * keep_all
+    middle, cotangent, text_embeds = ring.hold(middle, cotangent, text_embeds)
+    g_out.step()
     average_mid = group_sum(middle, per_group) / counts[:, None]
     apart_mid = middle - spread(average_mid, per_group)
     center_mid = apart_mid * keep_all
@@ -523,29 +542,28 @@
         per_group,
     )
     standard_mid = apart_mid * scaling_mid
-    standard_mid, cotangent, text_embeds = ring.hold(standard_mid, cotangent, text_embeds)
+    second_act = (jax.nn.silu(standard_mid * gain_mid_own) * keep_all).astype(bf16)
+    second_act, cotangent, text_embeds = ring.hold(second_act, cotangent, text_embeds)
+    g_self.begin()
     g_out.step()
-    second_act = (jax.nn.silu(standard_mid * gain_mid_own) * keep_all).astype(bf16)
     second_taps = shift_stack(tall, flat(second_act))
     second_taps, cotangent, text_embeds = ring.hold(second_taps, cotangent, text_embeds)
-    g_self.begin()
-    g_out.step()
-    out_grad = cotangent.astype(f32) * keep
-    feed_branch = flat(gather_rows(out_grad.astype(bf16)))
     w_out = g_out.whole
     g_self.step()
     second_out = product_back(second_taps, w_out)
-    second_out, text_embeds = ring.hold(second_out, text_embeds)
+    second_out, cotangent, text_embeds = ring.hold(second_out, cotangent, text_embeds)
     g_self.step()
     resnet = (masked + own_sum(second_out)) * keep
+    resnet, cotangent, text_embeds = ring.hold(resnet, cotangent, text_embeds)
+    g_self.step()
 
     attend_in, normal_self, scaling_self = norm_rows(resnet, gain_self_f)
-    attend_in = ring.hold(attend_in)
+    attend_all = flat(gather_rows(attend_in))
+    g_text.begin()
+    attend_all, cotangent = ring.hold(attend_all, cotangent)
     g_self.step()
-    attend_all = flat(gather_rows(attend_in))
-    attend_all = ring.hold(attend_all)
-    g_text.begin()
-    g_self.step()
+    out_grad = cotangent.astype(f32) * keep
+    feed_branch = flat(gather_rows(out_grad.astype(bf16)))
     w_self = g_self.whole
     qkv_full = w_self[:, : 3 * own_channels]
     cq_full = w_self[:, 3 * own_channels : 4 * own_channels]
@@ -632,7 +650,10 @@
     cross_dq = flat(cross_dq)
     cross_dq, cross_dk, cross_dv = ring.hold(cross_dq, cross_dk, cross_dv)
     s_feed.step()
-    cross_back = own_sum(product_back(cross_dq, cq_full))
+    cross_near = sum_near(product_back(cross_dq, cq_full), slot_count)
+    cross_near = ring.hold(cross_near)
+    s_feed.step()
+    cross_back = sum_far(cross_near)
     grad_cross_out = weight_grad(cross_branch, flat(cross_mix))
     grad_cross_query = weight_grad(cross_all, cross_dq)
     s_cross = Scattered(
@@ -640,29 +661,28 @@
         weight_grad(text_rows, flat(jnp.concatenate([cross_dk, cross_dv], axis=2))),
         jnp.concatenate([grad_cross_query, grad_cross_out], axis=1),
     )
-    cross_back = ring.hold(cross_back)
-    s_feed.step()
     cross_dv_rows, grad_gain_cross = norm_rows_back(
         cross_back, normal_cross, scaling_cross, gain_cross_f
     )
     self_grad = cross_grad + cross_dv_rows
 
     self_branch = flat(gather_rows(self_grad.astype(bf16)))
-    mixture_grad = product(self_branch, so_full).astype(bf16)
-    mixture_grad = rows3(ring.hold(mixture_grad))
+    self_branch = ring.hold(self_branch)
     s_feed.step()
+    mixture_grad = rows3(product(self_branch, so_full).astype(bf16))
     qkv_grad = flat(
         jnp.concatenate(
             attend_back(query_rows, key_rows, value_rows, mixture_grad, self_chances), axis=2
         )
     )
-    self_back = own_sum(product_back(qkv_grad, qkv_full))
-    self_back = ring.hold(self_back)
+    qkv_grad = ring.hold(qkv_grad)
     s_cross.step()
+    self_near = sum_near(product_back(qkv_grad, qkv_full), slot_count)
+    self_near = ring.hold(self_near)
+    s_cross.step()
+    self_back = sum_far(self_near)
     self_dv_rows, grad_gain_self = norm_rows_back(self_back, normal_self, scaling_self, gain_self_f)
     resnet_grad = (self_grad + self_dv_rows) * keep
-    resnet_grad = ring.hold(resnet_grad)
-    s_cross.step()
     resnet_branch = flat(gather_rows(resnet_grad.astype(bf16)))
     resnet_branch = ring.hold(resnet_branch)
     s_cross.step()
@@ -691,13 +711,28 @@
     middle_taps = shift_stack_back(wide, flat(middle_grad))
     middle_taps = ring.hold(middle_taps)
     s_self.step()
-    first_part = product_back(middle_taps, w_in)
-    first_part = ring.hold(first_part)
+    first_near = sum_near(product_back(middle_taps, w_in), slot_count)
+    first_near = ring.hold(first_near)
     s_self.step()
     s_in = Scattered(ring, weight_grad(first_all, middle_taps))
-    first_grad = own_sum(first_part)
-    first_grad, hidden = ring.hold(first_grad, hidden)
+    first_grad = sum_far(first_near)
+    first_grad, hidden, middle_grad = ring.hold(first_grad, hidden, middle_grad)
     s_out.step()
+
+    in_slope = silu_back(standard_in * gain_in_f, first_grad * keep)
+    in_gain_part = jnp.sum(in_slope * standard_in, axis=(0, 1))
+    hat_in = in_slope * gain_in_f
+    in_a, in_b = lax.psum(
+        (group_sum(hat_in, per_group), group_sum(hat_in * standard_in, per_group)), "mp"
+    )
+    in_a, in_b, in_gain_part, middle_grad, hidden = ring.hold(
+        in_a, in_b, in_gain_part, middle_grad, hidden
+    )
+    s_out.step()
+    in_a = spread(in_a / counts[:, None], per_group)
+    in_b = spread(in_b / counts[:, None], per_group)
+    grouped_grad = scaling_in * (hat_in - (in_a + standard_in * in_b))
+    latent_grad = ((resnet_grad + grouped_grad) * keep).astype(bf16)
 
     time_sum = jnp.sum(middle_grad.astype(f32), axis=1)
     time_sum_all = share_small(time_sum, "dp").reshape(-1, own_channels)
@@ -708,25 +743,10 @@
         precision=highest,
         preferred_element_type=f32,
     )
-
-    in_slope = silu_back(standard_in * gain_in_f, first_grad * keep)
-    in_gain_part = jnp.sum(in_slope * standard_in, axis=(0, 1))
-    hat_in = in_slope * gain_in_f
-    in_a, in_b = lax.psum(
-        (group_sum(hat_in, per_group), group_sum(hat_in * standard_in, per_group)), "mp"
-    )
-    in_a, in_b, grad_time = ring.hold(in_a, in_b, grad_time)
+    latent_grad, grad_time, in_gain_part, hidden = ring.hold(
+        latent_grad, grad_time, in_gain_part, hidden
+    )
     s_out.step()
-    in_a = spread(in_a / counts[:, None], per_group)
-    in_b = spread(in_b / counts[:, None], per_group)
-    grouped_grad = scaling_in * (hat_in - (in_a + standard_in * in_b))
-    latent_grad = ((resnet_grad + grouped_grad) * keep).astype(bf16)
-    latent_grad, hidden = ring.hold(latent_grad, hidden)
-    s_out.step()
-    output = ((after_cross + own_sum(product_back(hidden, w_down))) * keep).astype(bf16)
-    output = ring.hold(output)
-    s_out.step()
-    s_in.step()
 
     mid_gain_whole = lax.dynamic_update_slice_in_dim(
         jnp.zeros((channels,), f32), mid_gain_part, channel_start, 0
@@ -739,7 +759,13 @@
     gain_sums = lax.all_to_all(
         gain_parts.reshape(dp_size * mp_size, 5, share), ("dp", "mp"), 0, 0, tiled=True
     ).sum(0)
-    gain_sums = ring.hold(gain_sums)
+    gain_sums, hidden = ring.hold(gain_sums, hidden)
+    s_out.step()
+    output_near = sum_near(product_back(hidden, w_down), slot_count)
+    output_near = ring.hold(output_near)
+    s_in.step()
+    output = ((after_cross + sum_far(output_near)) * keep).astype(bf16)
+    output = ring.hold(output)
     s_in.step()
     s_in.step()
     s_in.step()

time: 878 us -> 858 us (0.977)
  between operations: 27.6 us -> 10.8 us
  waiting for transfers between devices: 323 us -> 337 us
  other arithmetic: 102 us -> 91.3 us
    ppermute x48, waiting for transfers between devices: 49.9 us -> 80.5 us  [step(): lax.ppermute(to_left, 'dp', self.left)]
    ppermute x48, waiting for transfers between devices: 244 us -> 235 us  [step(): lax.ppermute(to_right, 'dp', self.right)]
    unnamed x385 -> x365, local copies, waits for them, and re-layouts: 19.4 us -> 28.4 us
    convert_element_type x10 -> x12, other arithmetic: 17.5 us -> 20 us  [step(): behind = (behind.astype(f32) + self.from_right).astype(bf16)]
  transfers between devices with their start and end apart: 141 -> 141, of which waited for: 74 -> 83; matrix products, arithmetic and copies ran while one was open for 37% -> 36% of each run, Pallas kernels for 0% -> 0%
where the time goes in v3:
time: 858 us; the launch traced here: 849 us
  waiting for transfers between devices  337 us (39%)
  local copies, waits for them, and re-layouts  152 us (18%)
  starting transfers between devices  139 us (16%)
  matrix products  112 us (13%)
  other arithmetic  91.3 us (11%)
  between operations  10.8 us (1%)
    ppermute x48, waiting for transfers between devices, step(): lax.ppermute(to_right, 'dp', self.right)  235 us
    ppermute x48, waiting for transfers between devices, step(): lax.ppermute(to_left, 'dp', self.left)  80.5 us
    ppermute x48, starting transfers between devices, step(): lax.ppermute(to_right, 'dp', self.right)  58.3 us
    dynamic_update_slice x53, local copies, waits for them, and re-layouts, put(): self.whole = lax.dynamic_update_slice(self.whole, part[None], place)  50 us
    ppermute x48, starting transfers between devices, step(): lax.ppermute(to_left, 'dp', self.left)  44.2 us
    dot_general x13, matrix products, product(): return jnp.dot(former, latter, preferred_element_type=f32)  37.6 us
    dot_general x8, matrix products, product_back(): lax.dot_general(former, latter, (((1,), (1,)), ((), ())), preferred_eleme...  29.7 us
    unnamed x365, local copies, waits for them, and re-layouts  28.4 us
  transfers between devices with their start and end apart: 141, of which 83 were waited for; matrix products, arithmetic and copies ran while one was open for 36% of the time, Pallas kernels for 0%

profile of v3, /device:TPU:0, one launch (start us, length us, event | category | flops | bytes accessed | tf_op | source)
XLA Modules:
  0.0 848.5 jit_solution(18219928092955417682)
XLA Ops:
  2.9 3.1 collective-permute-start
  6.9 6.2 all-to-all-start.1
  18.9 3.6 broadcast.530.clone
  24.9 3.6 broadcast.530.clone.1
  36.8 3.2 all-to-all-start
  47.2 16.5 %collective-permute-done.2 = bf16[160,2880]{1,0:T(8,128)(2,1)} collective-permute-done((bf16[160,2880]{1,0:T(8,128)(2,1)S(1)}, bf16[160,2880]{1,0:T(8,128)(2,1)}, u32[]{:S(2)}, u32[]{:S(2)}) %collective-permute-start.2) | collective-permute-done | bytes 921632 | tf_op jit(solution)/shard_map/ppermute | solution.py:144
  78.6 16.6 %collective-permute-done.7 = bf16[160,2880]{1,0:T(8,128)(2,1)S(1)} collective-permute-done((bf16[160,2880]{1,0:T(8,128)(2,1)}, bf16[160,2880]{1,0:T(8,128)(2,1)S(1)}, u32[]{:S(2)}, u32[]{:S(2)}) %collective-permute-start.7) | collective-permute-done | bytes 921632 | tf_op jit(solution)/shard_map/ppermute | solution.py:144
  100.7 8.1 collective-permute-done.9
  112.1 3.3 all-to-all-start.2
  120.4 9.2 %convolution_convert_fusion.5 = bf16[512,2880]{0,1:T(8,128)(2,1)} fusion(bf16[512,1280]{1,0:T(8,128)(2,1)} %bitcast.870, bf16[1280,2880]{1,0:T(8,128)(2,1)} %bitcast.35), kind=kOutput, calls=%fused_computation.12 | convolution fusion | flops 3776348160 | bytes 11632640 | tf_op jit(solution)/shard_map/dot_general | solution.py:221
  132.3 4.8 collective-permute-done.11
  155.8 3.9 collective-permute-done.13
  169.2 12.0 %collective-permute-done.15 = bf16[160,2880]{1,0:T(8,128)(2,1)S(1)} collective-permute-done((bf16[160,2880]{1,0:T(8,128)(2,1)}, bf16[160,2880]{1,0:T(8,128)(2,1)S(1)}, u32[]{:S(2)}, u32[]{:S(2)}) %collective-permute-start.15) | collective-permute-done | bytes 921632 | tf_op jit(solution)/shard_map/ppermute | solution.py:144
  192.1 2.6 concatenate.205
  207.9 6.7 fusion.231
  217.0 14.1 %collective-permute-done.23 = bf16[160,1920]{1,0:T(8,128)(2,1)} collective-permute-done((bf16[160,1920]{1,0:T(8,128)(2,1)S(1)}, bf16[160,1920]{1,0:T(8,128)(2,1)}, u32[]{:S(2)}, u32[]{:S(2)}) %collective-permute-start.23) | collective-permute-done | bytes 614432 | tf_op jit(solution)/shard_map/ppermute | solution.py:144
  239.3 4.6 collective-permute-done.22
  255.6 2.7 collective-permute-done.30
  292.6 3.4 collective-permute-done.38
  308.3 2.9 collective-permute-done.37
  314.6 10.1 %collective-permute-done.45 = bf16[160,2560]{1,0:T(8,128)(2,1)} collective-permute-done((bf16[160,2560]{1,0:T(8,128)(2,1)}, bf16[160,2560]{1,0:T(8,128)(2,1)}, u32[]{:S(2)}, u32[]{:S(2)}) %collective-permute-start.45) | collective-permute-done | bytes 819232 | tf_op jit(solution)/shard_map/ppermute | solution.py:144
  350.0 13.8 %collective-permute-done.54 = bf16[160,2560]{1,0:T(8,128)(2,1)S(1)} collective-permute-done((bf16[160,2560]{1,0:T(8,128)(2,1)}, bf16[160,2560]{1,0:T(8,128)(2,1)S(1)}, u32[]{:S(2)}, u32[]{:S(2)}) %collective-permute-start.54) | collective-permute-done | bytes 819232 | tf_op jit(solution)/shard_map/ppermute | solution.py:144
  370.6 5.0 collective-permute-done.56
  379.2 7.2 collective-permute-done.58
  389.8 3.5 fusion.232
  393.4 5.7 multiply_convert_fusion.1
  403.4 4.7 collective-permute-done.62
  411.9 5.4 collective-permute-done.64
  424.6 3.6 fusion.233
  430.6 3.8 convolution_convert_fusion.2
  434.5 5.8 collective-permute-done.71
  444.3 5.8 collective-permute-done.75
  454.8 7.8 collective-permute-done.80
  469.7 2.8 collective-permute-done.82
  483.4 3.0 convolution_convert_fusion.16
  493.5 3.2 convolution_convert_fusion.12
  497.1 2.5 fusion.64
  513.9 3.4 fusion.36
  519.4 4.1 collective-permute-done.87
  525.8 12.1 %collective-permute-done.91 = bf16[160,2560]{1,0:T(8,128)(2,1)} collective-permute-done((bf16[160,2560]{1,0:T(8,128)(2,1)}, bf16[160,2560]{1,0:T(8,128)(2,1)}, u32[]{:S(2)}, u32[]{:S(2)}) %collective-permute-start.91) | collective-permute-done | bytes 819232 | tf_op jit(solution)/shard_map/ppermute | solution.py:144
  538.7 3.4 fusion.34
  557.0 4.5 collective-permute-done.93
  570.7 4.6 collective-permute-done.97
  581.8 8.1 collective-permute-done.102
  601.5 8.3 collective-permute-done.104
  616.0 9.4 %convolution_convert_fusion.4 = bf16[512,2880]{0,1:T(8,128)(2,1)S(1)} fusion(bf16[512,1280]{1,0:T(8,128)(2,1)S(1)} %bitcast.884, bf16[1280,2880]{1,0:T(8,128)(2,1)} %bitcast.69), kind=kOutput, calls=%fused_computation.11 | convolution fusion | flops 3776348160 | bytes 11632640 | tf_op jit(solution)/shard_map/dot_general | solution.py:221
  625.4 4.5 convolution_convert_fusion.1
  648.8 5.4 collective-permute-done.110
  660.9 3.8 concatenate.253
  665.9 3.9 concatenate.252
  673.8 6.9 collective-permute-done.116
  684.6 6.8 fusion.234
  697.7 4.6 convolution_convert_fusion
  702.3 13.4 %collective-permute-done.120 = bf16[160,2880]{1,0:T(8,128)(2,1)S(1)} collective-permute-done((bf16[160,2880]{1,0:T(8,128)(2,1)S(1)}, bf16[160,2880]{1,0:T(8,128)(2,1)S(1)}, u32[]{:S(2)}, u32[]{:S(2)}) %collective-permute-start.120) | collective-permute-done | bytes 921632 | tf_op jit(solution)/shard_map/ppermute | solution.py:144
  721.1 14.6 %collective-permute-done.122 = bf16[160,2880]{1,0:T(8,128)(2,1)S(1)} collective-permute-done((bf16[160,2880]{1,0:T(8,128)(2,1)S(1)}, bf16[160,2880]{1,0:T(8,128)(2,1)S(1)}, u32[]{:S(2)}, u32[]{:S(2)}) %collective-permute-start.122) | collective-permute-done | bytes 921632 | tf_op jit(solution)/shard_map/ppermute | solution.py:144
  740.9 6.0 all-reduce
  748.2 4.1 all-to-all-start.3
  756.4 2.7 all-to-all-done.3
  762.0 2.6 all-to-all-start.4
  776.6 3.8 fusion.235
  780.6 10.8 %collective-permute-done.131 = bf16[160,2880]{1,0:T(8,128)(2,1)} collective-permute-done((bf16[160,2880]{1,0:T(8,128)(2,1)}, bf16[160,2880]{1,0:T(8,128)(2,1)}, u32[]{:S(2)}, u32[]{:S(2)}) %collective-permute-start.131) | collective-permute-done | bytes 921632 | tf_op jit(solution)/shard_map/ppermute | solution.py:145
  800.5 16.7 %collective-permute-done.133 = bf16[160,2880]{1,0:T(8,128)(2,1)S(1)} collective-permute-done((bf16[160,2880]{1,0:T(8,128)(2,1)S(1)}, bf16[160,2880]{1,0:T(8,128)(2,1)S(1)}, u32[]{:S(2)}, u32[]{:S(2)}) %collective-permute-start.133) | collective-permute-done | bytes 921632 | tf_op jit(solution)/shard_map/ppermute | solution.py:145
  824.9 15.8 %collective-permute-done.135 = bf16[160,2880]{1,0:T(8,128)(2,1)S(1)} collective-permute-done((bf16[160,2880]{1,0:T(8,128)(2,1)S(1)}, bf16[160,2880]{1,0:T(8,128)(2,1)S(1)}, u32[]{:S(2)}, u32[]{:S(2)}) %collective-permute-start.135) | collective-permute-done | bytes 921632 | tf_op jit(solution)/shard_map/ppermute | solution.py:145
  842.1 2.7 fusion.23
  (1024 shorter events, 425.9 us)
Async XLA Ops:
  2.9 31.2 %collective-permute-start = (bf16[160,2880]{1,0:T(8,128)(2,1)S(1)}, bf16[160,2880]{1,0:T(8,128)(2,1)S(1)}, u32[]{:S(2)}, u32[]{:S(2)}) collective-permute-start(bf16[160,2880]{1,0:T(8,128)(2,1)S(1)} %concatenate.197), channel_id=1, source_target_pairs={{0,8},{8,16},{16,24},{24,28},{28,20},{20,12},{12,4},{4,0},{1,9},{9... | collective-permute-start | bytes 2764808 | tf_op jit(solution)/shard_map/ppermute | solution.py:144
  5.9 28.2 %collective-permute-start.1 = (bf16[160,2880]{1,0:T(8,128)(2,1)S(1)}, bf16[160,2880]{1,0:T(8,128)(2,1)}, u32[]{:S(2)}, u32[]{:S(2)}) collective-permute-start(bf16[160,2880]{1,0:T(8,128)(2,1)S(1)} %concatenate.197), channel_id=1, source_target_pairs={{8,0},{16,8},{24,16},{28,24},{20,28},{12,20},{4,12},{0,4},{9,1},{1... | collective-permute-start | bytes 2764808 | tf_op jit(solution)/shard_map/ppermute | solution.py:145
  6.9 27.2 %all-to-all-start.1 = ((f32[8,1,802]{2,1,0:T(1,128)}), f32[8,1,802]{2,1,0:T(1,128)S(1)}, u32[]{:S(2)}, u32[]{:S(2)}) async-start(f32[8,1,802]{2,1,0:T(1,128)} %broadcast_in_dim.340), calls=%async_computation.1 | async-start | bytes 57344 | tf_op jit(solution)/shard_map/all_to_all | solution.py:159
  40.0 23.7 %collective-permute-start.2 = (bf16[160,2880]{1,0:T(8,128)(2,1)S(1)}, bf16[160,2880]{1,0:T(8,128)(2,1)}, u32[]{:S(2)}, u32[]{:S(2)}) collective-permute-start(bf16[160,2880]{1,0:T(8,128)(2,1)S(1)} %collective-permute-done), channel_id=1, source_target_pairs={{0,8},{8,16},{16,24},{24,28},{28,20},{20,12},{12,4},{4,0},{1,9},{9... | collective-permute-start | bytes 2764808 | tf_op jit(solution)/shard_map/ppermute | solution.py:144
  42.1 23.1 %collective-permute-start.3 = (bf16[160,2880]{1,0:T(8,128)(2,1)}, bf16[160,2880]{1,0:T(8,128)(2,1)S(1)}, u32[]{:S(2)}, u32[]{:S(2)}) collective-permute-start(bf16[160,2880]{1,0:T(8,128)(2,1)} %collective-permute-done.1), channel_id=1, source_target_pairs={{8,0},{16,8},{24,16},{28,24},{20,28},{12,20},{4,12},{0,4},{9,1},{1... | collective-permute-start | bytes 2764808 | tf_op jit(solution)/shard_map/ppermute | solution.py:145
  71.6 23.5 %collective-permute-start.7 = (bf16[160,2880]{1,0:T(8,128)(2,1)}, bf16[160,2880]{1,0:T(8,128)(2,1)S(1)}, u32[]{:S(2)}, u32[]{:S(2)}) collective-permute-start(bf16[160,2880]{1,0:T(8,128)(2,1)} %collective-permute-done.2), channel_id=1, source_target_pairs={{0,8},{8,16},{16,24},{24,28},{28,20},{20,12},{12,4},{4,0},{1,9},{9... | collective-permute-start | bytes 2764808 | tf_op jit(solution)/shard_map/ppermute | solution.py:144
  73.2 23.2 %collective-permute-start.8 = (bf16[160,2880]{1,0:T(8,128)(2,1)}, bf16[160,2880]{1,0:T(8,128)(2,1)S(1)}, u32[]{:S(2)}, u32[]{:S(2)}) collective-permute-start(bf16[160,2880]{1,0:T(8,128)(2,1)} %copy-done.78), channel_id=1, source_target_pairs={{8,0},{16,8},{24,16},{28,24},{20,28},{12,20},{4,12},{0,4},{9,1},{1... | collective-permute-start | bytes 2764808 | tf_op jit(solution)/shard_map/ppermute | solution.py:145
  112.1 20.1 %all-to-all-start.2 = ((f32[8,2,320]{2,1,0:T(2,128)}), f32[8,2,320]{2,1,0:T(2,128)S(1)}, u32[]{:S(2)}, u32[]{:S(2)}) async-start(f32[8,2,320]{2,1,0:T(2,128)} %reshape.808), calls=%async_computation.2 | async-start | bytes 49152 | tf_op jit(solution)/shard_map/all_to_all | solution.py:527
  115.5 21.6 %collective-permute-start.11 = (bf16[160,2880]{1,0:T(8,128)(2,1)}, bf16[160,2880]{1,0:T(8,128)(2,1)}, u32[]{:S(2)}, u32[]{:S(2)}) collective-permute-start(bf16[160,2880]{1,0:T(8,128)(2,1)} %copy-done.32), channel_id=1, source_target_pairs={{0,8},{8,16},{16,24},{24,28},{28,20},{20,12},{12,4},{4,0},{1,9},{9... | collective-permute-start | bytes 2764808 | tf_op jit(solution)/shard_map/ppermute | solution.py:144
  117.4 21.2 %collective-permute-start.12 = (bf16[160,2880]{1,0:T(8,128)(2,1)}, bf16[160,2880]{1,0:T(8,128)(2,1)}, u32[]{:S(2)}, u32[]{:S(2)}) collective-permute-start(bf16[160,2880]{1,0:T(8,128)(2,1)} %copy-done.32), channel_id=1, source_target_pairs={{8,0},{16,8},{24,16},{28,24},{20,28},{12,20},{4,12},{0,4},{9,1},{1... | collective-permute-start | bytes 2764808 | tf_op jit(solution)/shard_map/ppermute | solution.py:145
  139.6 20.1 %collective-permute-start.13 = (bf16[160,2880]{1,0:T(8,128)(2,1)}, bf16[160,2880]{1,0:T(8,128)(2,1)}, u32[]{:S(2)}, u32[]{:S(2)}) collective-permute-start(bf16[160,2880]{1,0:T(8,128)(2,1)} %collective-permute-done.11), channel_id=1, source_target_pairs={{0,8},{8,16},{16,24},{24,28},{28,20},{20,12},{12,4},{4,0},{1,9},{9... | collective-permute-start | bytes 2764808 | tf_op jit(solution)/shard_map/ppermute | solution.py:144
  141.1 19.8 %collective-permute-start.14 = (bf16[160,2880]{1,0:T(8,128)(2,1)}, bf16[160,2880]{1,0:T(8,128)(2,1)}, u32[]{:S(2)}, u32[]{:S(2)}) collective-permute-start(bf16[160,2880]{1,0:T(8,128)(2,1)} %collective-permute-done.12), channel_id=1, source_target_pairs={{8,0},{16,8},{24,16},{28,24},{20,28},{12,20},{4,12},{0,4},{9,1},{1... | collective-permute-start | bytes 2764808 | tf_op jit(solution)/shard_map/ppermute | solution.py:145
  162.3 18.8 %collective-permute-start.15 = (bf16[160,2880]{1,0:T(8,128)(2,1)}, bf16[160,2880]{1,0:T(8,128)(2,1)S(1)}, u32[]{:S(2)}, u32[]{:S(2)}) collective-permute-start(bf16[160,2880]{1,0:T(8,128)(2,1)} %collective-permute-done.13), channel_id=1, source_target_pairs={{0,8},{8,16},{16,24},{24,28},{28,20},{20,12},{12,4},{4,0},{1,9},{9... | collective-permute-start | bytes 2764808 | tf_op jit(solution)/shard_map/ppermute | solution.py:144
  163.7 18.4 %collective-permute-start.16 = (bf16[160,2880]{1,0:T(8,128)(2,1)}, bf16[160,2880]{1,0:T(8,128)(2,1)S(1)}, u32[]{:S(2)}, u32[]{:S(2)}) collective-permute-start(bf16[160,2880]{1,0:T(8,128)(2,1)} %collective-permute-done.14), channel_id=1, source_target_pairs={{8,0},{16,8},{24,16},{28,24},{20,28},{12,20},{4,12},{0,4},{9,1},{1... | collective-permute-start | bytes 2764808 | tf_op jit(solution)/shard_map/ppermute | solution.py:145
  187.9 13.8 %collective-permute-start.17 = (bf16[80,2880]{1,0:T(8,128)(2,1)}, bf16[80,2880]{1,0:T(8,128)(2,1)}, u32[]{:S(2)}, u32[]{:S(2)}) collective-permute-start(bf16[80,2880]{1,0:T(8,128)(2,1)} %slice.982), channel_id=1, source_target_pairs={{0,8},{8,16},{16,24},{24,28},{28,20},{20,12},{12,4},{4,0},{1,9},{9... | collective-permute-start | bytes 1382408 | tf_op jit(solution)/shard_map/ppermute | solution.py:144
  214.7 20.6 %collective-permute-start.21 = (bf16[2,2,64,1280]{3,2,0,1:T(8,128)(2,1)S(1)}, bf16[2,2,64,1280]{3,2,0,1:T(8,128)(2,1)S(1)}, u32[]{:S(2)}, u32[]{:S(2)}) collective-permute-start(bf16[2,2,64,1280]{3,2,0,1:T(8,128)(2,1)S(1)} %fusion.84), channel_id=1, source_target_pairs={{0,1},{1,0},{2,3},{3,2},{4,5},{5,4},{6,7},{7,6},{8,9},{9,8},{10,11... | collective-permute-start | bytes 1966088 | tf_op jit(solution)/shard_map/ppermute | solution.py:196
  214.8 16.4 %collective-permute-start.23 = (bf16[160,1920]{1,0:T(8,128)(2,1)S(1)}, bf16[160,1920]{1,0:T(8,128)(2,1)}, u32[]{:S(2)}, u32[]{:S(2)}) collective-permute-start(bf16[160,1920]{1,0:T(8,128)(2,1)S(1)} %collective-permute-done.19), channel_id=1, source_target_pairs={{0,8},{8,16},{16,24},{24,28},{28,20},{20,12},{12,4},{4,0},{1,9},{9... | collective-permute-start | bytes 1843208 | tf_op jit(solution)/shard_map/ppermute | solution.py:144
  216.0 16.0 %collective-permute-start.24 = (bf16[160,1920]{1,0:T(8,128)(2,1)S(1)}, bf16[160,1920]{1,0:T(8,128)(2,1)}, u32[]{:S(2)}, u32[]{:S(2)}) collective-permute-start(bf16[160,1920]{1,0:T(8,128)(2,1)S(1)} %collective-permute-done.20), channel_id=1, source_target_pairs={{8,0},{16,8},{24,16},{28,24},{20,28},{12,20},{4,12},{0,4},{9,1},{1... | collective-permute-start | bytes 1843208 | tf_op jit(solution)/shard_map/ppermute | solution.py:145
  232.1 15.3 %collective-permute-start.28 = (bf16[160,1920]{1,0:T(8,128)(2,1)}, bf16[160,1920]{1,0:T(8,128)(2,1)S(1)}, u32[]{:S(2)}, u32[]{:S(2)}) collective-permute-start(bf16[160,1920]{1,0:T(8,128)(2,1)} %collective-permute-done.23), channel_id=1, source_target_pairs={{0,8},{8,16},{16,24},{24,28},{28,20},{20,12},{12,4},{4,0},{1,9},{9... | collective-permute-start | bytes 1843208 | tf_op jit(solution)/shard_map/ppermute | solution.py:144
  232.9 15.2 %collective-permute-start.29 = (bf16[160,1920]{1,0:T(8,128)(2,1)}, bf16[160,1920]{1,0:T(8,128)(2,1)S(1)}, u32[]{:S(2)}, u32[]{:S(2)}) collective-permute-start(bf16[160,1920]{1,0:T(8,128)(2,1)} %collective-permute-done.24), channel_id=1, source_target_pairs={{8,0},{16,8},{24,16},{28,24},{20,28},{12,20},{4,12},{0,4},{9,1},{1... | collective-permute-start | bytes 1843208 | tf_op jit(solution)/shard_map/ppermute | solution.py:145
  264.5 19.6 %collective-permute-start.52 = (bf16[2,64,1280]{2,1,0:T(8,128)(2,1)S(1)}, bf16[2,64,1280]{2,1,0:T(8,128)(2,1)}, u32[]{:S(2)}, u32[]{:S(2)}) collective-permute-start(bf16[2,64,1280]{2,1,0:T(8,128)(2,1)S(1)} %fusion.99), channel_id=1, source_target_pairs={{0,2},{2,0},{1,3},{3,1},{4,6},{6,4},{5,7},{7,5},{8,10},{10,8},{9,1... | collective-permute-start | bytes 983048 | tf_op jit(solution)/shard_map/ppermute | solution.py:175
  266.2 18.0 %collective-permute-start.51 = (bf16[2,64,1280]{2,1,0:T(8,128)(2,1)S(1)}, bf16[2,64,1280]{2,1,0:T(8,128)(2,1)}, u32[]{:S(2)}, u32[]{:S(2)}) collective-permute-start(bf16[2,64,1280]{2,1,0:T(8,128)(2,1)S(1)} %fusion.99), channel_id=1, source_target_pairs={{0,1},{1,0},{2,3},{3,2},{4,5},{5,4},{6,7},{7,6},{8,9},{9,8},{10,11... | collective-permute-start | bytes 983048 | tf_op jit(solution)/shard_map/ppermute | solution.py:176
  285.5 16.8 %collective-permute-start.36 = (bf16[2,2,64,1280]{3,2,0,1:T(8,128)(2,1)S(1)}, bf16[2,2,64,1280]{3,2,0,1:T(8,128)(2,1)S(1)}, u32[]{:S(2)}, u32[]{:S(2)}) collective-permute-start(bf16[2,2,64,1280]{3,2,0,1:T(8,128)(2,1)S(1)} %fusion.85), channel_id=1, source_target_pairs={{0,1},{1,0},{2,3},{3,2},{4,5},{5,4},{6,7},{7,6},{8,9},{9,8},{10,11... | collective-permute-start | bytes 1966088 | tf_op jit(solution)/shard_map/ppermute | solution.py:196
  306.2 18.5 %collective-permute-start.45 = (bf16[160,2560]{1,0:T(8,128)(2,1)}, bf16[160,2560]{1,0:T(8,128)(2,1)}, u32[]{:S(2)}, u32[]{:S(2)}) collective-permute-start(bf16[160,2560]{1,0:T(8,128)(2,1)} %copy-done.47), channel_id=1, source_target_pairs={{0,8},{8,16},{16,24},{24,28},{28,20},{20,12},{12,4},{4,0},{1,9},{9... | collective-permute-start | bytes 2457608 | tf_op jit(solution)/shard_map/ppermute | solution.py:144
  307.1 17.7 %collective-permute-start.46 = (bf16[160,2560]{1,0:T(8,128)(2,1)}, bf16[160,2560]{1,0:T(8,128)(2,1)}, u32[]{:S(2)}, u32[]{:S(2)}) collective-permute-start(bf16[160,2560]{1,0:T(8,128)(2,1)} %copy-done.47), channel_id=1, source_target_pairs={{8,0},{16,8},{24,16},{28,24},{20,28},{12,20},{4,12},{0,4},{9,1},{1... | collective-permute-start | bytes 2457608 | tf_op jit(solution)/shard_map/ppermute | solution.py:145
  312.9 18.2 %collective-permute-start.43 = (bf16[2,64,1280]{2,1,0:T(8,128)(2,1)S(1)}, bf16[2,64,1280]{2,1,0:T(8,128)(2,1)S(1)}, u32[]{:S(2)}, u32[]{:S(2)}) collective-permute-start(bf16[2,64,1280]{2,1,0:T(8,128)(2,1)S(1)} %multiply_convert_fusion.7), channel_id=1, source_target_pairs={{0,2},{2,0},{1,3},{3,1},{4,6},{6,4},{5,7},{7,5},{8,10},{10,8},{9,1... | collective-permute-start | bytes 983048 | tf_op jit(solution)/shard_map/ppermute | solution.py:175
  314.6 16.5 %collective-permute-start.42 = (bf16[2,64,1280]{2,1,0:T(8,128)(2,1)S(1)}, bf16[2,64,1280]{2,1,0:T(8,128)(2,1)S(1)}, u32[]{:S(2)}, u32[]{:S(2)}) collective-permute-start(bf16[2,64,1280]{2,1,0:T(8,128)(2,1)S(1)} %multiply_convert_fusion.7), channel_id=1, source_target_pairs={{0,1},{1,0},{2,3},{3,2},{4,5},{5,4},{6,7},{7,6},{8,9},{9,8},{10,11... | collective-permute-start | bytes 983048 | tf_op jit(solution)/shard_map/ppermute | solution.py:176
  324.8 17.2 %collective-permute-start.47 = (bf16[160,2560]{1,0:T(8,128)(2,1)}, bf16[160,2560]{1,0:T(8,128)(2,1)}, u32[]{:S(2)}, u32[]{:S(2)}) collective-permute-start(bf16[160,2560]{1,0:T(8,128)(2,1)} %collective-permute-done.45), channel_id=1, source_target_pairs={{0,8},{8,16},{16,24},{24,28},{28,20},{20,12},{12,4},{4,0},{1,9},{9... | collective-permute-start | bytes 2457608 | tf_op jit(solution)/shard_map/ppermute | solution.py:144
  326.3 16.5 %collective-permute-start.48 = (bf16[160,2560]{1,0:T(8,128)(2,1)}, bf16[160,2560]{1,0:T(8,128)(2,1)}, u32[]{:S(2)}, u32[]{:S(2)}) collective-permute-start(bf16[160,2560]{1,0:T(8,128)(2,1)} %collective-permute-done.46), channel_id=1, source_target_pairs={{8,0},{16,8},{24,16},{28,24},{20,28},{12,20},{4,12},{0,4},{9,1},{1... | collective-permute-start | bytes 2457608 | tf_op jit(solution)/shard_map/ppermute | solution.py:145
  342.9 20.9 %collective-permute-start.54 = (bf16[160,2560]{1,0:T(8,128)(2,1)}, bf16[160,2560]{1,0:T(8,128)(2,1)S(1)}, u32[]{:S(2)}, u32[]{:S(2)}) collective-permute-start(bf16[160,2560]{1,0:T(8,128)(2,1)} %collective-permute-done.47), channel_id=1, source_target_pairs={{0,8},{8,16},{16,24},{24,28},{28,20},{20,12},{12,4},{4,0},{1,9},{9... | collective-permute-start | bytes 2457608 | tf_op jit(solution)/shard_map/ppermute | solution.py:144
  344.3 20.5 %collective-permute-start.55 = (bf16[160,2560]{1,0:T(8,128)(2,1)}, bf16[160,2560]{1,0:T(8,128)(2,1)S(1)}, u32[]{:S(2)}, u32[]{:S(2)}) collective-permute-start(bf16[160,2560]{1,0:T(8,128)(2,1)} %collective-permute-done.48), channel_id=1, source_target_pairs={{8,0},{16,8},{24,16},{28,24},{20,28},{12,20},{4,12},{0,4},{9,1},{1... | collective-permute-start | bytes 2457608 | tf_op jit(solution)/shard_map/ppermute | solution.py:145
  349.4 20.1 %collective-permute-start.50 = (bf16[2,64,1280]{2,1,0:T(8,128)(2,1)S(1)}, bf16[2,64,1280]{2,1,0:T(8,128)(2,1)S(1)}, u32[]{:S(2)}, u32[]{:S(2)}) collective-permute-start(bf16[2,64,1280]{2,1,0:T(8,128)(2,1)S(1)} %fusion.113), channel_id=1, source_target_pairs={{0,2},{2,0},{1,3},{3,1},{4,6},{6,4},{5,7},{7,5},{8,10},{10,8},{9,1... | collective-permute-start | bytes 983048 | tf_op jit(solution)/shard_map/ppermute | solution.py:208
  477.1 36.3 %collective-permute-start.85 = (bf16[160,2560]{1,0:T(8,128)(2,1)}, bf16[160,2560]{1,0:T(8,128)(2,1)}, u32[]{:S(2)}, u32[]{:S(2)}) collective-permute-start(bf16[160,2560]{1,0:T(8,128)(2,1)} %pad_maximum_fusion.18), channel_id=1, source_target_pairs={{0,8},{8,16},{16,24},{24,28},{28,20},{20,12},{12,4},{4,0},{1,9},{9... | collective-permute-start | bytes 2457608 | tf_op jit(solution)/shard_map/ppermute | solution.py:144
  478.2 35.2 %collective-permute-start.86 = (bf16[160,2560]{1,0:T(8,128)(2,1)}, bf16[160,2560]{1,0:T(8,128)(2,1)}, u32[]{:S(2)}, u32[]{:S(2)}) collective-permute-start(bf16[160,2560]{1,0:T(8,128)(2,1)} %pad_maximum_fusion.19), channel_id=1, source_target_pairs={{8,0},{16,8},{24,16},{28,24},{20,28},{12,20},{4,12},{0,4},{9,1},{1... | collective-permute-start | bytes 2457608 | tf_op jit(solution)/shard_map/ppermute | solution.py:145
  517.4 20.5 %collective-permute-start.91 = (bf16[160,2560]{1,0:T(8,128)(2,1)}, bf16[160,2560]{1,0:T(8,128)(2,1)}, u32[]{:S(2)}, u32[]{:S(2)}) collective-permute-start(bf16[160,2560]{1,0:T(8,128)(2,1)} %get-tuple-element.334), channel_id=1, source_target_pairs={{0,8},{8,16},{16,24},{24,28},{28,20},{20,12},{12,4},{4,0},{1,9},{9... | collective-permute-start | bytes 2457608 | tf_op jit(solution)/shard_map/ppermute | solution.py:144
  518.5 20.3 %collective-permute-start.92 = (bf16[160,2560]{1,0:T(8,128)(2,1)}, bf16[160,2560]{1,0:T(8,128)(2,1)}, u32[]{:S(2)}, u32[]{:S(2)}) collective-permute-start(bf16[160,2560]{1,0:T(8,128)(2,1)} %get-tuple-element.335), channel_id=1, source_target_pairs={{8,0},{16,8},{24,16},{28,24},{20,28},{12,20},{4,12},{0,4},{9,1},{1... | collective-permute-start | bytes 2457608 | tf_op jit(solution)/shard_map/ppermute | solution.py:145
  525.4 19.2 %collective-permute-start.89 = (bf16[2,64,1280]{2,1,0:T(8,128)(2,1)}, bf16[2,64,1280]{2,1,0:T(8,128)(2,1)S(1)}, u32[]{:S(2)}, u32[]{:S(2)}) collective-permute-start(bf16[2,64,1280]{2,1,0:T(8,128)(2,1)} %get-tuple-element.528), channel_id=1, source_target_pairs={{0,2},{2,0},{1,3},{3,1},{4,6},{6,4},{5,7},{7,5},{8,10},{10,8},{9,1... | collective-permute-start | bytes 983048 | tf_op jit(solution)/shard_map/ppermute | solution.py:175
  525.8 18.8 %collective-permute-start.88 = (bf16[2,64,1280]{2,1,0:T(8,128)(2,1)}, bf16[2,64,1280]{2,1,0:T(8,128)(2,1)S(1)}, u32[]{:S(2)}, u32[]{:S(2)}) collective-permute-start(bf16[2,64,1280]{2,1,0:T(8,128)(2,1)} %get-tuple-element.528), channel_id=1, source_target_pairs={{0,1},{1,0},{2,3},{3,2},{4,5},{5,4},{6,7},{7,6},{8,9},{9,8},{10,11... | collective-permute-start | bytes 983048 | tf_op jit(solution)/shard_map/ppermute | solution.py:176
  542.1 19.4 %collective-permute-start.93 = (bf16[160,2560]{1,0:T(8,128)(2,1)}, bf16[160,2560]{1,0:T(8,128)(2,1)}, u32[]{:S(2)}, u32[]{:S(2)}) collective-permute-start(bf16[160,2560]{1,0:T(8,128)(2,1)} %get-tuple-element.337), channel_id=1, source_target_pairs={{0,8},{8,16},{16,24},{24,28},{28,20},{20,12},{12,4},{4,0},{1,9},{9... | collective-permute-start | bytes 2457608 | tf_op jit(solution)/shard_map/ppermute | solution.py:144
  543.0 19.5 %collective-permute-start.94 = (bf16[160,2560]{1,0:T(8,128)(2,1)}, bf16[160,2560]{1,0:T(8,128)(2,1)}, u32[]{:S(2)}, u32[]{:S(2)}) collective-permute-start(bf16[160,2560]{1,0:T(8,128)(2,1)} %get-tuple-element.338), channel_id=1, source_target_pairs={{8,0},{16,8},{24,16},{28,24},{20,28},{12,20},{4,12},{0,4},{9,1},{1... | collective-permute-start | bytes 2457608 | tf_op jit(solution)/shard_map/ppermute | solution.py:145
  576.5 13.4 %collective-permute-start.102 = (bf16[416,640]{1,0:T(8,128)(2,1)S(1)}, bf16[416,640]{1,0:T(8,128)(2,1)S(1)}, u32[]{:S(2)}, u32[]{:S(2)}) collective-permute-start(bf16[416,640]{1,0:T(8,128)(2,1)S(1)} %fusion.105), channel_id=1, source_target_pairs={{0,8},{8,16},{16,24},{24,28},{28,20},{20,12},{12,4},{4,0},{1,9},{9... | collective-permute-start | bytes 1597448 | tf_op jit(solution)/shard_map/ppermute | solution.py:144
  580.6 13.4 %collective-permute-start.103 = (bf16[416,640]{1,0:T(8,128)(2,1)S(1)}, bf16[416,640]{1,0:T(8,128)(2,1)S(1)}, u32[]{:S(2)}, u32[]{:S(2)}) collective-permute-start(bf16[416,640]{1,0:T(8,128)(2,1)S(1)} %pad_maximum_fusion.37), channel_id=1, source_target_pairs={{8,0},{16,8},{24,16},{28,24},{20,28},{12,20},{4,12},{0,4},{9,1},{1... | collective-permute-start | bytes 1597448 | tf_op jit(solution)/shard_map/ppermute | solution.py:145
  594.9 14.8 %collective-permute-start.104 = (bf16[416,640]{1,0:T(8,128)(2,1)}, bf16[416,640]{1,0:T(8,128)(2,1)}, u32[]{:S(2)}, u32[]{:S(2)}) collective-permute-start(bf16[416,640]{1,0:T(8,128)(2,1)} %add_convert_fusion.3), channel_id=1, source_target_pairs={{0,8},{8,16},{16,24},{24,28},{28,20},{20,12},{12,4},{4,0},{1,9},{9... | collective-permute-start | bytes 1597448 | tf_op jit(solution)/shard_map/ppermute | solution.py:144
  596.7 14.7 %collective-permute-start.105 = (bf16[416,640]{1,0:T(8,128)(2,1)}, bf16[416,640]{1,0:T(8,128)(2,1)}, u32[]{:S(2)}, u32[]{:S(2)}) collective-permute-start(bf16[416,640]{1,0:T(8,128)(2,1)} %add_convert_fusion.2), channel_id=1, source_target_pairs={{8,0},{16,8},{24,16},{28,24},{20,28},{12,20},{4,12},{0,4},{9,1},{1... | collective-permute-start | bytes 1597448 | tf_op jit(solution)/shard_map/ppermute | solution.py:145
  600.4 14.2 %collective-permute-start.101 = (bf16[2,64,1280]{2,1,0:T(8,128)(2,1)}, bf16[2,64,1280]{2,1,0:T(8,128)(2,1)S(1)}, u32[]{:S(2)}, u32[]{:S(2)}) collective-permute-start(bf16[2,64,1280]{2,1,0:T(8,128)(2,1)} %collective-permute-done.100), channel_id=1, source_target_pairs={{0,1},{1,0},{2,3},{3,2},{4,5},{5,4},{6,7},{7,6},{8,9},{9,8},{10,11... | collective-permute-start | bytes 983048 | tf_op jit(solution)/shard_map/ppermute | solution.py:177
  612.6 22.8 %collective-permute-start.106 = (bf16[416,640]{1,0:T(8,128)(2,1)S(1)}, bf16[416,640]{1,0:T(8,128)(2,1)S(1)}, u32[]{:S(2)}, u32[]{:S(2)}) collective-permute-start(bf16[416,640]{1,0:T(8,128)(2,1)S(1)} %add_convert_fusion.1), channel_id=1, source_target_pairs={{0,8},{8,16},{16,24},{24,28},{28,20},{20,12},{12,4},{4,0},{1,9},{9... | collective-permute-start | bytes 1597448 | tf_op jit(solution)/shard_map/ppermute | solution.py:144
  613.4 22.0 %collective-permute-start.107 = (bf16[416,640]{1,0:T(8,128)(2,1)S(1)}, bf16[416,640]{1,0:T(8,128)(2,1)S(1)}, u32[]{:S(2)}, u32[]{:S(2)}) collective-permute-start(bf16[416,640]{1,0:T(8,128)(2,1)S(1)} %add_convert_fusion), channel_id=1, source_target_pairs={{8,0},{16,8},{24,16},{28,24},{20,28},{12,20},{4,12},{0,4},{9,1},{1... | collective-permute-start | bytes 1597448 | tf_op jit(solution)/shard_map/ppermute | solution.py:145
  695.5 20.2 %collective-permute-start.120 = (bf16[160,2880]{1,0:T(8,128)(2,1)S(1)}, bf16[160,2880]{1,0:T(8,128)(2,1)S(1)}, u32[]{:S(2)}, u32[]{:S(2)}) collective-permute-start(bf16[160,2880]{1,0:T(8,128)(2,1)S(1)} %pad_maximum_fusion.14), channel_id=1, source_target_pairs={{0,8},{8,16},{16,24},{24,28},{28,20},{20,12},{12,4},{4,0},{1,9},{9... | collective-permute-start | bytes 2764808 | tf_op jit(solution)/shard_map/ppermute | solution.py:144
  697.5 18.5 %collective-permute-start.121 = (bf16[160,2880]{1,0:T(8,128)(2,1)S(1)}, bf16[160,2880]{1,0:T(8,128)(2,1)S(1)}, u32[]{:S(2)}, u32[]{:S(2)}) collective-permute-start(bf16[160,2880]{1,0:T(8,128)(2,1)S(1)} %pad_maximum_fusion.15), channel_id=1, source_target_pairs={{8,0},{16,8},{24,16},{28,24},{20,28},{12,20},{4,12},{0,4},{9,1},{1... | collective-permute-start | bytes 2764808 | tf_op jit(solution)/shard_map/ppermute | solution.py:145
  697.6 22.8 %collective-permute-start.112 = (bf16[2,2,64,1280]{3,2,1,0:T(8,128)(2,1)S(1)}, bf16[2,2,64,1280]{3,2,1,0:T(8,128)(2,1)S(1)}, u32[]{:S(2)}, u32[]{:S(2)}) collective-permute-start(bf16[2,2,64,1280]{3,2,1,0:T(8,128)(2,1)S(1)} %fusion.83), channel_id=1, source_target_pairs={{0,1},{1,0},{2,3},{3,2},{4,5},{5,4},{6,7},{7,6},{8,9},{9,8},{10,11... | collective-permute-start | bytes 1966088 | tf_op jit(solution)/shard_map/ppermute | solution.py:196
  716.5 19.2 %collective-permute-start.122 = (bf16[160,2880]{1,0:T(8,128)(2,1)S(1)}, bf16[160,2880]{1,0:T(8,128)(2,1)S(1)}, u32[]{:S(2)}, u32[]{:S(2)}) collective-permute-start(bf16[160,2880]{1,0:T(8,128)(2,1)S(1)} %get-tuple-element.379), channel_id=1, source_target_pairs={{0,8},{8,16},{16,24},{24,28},{28,20},{20,12},{12,4},{4,0},{1,9},{9... | collective-permute-start | bytes 2764808 | tf_op jit(solution)/shard_map/ppermute | solution.py:144
  719.0 17.1 %collective-permute-start.123 = (bf16[160,2880]{1,0:T(8,128)(2,1)S(1)}, bf16[160,2880]{1,0:T(8,128)(2,1)S(1)}, u32[]{:S(2)}, u32[]{:S(2)}) collective-permute-start(bf16[160,2880]{1,0:T(8,128)(2,1)S(1)} %get-tuple-element.380), channel_id=1, source_target_pairs={{8,0},{16,8},{24,16},{28,24},{20,28},{12,20},{4,12},{0,4},{9,1},{1... | collective-permute-start | bytes 2764808 | tf_op jit(solution)/shard_map/ppermute | solution.py:145
  720.6 19.2 %collective-permute-start.115 = (bf16[2,64,1280]{2,1,0:T(8,128)(2,1)S(1)}, bf16[2,64,1280]{2,1,0:T(8,128)(2,1)S(1)}, u32[]{:S(2)}, u32[]{:S(2)}) collective-permute-start(bf16[2,64,1280]{2,1,0:T(8,128)(2,1)S(1)} %fusion.117), channel_id=1, source_target_pairs={{0,2},{2,0},{1,3},{3,1},{4,6},{6,4},{5,7},{7,5},{8,10},{10,8},{9,1... | collective-permute-start | bytes 983048 | tf_op jit(solution)/shard_map/ppermute | solution.py:208
  737.8 14.4 %collective-permute-start.125 = (bf16[160,2880]{1,0:T(8,128)(2,1)}, bf16[160,2880]{1,0:T(8,128)(2,1)}, u32[]{:S(2)}, u32[]{:S(2)}) collective-permute-start(bf16[160,2880]{1,0:T(8,128)(2,1)} %get-tuple-element.382), channel_id=1, source_target_pairs={{0,8},{8,16},{16,24},{24,28},{28,20},{20,12},{12,4},{4,0},{1,9},{9... | collective-permute-start | bytes 2764808 | tf_op jit(solution)/shard_map/ppermute | solution.py:144
  739.4 14.0 %collective-permute-start.126 = (bf16[160,2880]{1,0:T(8,128)(2,1)}, bf16[160,2880]{1,0:T(8,128)(2,1)}, u32[]{:S(2)}, u32[]{:S(2)}) collective-permute-start(bf16[160,2880]{1,0:T(8,128)(2,1)} %get-tuple-element.383), channel_id=1, source_target_pairs={{8,0},{16,8},{24,16},{28,24},{20,28},{12,20},{4,12},{0,4},{9,1},{1... | collective-permute-start | bytes 2764808 | tf_op jit(solution)/shard_map/ppermute | solution.py:145
  762.0 13.5 %all-to-all-start.4 = ((f32[32,1,800]{2,1,0:T(1,128)}), f32[32,1,800]{2,1,0:T(1,128)S(1)}, u32[]{:S(2)}, u32[]{:S(2)}) async-start(f32[32,1,800]{2,1,0:T(1,128)} %reshape.903), calls=%async_computation.4 | async-start | bytes 229376 | tf_op jit(solution)/shard_map/all_to_all | solution.py:759
  769.6 21.8 %collective-permute-start.131 = (bf16[160,2880]{1,0:T(8,128)(2,1)}, bf16[160,2880]{1,0:T(8,128)(2,1)}, u32[]{:S(2)}, u32[]{:S(2)}) collective-permute-start(bf16[160,2880]{1,0:T(8,128)(2,1)} %pad_maximum_fusion.17), channel_id=1, source_target_pairs={{8,0},{16,8},{24,16},{28,24},{20,28},{12,20},{4,12},{0,4},{9,1},{1... | collective-permute-start | bytes 2764808 | tf_op jit(solution)/shard_map/ppermute | solution.py:145
  770.0 23.1 %collective-permute-start.130 = (bf16[160,2880]{1,0:T(8,128)(2,1)}, bf16[160,2880]{1,0:T(8,128)(2,1)}, u32[]{:S(2)}, u32[]{:S(2)}) collective-permute-start(bf16[160,2880]{1,0:T(8,128)(2,1)} %pad_maximum_fusion.16), channel_id=1, source_target_pairs={{0,8},{8,16},{16,24},{24,28},{28,20},{20,12},{12,4},{4,0},{1,9},{9... | collective-permute-start | bytes 2764808 | tf_op jit(solution)/shard_map/ppermute | solution.py:144
  780.5 18.2 %collective-permute-start.124 = (bf16[2,2,64,1280]{3,2,0,1:T(8,128)(2,1)S(1)}, bf16[2,2,64,1280]{3,2,0,1:T(8,128)(2,1)S(1)}, u32[]{:S(2)}, u32[]{:S(2)}) collective-permute-start(bf16[2,2,64,1280]{3,2,0,1:T(8,128)(2,1)S(1)} %fusion.90), channel_id=1, source_target_pairs={{0,1},{1,0},{2,3},{3,2},{4,5},{5,4},{6,7},{7,6},{8,9},{9,8},{10,11... | collective-permute-start | bytes 1966088 | tf_op jit(solution)/shard_map/ppermute | solution.py:196
  795.5 21.7 %collective-permute-start.133 = (bf16[160,2880]{1,0:T(8,128)(2,1)S(1)}, bf16[160,2880]{1,0:T(8,128)(2,1)S(1)}, u32[]{:S(2)}, u32[]{:S(2)}) collective-permute-start(bf16[160,2880]{1,0:T(8,128)(2,1)S(1)} %get-tuple-element.392), channel_id=1, source_target_pairs={{8,0},{16,8},{24,16},{28,24},{20,28},{12,20},{4,12},{0,4},{9,1},{1... | collective-permute-start | bytes 2764808 | tf_op jit(solution)/shard_map/ppermute | solution.py:145
  797.1 21.3 %collective-permute-start.132 = (bf16[160,2880]{1,0:T(8,128)(2,1)S(1)}, bf16[160,2880]{1,0:T(8,128)(2,1)S(1)}, u32[]{:S(2)}, u32[]{:S(2)}) collective-permute-start(bf16[160,2880]{1,0:T(8,128)(2,1)S(1)} %get-tuple-element.391), channel_id=1, source_target_pairs={{0,8},{8,16},{16,24},{24,28},{28,20},{20,12},{12,4},{4,0},{1,9},{9... | collective-permute-start | bytes 2764808 | tf_op jit(solution)/shard_map/ppermute | solution.py:144
  798.9 25.1 %collective-permute-start.127 = (bf16[2,64,1280]{2,1,0:T(8,128)(2,1)S(1)}, bf16[2,64,1280]{2,1,0:T(8,128)(2,1)S(1)}, u32[]{:S(2)}, u32[]{:S(2)}) collective-permute-start(bf16[2,64,1280]{2,1,0:T(8,128)(2,1)S(1)} %fusion.118), channel_id=1, source_target_pairs={{0,2},{2,0},{1,3},{3,1},{4,6},{6,4},{5,7},{7,5},{8,10},{10,8},{9,1... | collective-permute-start | bytes 983048 | tf_op jit(solution)/shard_map/ppermute | solution.py:208
  820.3 20.4 %collective-permute-start.135 = (bf16[160,2880]{1,0:T(8,128)(2,1)S(1)}, bf16[160,2880]{1,0:T(8,128)(2,1)S(1)}, u32[]{:S(2)}, u32[]{:S(2)}) collective-permute-start(bf16[160,2880]{1,0:T(8,128)(2,1)S(1)} %get-tuple-element.394), channel_id=1, source_target_pairs={{8,0},{16,8},{24,16},{28,24},{20,28},{12,20},{4,12},{0,4},{9,1},{1... | collective-permute-start | bytes 2764808 | tf_op jit(solution)/shard_map/ppermute | solution.py:145
  821.9 20.1 %collective-permute-start.134 = (bf16[160,2880]{1,0:T(8,128)(2,1)S(1)}, bf16[160,2880]{1,0:T(8,128)(2,1)S(1)}, u32[]{:S(2)}, u32[]{:S(2)}) collective-permute-start(bf16[160,2880]{1,0:T(8,128)(2,1)S(1)} %get-tuple-element.393), channel_id=1, source_target_pairs={{0,8},{8,16},{16,24},{24,28},{28,20},{20,12},{12,4},{4,0},{1,9},{9... | collective-permute-start | bytes 2764808 | tf_op jit(solution)/shard_map/ppermute | solution.py:144
  (237 other events, 2927.3 us)

commit v4 on v3

--- a/solution.py
+++ b/solution.py
@@ -714,7 +714,9 @@
     first_near = sum_near(product_back(middle_taps, w_in), slot_count)
     first_near = ring.hold(first_near)
     s_self.step()
-    s_in = Scattered(ring, weight_grad(first_all, middle_taps))
+    in_grad = weight_grad(first_all, middle_taps)
+    cut = in_grad.shape[1] // 256 * 128
+    s_in = Scattered(ring, in_grad[:, :cut])
     first_grad = sum_far(first_near)
     first_grad, hidden, middle_grad = ring.hold(first_grad, hidden, middle_grad)
     s_out.step()
@@ -734,42 +736,56 @@
     grouped_grad = scaling_in * (hat_in - (in_a + standard_in * in_b))
     latent_grad = ((resnet_grad + grouped_grad) * keep).astype(bf16)
 
-    time_sum = jnp.sum(middle_grad.astype(f32), axis=1)
-    time_sum_all = share_small(time_sum, "dp").reshape(-1, own_channels)
+    latent_grad, in_gain_part, middle_grad, hidden = ring.hold(
+        latent_grad, in_gain_part, middle_grad, hidden
+    )
+    s_out.step()
+    s_out.step()
+    in_gain_part, middle_grad, hidden = ring.hold(in_gain_part, middle_grad, hidden)
+    other = Ring()
+    other.last = ring.last
+    s_rest = Scattered(other, in_grad[:, cut:])
+    s_in.step()
+    s_rest.step()
+
+    mid_gain_whole = lax.dynamic_update_slice_in_dim(
+        jnp.zeros((channels,), f32), mid_gain_part, channel_start, 0
+    )
+    gain_parts = jnp.stack(
+        [in_gain_part, mid_gain_whole, grad_gain_self, grad_gain_cross, grad_gain_feed]
+    )
+    gain_parts = jnp.swapaxes(gain_parts.reshape(5, dp_size, share), 0, 1)
+    gain_parts = jnp.broadcast_to(gain_parts[:, None], (dp_size, mp_size, 5, share))
+    time_sum = jnp.sum(middle_grad.astype(f32), axis=1).reshape(1, -1)
+    payload = jnp.concatenate(
+        [
+            gain_parts.reshape(dp_size * mp_size, 5 * share),
+            jnp.broadcast_to(time_sum, (dp_size * mp_size, time_sum.shape[1])),
+        ],
+        axis=1,
+    )
+    payload = lax.all_to_all(payload, ("dp", "mp"), 0, 0, tiled=True)
+    gain_sums = payload[:, : 5 * share].sum(0).reshape(5, share)
+    time_sum_all = payload[:, 5 * share :].reshape(dp_size, mp_size, -1)
+    time_sum_all = lax.dynamic_index_in_dim(time_sum_all, mp_index, 1, keepdims=False)
     grad_time = jnp.einsum(
         "sa,sb->ab",
         time_act.astype(f32),
-        time_sum_all,
+        time_sum_all.reshape(-1, own_channels),
         precision=highest,
         preferred_element_type=f32,
     )
-    latent_grad, grad_time, in_gain_part, hidden = ring.hold(
-        latent_grad, grad_time, in_gain_part, hidden
-    )
-    s_out.step()
-
-    mid_gain_whole = lax.dynamic_update_slice_in_dim(
-        jnp.zeros((channels,), f32), mid_gain_part, channel_start, 0
-    )
-    gain_parts = jnp.stack(
-        [in_gain_part, mid_gain_whole, grad_gain_self, grad_gain_cross, grad_gain_feed]
-    )
-    gain_parts = jnp.swapaxes(gain_parts.reshape(5, dp_size, share), 0, 1)
-    gain_parts = jnp.broadcast_to(gain_parts[:, None], (dp_size, mp_size, 5, share))
-    gain_sums = lax.all_to_all(
-        gain_parts.reshape(dp_size * mp_size, 5, share), ("dp", "mp"), 0, 0, tiled=True
-    ).sum(0)
-    gain_sums, hidden = ring.hold(gain_sums, hidden)
-    s_out.step()
+    gain_sums, grad_time, hidden = ring.hold(gain_sums, grad_time, hidden)
+    s_in.step()
+    s_rest.step()
     output_near = sum_near(product_back(hidden, w_down), slot_count)
-    output_near = ring.hold(output_near)
     s_in.step()
+    s_rest.step()
     output = ((after_cross + sum_far(output_near)) * keep).astype(bf16)
-    output = ring.hold(output)
     s_in.step()
-    s_in.step()
-    s_in.step()
-    sum_in, sum_out, sum_self = s_in.part, s_out.part, s_self.part
+    s_rest.step()
+    sum_in = jnp.concatenate([s_in.part, s_rest.part], axis=1)
+    sum_out, sum_self = s_out.part, s_self.part
     sum_feed, sum_down = s_feed.part, s_down.part
     text_share = cross_key.shape[0]
     sum_text, sum_cross = s_cross.part[:text_share], s_cross.part[text_share:]

time: 858 us -> 854 us (level)
  waiting for transfers between devices: 337 us -> 326 us
    ppermute x48 -> x52, starting transfers between devices: 44.2 us -> 56.3 us  [step(): lax.ppermute(to_left, 'dp', self.left)]
    ppermute x48 -> x52, waiting for transfers between devices: 235 us -> 230 us  [step(): lax.ppermute(to_right, 'dp', self.right)]
    ppermute x48 -> x52, starting transfers between devices: 58.3 us -> 54.5 us  [step(): lax.ppermute(to_right, 'dp', self.right)]
    convert_element_type x12 -> x14, other arithmetic: 20 us -> 16.4 us  [step(): behind = (behind.astype(f32) + self.from_right).astype(bf16)]
    ppermute x48 -> x52, waiting for transfers between devices: 80.5 us -> 77.2 us  [step(): lax.ppermute(to_left, 'dp', self.left)]
  transfers between devices with their start and end apart: 141 -> 148, of which waited for: 83 -> 87; matrix products, arithmetic and copies ran while one was open for 36% -> 36% of each run, Pallas kernels for 0% -> 0%
where the time goes in v4:
time: 854 us; the launch traced here: 845 us
  waiting for transfers between devices  326 us (38%)
  local copies, waits for them, and re-layouts  153 us (18%)
  starting transfers between devices  144 us (17%)
  matrix products  114 us (13%)
  other arithmetic  91 us (11%)
  between operations  10.7 us (1%)
    ppermute x52, waiting for transfers between devices, step(): lax.ppermute(to_right, 'dp', self.right)  230 us
    ppermute x52, waiting for transfers between devices, step(): lax.ppermute(to_left, 'dp', self.left)  77.2 us
    ppermute x52, starting transfers between devices, step(): lax.ppermute(to_left, 'dp', self.left)  56.3 us
    ppermute x52, starting transfers between devices, step(): lax.ppermute(to_right, 'dp', self.right)  54.5 us
    dynamic_update_slice x53, local copies, waits for them, and re-layouts, put(): self.whole = lax.dynamic_update_slice(self.whole, part[None], place)  49.9 us
    dot_general x13, matrix products, product(): return jnp.dot(former, latter, preferred_element_type=f32)  37.6 us
    dot_general x8, matrix products, product_back(): lax.dot_general(former, latter, (((1,), (1,)), ((), ())), preferred_eleme...  31.1 us
    unnamed x365, local copies, waits for them, and re-layouts  29 us
  transfers between devices with their start and end apart: 148, of which 87 were waited for; matrix products, arithmetic and copies ran while one was open for 36% of the time, Pallas kernels for 0%

profile of v4, /device:TPU:0, one launch (start us, length us, event | category | flops | bytes accessed | tf_op | source)
XLA Modules:
  0.0 844.6 jit_solution(6382001757506426429)
XLA Ops:
  2.9 3.1 collective-permute-start
  6.9 6.2 all-to-all-start.1
  18.8 3.6 broadcast.529.clone
  24.9 3.6 broadcast.529.clone.1
  36.7 3.2 all-to-all-start
  47.1 16.5 %collective-permute-done.2 = bf16[160,2880]{1,0:T(8,128)(2,1)} collective-permute-done((bf16[160,2880]{1,0:T(8,128)(2,1)S(1)}, bf16[160,2880]{1,0:T(8,128)(2,1)}, u32[]{:S(2)}, u32[]{:S(2)}) %collective-permute-start.2) | collective-permute-done | bytes 921632 | tf_op jit(solution)/shard_map/ppermute | solution.py:144
  78.5 16.6 %collective-permute-done.7 = bf16[160,2880]{1,0:T(8,128)(2,1)S(1)} collective-permute-done((bf16[160,2880]{1,0:T(8,128)(2,1)}, bf16[160,2880]{1,0:T(8,128)(2,1)S(1)}, u32[]{:S(2)}, u32[]{:S(2)}) %collective-permute-start.7) | collective-permute-done | bytes 921632 | tf_op jit(solution)/shard_map/ppermute | solution.py:144
  100.6 8.1 collective-permute-done.9
  112.0 3.3 all-to-all-start.2
  120.3 9.2 %convolution_convert_fusion.5 = bf16[512,2880]{0,1:T(8,128)(2,1)} fusion(bf16[512,1280]{1,0:T(8,128)(2,1)} %bitcast.913, bf16[1280,2880]{1,0:T(8,128)(2,1)} %bitcast.35), kind=kOutput, calls=%fused_computation.12 | convolution fusion | flops 3776348160 | bytes 11632640 | tf_op jit(solution)/shard_map/dot_general | solution.py:221
  132.1 4.8 collective-permute-done.11
  155.7 3.9 collective-permute-done.13
  169.1 11.9 %collective-permute-done.15 = bf16[160,2880]{1,0:T(8,128)(2,1)S(1)} collective-permute-done((bf16[160,2880]{1,0:T(8,128)(2,1)}, bf16[160,2880]{1,0:T(8,128)(2,1)S(1)}, u32[]{:S(2)}, u32[]{:S(2)}) %collective-permute-start.15) | collective-permute-done | bytes 921632 | tf_op jit(solution)/shard_map/ppermute | solution.py:144
  192.0 2.6 concatenate.217
  207.7 6.7 fusion.239
  216.8 14.1 %collective-permute-done.23 = bf16[160,1920]{1,0:T(8,128)(2,1)} collective-permute-done((bf16[160,1920]{1,0:T(8,128)(2,1)S(1)}, bf16[160,1920]{1,0:T(8,128)(2,1)}, u32[]{:S(2)}, u32[]{:S(2)}) %collective-permute-start.23) | collective-permute-done | bytes 614432 | tf_op jit(solution)/shard_map/ppermute | solution.py:144
  239.2 4.6 collective-permute-done.22
  255.4 2.7 collective-permute-done.30
  292.3 3.4 collective-permute-done.38
  308.1 2.9 collective-permute-done.37
  314.4 10.1 %collective-permute-done.45 = bf16[160,2560]{1,0:T(8,128)(2,1)} collective-permute-done((bf16[160,2560]{1,0:T(8,128)(2,1)}, bf16[160,2560]{1,0:T(8,128)(2,1)}, u32[]{:S(2)}, u32[]{:S(2)}) %collective-permute-start.45) | collective-permute-done | bytes 819232 | tf_op jit(solution)/shard_map/ppermute | solution.py:144
  349.9 13.8 %collective-permute-done.54 = bf16[160,2560]{1,0:T(8,128)(2,1)S(1)} collective-permute-done((bf16[160,2560]{1,0:T(8,128)(2,1)}, bf16[160,2560]{1,0:T(8,128)(2,1)S(1)}, u32[]{:S(2)}, u32[]{:S(2)}) %collective-permute-start.54) | collective-permute-done | bytes 819232 | tf_op jit(solution)/shard_map/ppermute | solution.py:144
  370.3 5.1 collective-permute-done.56
  379.0 7.2 collective-permute-done.58
  389.7 3.5 fusion.240
  393.2 5.7 multiply_convert_fusion.1
  403.2 4.7 collective-permute-done.62
  411.7 5.4 collective-permute-done.64
  424.5 3.6 fusion.241
  430.5 3.8 convolution_convert_fusion.2
  434.3 5.8 collective-permute-done.71
  444.2 5.8 collective-permute-done.75
  454.4 8.0 collective-permute-done.80
  468.9 3.4 collective-permute-done.82
  483.2 3.0 convolution_convert_fusion.16
  493.3 3.2 convolution_convert_fusion.12
  513.8 3.4 fusion.31
  519.3 4.2 collective-permute-done.87
  525.7 12.0 %collective-permute-done.91 = bf16[160,2560]{1,0:T(8,128)(2,1)} collective-permute-done((bf16[160,2560]{1,0:T(8,128)(2,1)}, bf16[160,2560]{1,0:T(8,128)(2,1)}, u32[]{:S(2)}, u32[]{:S(2)}) %collective-permute-start.91) | collective-permute-done | bytes 819232 | tf_op jit(solution)/shard_map/ppermute | solution.py:144
  538.6 3.4 fusion.29
  556.9 4.5 collective-permute-done.93
  570.5 4.6 collective-permute-done.97
  581.7 8.1 collective-permute-done.102
  600.7 8.3 collective-permute-done.104
  615.2 9.4 %convolution_convert_fusion.4 = bf16[512,2880]{0,1:T(8,128)(2,1)S(1)} fusion(bf16[512,1280]{1,0:T(8,128)(2,1)S(1)} %bitcast.927, bf16[1280,2880]{1,0:T(8,128)(2,1)} %bitcast.69), kind=kOutput, calls=%fused_computation.11 | convolution fusion | flops 3776348160 | bytes 11632640 | tf_op jit(solution)/shard_map/dot_general | solution.py:221
  624.5 4.5 convolution_convert_fusion.1
  658.1 2.5 concatenate.265
  660.6 3.8 concatenate.264
  670.2 8.1 fusion.242
  680.7 4.5 convolution_convert_fusion
  693.2 4.2 collective-permute-done.118
  702.0 15.6 %collective-permute-done.120 = bf16[160,2880]{1,0:T(8,128)(2,1)S(1)} collective-permute-done((bf16[160,2880]{1,0:T(8,128)(2,1)S(1)}, bf16[160,2880]{1,0:T(8,128)(2,1)S(1)}, u32[]{:S(2)}, u32[]{:S(2)}) %collective-permute-start.120) | collective-permute-done | bytes 921632 | tf_op jit(solution)/shard_map/ppermute | solution.py:144
  717.6 2.5 collective-permute-done.121
  724.2 14.3 %collective-permute-done.123 = bf16[160,2880]{1,0:T(8,128)(2,1)S(1)} collective-permute-done((bf16[160,2880]{1,0:T(8,128)(2,1)S(1)}, bf16[160,2880]{1,0:T(8,128)(2,1)S(1)}, u32[]{:S(2)}, u32[]{:S(2)}) %collective-permute-start.123) | collective-permute-done | bytes 921632 | tf_op jit(solution)/shard_map/ppermute | solution.py:145
  743.4 6.0 all-reduce
  750.9 7.2 collective-permute-done.124
  760.1 3.4 all-to-all-start.3
  770.4 3.4 collective-permute-done.126
  786.1 4.0 fusion.243
  796.8 5.5 collective-permute-done.139
  809.0 3.0 collective-permute-done.133
  815.8 6.7 collective-permute-done.141
  827.2 5.0 collective-permute-done.135
  834.1 7.0 collective-permute-done.143
  (1055 shorter events, 441.4 us)
Async XLA Ops:
  2.9 31.2 %collective-permute-start = (bf16[160,2880]{1,0:T(8,128)(2,1)S(1)}, bf16[160,2880]{1,0:T(8,128)(2,1)S(1)}, u32[]{:S(2)}, u32[]{:S(2)}) collective-permute-start(bf16[160,2880]{1,0:T(8,128)(2,1)S(1)} %concatenate.209), channel_id=1, source_target_pairs={{0,8},{8,16},{16,24},{24,28},{28,20},{20,12},{12,4},{4,0},{1,9},{9... | collective-permute-start | bytes 2764808 | tf_op jit(solution)/shard_map/ppermute | solution.py:144
  5.9 28.1 %collective-permute-start.1 = (bf16[160,2880]{1,0:T(8,128)(2,1)S(1)}, bf16[160,2880]{1,0:T(8,128)(2,1)}, u32[]{:S(2)}, u32[]{:S(2)}) collective-permute-start(bf16[160,2880]{1,0:T(8,128)(2,1)S(1)} %concatenate.209), channel_id=1, source_target_pairs={{8,0},{16,8},{24,16},{28,24},{20,28},{12,20},{4,12},{0,4},{9,1},{1... | collective-permute-start | bytes 2764808 | tf_op jit(solution)/shard_map/ppermute | solution.py:145
  6.9 27.1 %all-to-all-start.1 = ((f32[8,1,802]{2,1,0:T(1,128)}), f32[8,1,802]{2,1,0:T(1,128)S(1)}, u32[]{:S(2)}, u32[]{:S(2)}) async-start(f32[8,1,802]{2,1,0:T(1,128)} %broadcast_in_dim.341), calls=%async_computation.1 | async-start | bytes 57344 | tf_op jit(solution)/shard_map/all_to_all | solution.py:159
  40.0 23.7 %collective-permute-start.2 = (bf16[160,2880]{1,0:T(8,128)(2,1)S(1)}, bf16[160,2880]{1,0:T(8,128)(2,1)}, u32[]{:S(2)}, u32[]{:S(2)}) collective-permute-start(bf16[160,2880]{1,0:T(8,128)(2,1)S(1)} %collective-permute-done), channel_id=1, source_target_pairs={{0,8},{8,16},{16,24},{24,28},{28,20},{20,12},{12,4},{4,0},{1,9},{9... | collective-permute-start | bytes 2764808 | tf_op jit(solution)/shard_map/ppermute | solution.py:144
  42.1 23.1 %collective-permute-start.3 = (bf16[160,2880]{1,0:T(8,128)(2,1)}, bf16[160,2880]{1,0:T(8,128)(2,1)S(1)}, u32[]{:S(2)}, u32[]{:S(2)}) collective-permute-start(bf16[160,2880]{1,0:T(8,128)(2,1)} %collective-permute-done.1), channel_id=1, source_target_pairs={{8,0},{16,8},{24,16},{28,24},{20,28},{12,20},{4,12},{0,4},{9,1},{1... | collective-permute-start | bytes 2764808 | tf_op jit(solution)/shard_map/ppermute | solution.py:145
  71.6 23.5 %collective-permute-start.7 = (bf16[160,2880]{1,0:T(8,128)(2,1)}, bf16[160,2880]{1,0:T(8,128)(2,1)S(1)}, u32[]{:S(2)}, u32[]{:S(2)}) collective-permute-start(bf16[160,2880]{1,0:T(8,128)(2,1)} %collective-permute-done.2), channel_id=1, source_target_pairs={{0,8},{8,16},{16,24},{24,28},{28,20},{20,12},{12,4},{4,0},{1,9},{9... | collective-permute-start | bytes 2764808 | tf_op jit(solution)/shard_map/ppermute | solution.py:144
  73.2 23.2 %collective-permute-start.8 = (bf16[160,2880]{1,0:T(8,128)(2,1)}, bf16[160,2880]{1,0:T(8,128)(2,1)S(1)}, u32[]{:S(2)}, u32[]{:S(2)}) collective-permute-start(bf16[160,2880]{1,0:T(8,128)(2,1)} %copy-done.76), channel_id=1, source_target_pairs={{8,0},{16,8},{24,16},{28,24},{20,28},{12,20},{4,12},{0,4},{9,1},{1... | collective-permute-start | bytes 2764808 | tf_op jit(solution)/shard_map/ppermute | solution.py:145
  112.0 20.1 %all-to-all-start.2 = ((f32[8,2,320]{2,1,0:T(2,128)}), f32[8,2,320]{2,1,0:T(2,128)S(1)}, u32[]{:S(2)}, u32[]{:S(2)}) async-start(f32[8,2,320]{2,1,0:T(2,128)} %reshape.857), calls=%async_computation.2 | async-start | bytes 49152 | tf_op jit(solution)/shard_map/all_to_all | solution.py:527
  115.3 21.6 %collective-permute-start.11 = (bf16[160,2880]{1,0:T(8,128)(2,1)}, bf16[160,2880]{1,0:T(8,128)(2,1)}, u32[]{:S(2)}, u32[]{:S(2)}) collective-permute-start(bf16[160,2880]{1,0:T(8,128)(2,1)} %copy-done.32), channel_id=1, source_target_pairs={{0,8},{8,16},{16,24},{24,28},{28,20},{20,12},{12,4},{4,0},{1,9},{9... | collective-permute-start | bytes 2764808 | tf_op jit(solution)/shard_map/ppermute | solution.py:144
  117.3 21.2 %collective-permute-start.12 = (bf16[160,2880]{1,0:T(8,128)(2,1)}, bf16[160,2880]{1,0:T(8,128)(2,1)}, u32[]{:S(2)}, u32[]{:S(2)}) collective-permute-start(bf16[160,2880]{1,0:T(8,128)(2,1)} %copy-done.32), channel_id=1, source_target_pairs={{8,0},{16,8},{24,16},{28,24},{20,28},{12,20},{4,12},{0,4},{9,1},{1... | collective-permute-start | bytes 2764808 | tf_op jit(solution)/shard_map/ppermute | solution.py:145
  139.5 20.1 %collective-permute-start.13 = (bf16[160,2880]{1,0:T(8,128)(2,1)}, bf16[160,2880]{1,0:T(8,128)(2,1)}, u32[]{:S(2)}, u32[]{:S(2)}) collective-permute-start(bf16[160,2880]{1,0:T(8,128)(2,1)} %collective-permute-done.11), channel_id=1, source_target_pairs={{0,8},{8,16},{16,24},{24,28},{28,20},{20,12},{12,4},{4,0},{1,9},{9... | collective-permute-start | bytes 2764808 | tf_op jit(solution)/shard_map/ppermute | solution.py:144
  141.0 19.8 %collective-permute-start.14 = (bf16[160,2880]{1,0:T(8,128)(2,1)}, bf16[160,2880]{1,0:T(8,128)(2,1)}, u32[]{:S(2)}, u32[]{:S(2)}) collective-permute-start(bf16[160,2880]{1,0:T(8,128)(2,1)} %collective-permute-done.12), channel_id=1, source_target_pairs={{8,0},{16,8},{24,16},{28,24},{20,28},{12,20},{4,12},{0,4},{9,1},{1... | collective-permute-start | bytes 2764808 | tf_op jit(solution)/shard_map/ppermute | solution.py:145
  162.2 18.8 %collective-permute-start.15 = (bf16[160,2880]{1,0:T(8,128)(2,1)}, bf16[160,2880]{1,0:T(8,128)(2,1)S(1)}, u32[]{:S(2)}, u32[]{:S(2)}) collective-permute-start(bf16[160,2880]{1,0:T(8,128)(2,1)} %collective-permute-done.13), channel_id=1, source_target_pairs={{0,8},{8,16},{16,24},{24,28},{28,20},{20,12},{12,4},{4,0},{1,9},{9... | collective-permute-start | bytes 2764808 | tf_op jit(solution)/shard_map/ppermute | solution.py:144
  163.6 18.4 %collective-permute-start.16 = (bf16[160,2880]{1,0:T(8,128)(2,1)}, bf16[160,2880]{1,0:T(8,128)(2,1)S(1)}, u32[]{:S(2)}, u32[]{:S(2)}) collective-permute-start(bf16[160,2880]{1,0:T(8,128)(2,1)} %collective-permute-done.14), channel_id=1, source_target_pairs={{8,0},{16,8},{24,16},{28,24},{20,28},{12,20},{4,12},{0,4},{9,1},{1... | collective-permute-start | bytes 2764808 | tf_op jit(solution)/shard_map/ppermute | solution.py:145
  214.5 20.6 %collective-permute-start.21 = (bf16[2,2,64,1280]{3,2,0,1:T(8,128)(2,1)S(1)}, bf16[2,2,64,1280]{3,2,0,1:T(8,128)(2,1)S(1)}, u32[]{:S(2)}, u32[]{:S(2)}) collective-permute-start(bf16[2,2,64,1280]{3,2,0,1:T(8,128)(2,1)S(1)} %fusion.87), channel_id=1, source_target_pairs={{0,1},{1,0},{2,3},{3,2},{4,5},{5,4},{6,7},{7,6},{8,9},{9,8},{10,11... | collective-permute-start | bytes 1966088 | tf_op jit(solution)/shard_map/ppermute | solution.py:196
  214.6 16.4 %collective-permute-start.23 = (bf16[160,1920]{1,0:T(8,128)(2,1)S(1)}, bf16[160,1920]{1,0:T(8,128)(2,1)}, u32[]{:S(2)}, u32[]{:S(2)}) collective-permute-start(bf16[160,1920]{1,0:T(8,128)(2,1)S(1)} %collective-permute-done.19), channel_id=1, source_target_pairs={{0,8},{8,16},{16,24},{24,28},{28,20},{20,12},{12,4},{4,0},{1,9},{9... | collective-permute-start | bytes 1843208 | tf_op jit(solution)/shard_map/ppermute | solution.py:144
  215.9 16.0 %collective-permute-start.24 = (bf16[160,1920]{1,0:T(8,128)(2,1)S(1)}, bf16[160,1920]{1,0:T(8,128)(2,1)}, u32[]{:S(2)}, u32[]{:S(2)}) collective-permute-start(bf16[160,1920]{1,0:T(8,128)(2,1)S(1)} %collective-permute-done.20), channel_id=1, source_target_pairs={{8,0},{16,8},{24,16},{28,24},{20,28},{12,20},{4,12},{0,4},{9,1},{1... | collective-permute-start | bytes 1843208 | tf_op jit(solution)/shard_map/ppermute | solution.py:145
  231.9 15.3 %collective-permute-start.28 = (bf16[160,1920]{1,0:T(8,128)(2,1)}, bf16[160,1920]{1,0:T(8,128)(2,1)S(1)}, u32[]{:S(2)}, u32[]{:S(2)}) collective-permute-start(bf16[160,1920]{1,0:T(8,128)(2,1)} %collective-permute-done.23), channel_id=1, source_target_pairs={{0,8},{8,16},{16,24},{24,28},{28,20},{20,12},{12,4},{4,0},{1,9},{9... | collective-permute-start | bytes 1843208 | tf_op jit(solution)/shard_map/ppermute | solution.py:144
  232.7 15.3 %collective-permute-start.29 = (bf16[160,1920]{1,0:T(8,128)(2,1)}, bf16[160,1920]{1,0:T(8,128)(2,1)S(1)}, u32[]{:S(2)}, u32[]{:S(2)}) collective-permute-start(bf16[160,1920]{1,0:T(8,128)(2,1)} %collective-permute-done.24), channel_id=1, source_target_pairs={{8,0},{16,8},{24,16},{28,24},{20,28},{12,20},{4,12},{0,4},{9,1},{1... | collective-permute-start | bytes 1843208 | tf_op jit(solution)/shard_map/ppermute | solution.py:145
  264.3 19.6 %collective-permute-start.52 = (bf16[2,64,1280]{2,1,0:T(8,128)(2,1)S(1)}, bf16[2,64,1280]{2,1,0:T(8,128)(2,1)}, u32[]{:S(2)}, u32[]{:S(2)}) collective-permute-start(bf16[2,64,1280]{2,1,0:T(8,128)(2,1)S(1)} %fusion.102), channel_id=1, source_target_pairs={{0,2},{2,0},{1,3},{3,1},{4,6},{6,4},{5,7},{7,5},{8,10},{10,8},{9,1... | collective-permute-start | bytes 983048 | tf_op jit(solution)/shard_map/ppermute | solution.py:175
  266.0 18.0 %collective-permute-start.51 = (bf16[2,64,1280]{2,1,0:T(8,128)(2,1)S(1)}, bf16[2,64,1280]{2,1,0:T(8,128)(2,1)}, u32[]{:S(2)}, u32[]{:S(2)}) collective-permute-start(bf16[2,64,1280]{2,1,0:T(8,128)(2,1)S(1)} %fusion.102), channel_id=1, source_target_pairs={{0,1},{1,0},{2,3},{3,2},{4,5},{5,4},{6,7},{7,6},{8,9},{9,8},{10,11... | collective-permute-start | bytes 983048 | tf_op jit(solution)/shard_map/ppermute | solution.py:176
  285.3 16.9 %collective-permute-start.36 = (bf16[2,2,64,1280]{3,2,0,1:T(8,128)(2,1)S(1)}, bf16[2,2,64,1280]{3,2,0,1:T(8,128)(2,1)S(1)}, u32[]{:S(2)}, u32[]{:S(2)}) collective-permute-start(bf16[2,2,64,1280]{3,2,0,1:T(8,128)(2,1)S(1)} %fusion.88), channel_id=1, source_target_pairs={{0,1},{1,0},{2,3},{3,2},{4,5},{5,4},{6,7},{7,6},{8,9},{9,8},{10,11... | collective-permute-start | bytes 1966088 | tf_op jit(solution)/shard_map/ppermute | solution.py:196
  306.0 18.5 %collective-permute-start.45 = (bf16[160,2560]{1,0:T(8,128)(2,1)}, bf16[160,2560]{1,0:T(8,128)(2,1)}, u32[]{:S(2)}, u32[]{:S(2)}) collective-permute-start(bf16[160,2560]{1,0:T(8,128)(2,1)} %copy-done.45), channel_id=1, source_target_pairs={{0,8},{8,16},{16,24},{24,28},{28,20},{20,12},{12,4},{4,0},{1,9},{9... | collective-permute-start | bytes 2457608 | tf_op jit(solution)/shard_map/ppermute | solution.py:144
  307.0 17.7 %collective-permute-start.46 = (bf16[160,2560]{1,0:T(8,128)(2,1)}, bf16[160,2560]{1,0:T(8,128)(2,1)}, u32[]{:S(2)}, u32[]{:S(2)}) collective-permute-start(bf16[160,2560]{1,0:T(8,128)(2,1)} %copy-done.45), channel_id=1, source_target_pairs={{8,0},{16,8},{24,16},{28,24},{20,28},{12,20},{4,12},{0,4},{9,1},{1... | collective-permute-start | bytes 2457608 | tf_op jit(solution)/shard_map/ppermute | solution.py:145
  312.7 18.3 %collective-permute-start.43 = (bf16[2,64,1280]{2,1,0:T(8,128)(2,1)S(1)}, bf16[2,64,1280]{2,1,0:T(8,128)(2,1)S(1)}, u32[]{:S(2)}, u32[]{:S(2)}) collective-permute-start(bf16[2,64,1280]{2,1,0:T(8,128)(2,1)S(1)} %multiply_convert_fusion.7), channel_id=1, source_target_pairs={{0,2},{2,0},{1,3},{3,1},{4,6},{6,4},{5,7},{7,5},{8,10},{10,8},{9,1... | collective-permute-start | bytes 983048 | tf_op jit(solution)/shard_map/ppermute | solution.py:175
  314.4 16.6 %collective-permute-start.42 = (bf16[2,64,1280]{2,1,0:T(8,128)(2,1)S(1)}, bf16[2,64,1280]{2,1,0:T(8,128)(2,1)S(1)}, u32[]{:S(2)}, u32[]{:S(2)}) collective-permute-start(bf16[2,64,1280]{2,1,0:T(8,128)(2,1)S(1)} %multiply_convert_fusion.7), channel_id=1, source_target_pairs={{0,1},{1,0},{2,3},{3,2},{4,5},{5,4},{6,7},{7,6},{8,9},{9,8},{10,11... | collective-permute-start | bytes 983048 | tf_op jit(solution)/shard_map/ppermute | solution.py:176
  324.7 17.1 %collective-permute-start.47 = (bf16[160,2560]{1,0:T(8,128)(2,1)}, bf16[160,2560]{1,0:T(8,128)(2,1)}, u32[]{:S(2)}, u32[]{:S(2)}) collective-permute-start(bf16[160,2560]{1,0:T(8,128)(2,1)} %collective-permute-done.45), channel_id=1, source_target_pairs={{0,8},{8,16},{16,24},{24,28},{28,20},{20,12},{12,4},{4,0},{1,9},{9... | collective-permute-start | bytes 2457608 | tf_op jit(solution)/shard_map/ppermute | solution.py:144
  326.2 16.5 %collective-permute-start.48 = (bf16[160,2560]{1,0:T(8,128)(2,1)}, bf16[160,2560]{1,0:T(8,128)(2,1)}, u32[]{:S(2)}, u32[]{:S(2)}) collective-permute-start(bf16[160,2560]{1,0:T(8,128)(2,1)} %collective-permute-done.46), channel_id=1, source_target_pairs={{8,0},{16,8},{24,16},{28,24},{20,28},{12,20},{4,12},{0,4},{9,1},{1... | collective-permute-start | bytes 2457608 | tf_op jit(solution)/shard_map/ppermute | solution.py:145
  342.8 20.9 %collective-permute-start.54 = (bf16[160,2560]{1,0:T(8,128)(2,1)}, bf16[160,2560]{1,0:T(8,128)(2,1)S(1)}, u32[]{:S(2)}, u32[]{:S(2)}) collective-permute-start(bf16[160,2560]{1,0:T(8,128)(2,1)} %collective-permute-done.47), channel_id=1, source_target_pairs={{0,8},{8,16},{16,24},{24,28},{28,20},{20,12},{12,4},{4,0},{1,9},{9... | collective-permute-start | bytes 2457608 | tf_op jit(solution)/shard_map/ppermute | solution.py:144
  344.1 20.5 %collective-permute-start.55 = (bf16[160,2560]{1,0:T(8,128)(2,1)}, bf16[160,2560]{1,0:T(8,128)(2,1)S(1)}, u32[]{:S(2)}, u32[]{:S(2)}) collective-permute-start(bf16[160,2560]{1,0:T(8,128)(2,1)} %collective-permute-done.48), channel_id=1, source_target_pairs={{8,0},{16,8},{24,16},{28,24},{20,28},{12,20},{4,12},{0,4},{9,1},{1... | collective-permute-start | bytes 2457608 | tf_op jit(solution)/shard_map/ppermute | solution.py:145
  349.3 20.0 %collective-permute-start.50 = (bf16[2,64,1280]{2,1,0:T(8,128)(2,1)S(1)}, bf16[2,64,1280]{2,1,0:T(8,128)(2,1)S(1)}, u32[]{:S(2)}, u32[]{:S(2)}) collective-permute-start(bf16[2,64,1280]{2,1,0:T(8,128)(2,1)S(1)} %fusion.120), channel_id=1, source_target_pairs={{0,2},{2,0},{1,3},{3,1},{4,6},{6,4},{5,7},{7,5},{8,10},{10,8},{9,1... | collective-permute-start | bytes 983048 | tf_op jit(solution)/shard_map/ppermute | solution.py:208
  477.0 36.3 %collective-permute-start.85 = (bf16[160,2560]{1,0:T(8,128)(2,1)}, bf16[160,2560]{1,0:T(8,128)(2,1)}, u32[]{:S(2)}, u32[]{:S(2)}) collective-permute-start(bf16[160,2560]{1,0:T(8,128)(2,1)} %pad_maximum_fusion.16), channel_id=1, source_target_pairs={{0,8},{8,16},{16,24},{24,28},{28,20},{20,12},{12,4},{4,0},{1,9},{9... | collective-permute-start | bytes 2457608 | tf_op jit(solution)/shard_map/ppermute | solution.py:144
  478.1 35.2 %collective-permute-start.86 = (bf16[160,2560]{1,0:T(8,128)(2,1)}, bf16[160,2560]{1,0:T(8,128)(2,1)}, u32[]{:S(2)}, u32[]{:S(2)}) collective-permute-start(bf16[160,2560]{1,0:T(8,128)(2,1)} %pad_maximum_fusion.17), channel_id=1, source_target_pairs={{8,0},{16,8},{24,16},{28,24},{20,28},{12,20},{4,12},{0,4},{9,1},{1... | collective-permute-start | bytes 2457608 | tf_op jit(solution)/shard_map/ppermute | solution.py:145
  517.2 20.5 %collective-permute-start.91 = (bf16[160,2560]{1,0:T(8,128)(2,1)}, bf16[160,2560]{1,0:T(8,128)(2,1)}, u32[]{:S(2)}, u32[]{:S(2)}) collective-permute-start(bf16[160,2560]{1,0:T(8,128)(2,1)} %get-tuple-element.344), channel_id=1, source_target_pairs={{0,8},{8,16},{16,24},{24,28},{28,20},{20,12},{12,4},{4,0},{1,9},{9... | collective-permute-start | bytes 2457608 | tf_op jit(solution)/shard_map/ppermute | solution.py:144
  518.3 20.3 %collective-permute-start.92 = (bf16[160,2560]{1,0:T(8,128)(2,1)}, bf16[160,2560]{1,0:T(8,128)(2,1)}, u32[]{:S(2)}, u32[]{:S(2)}) collective-permute-start(bf16[160,2560]{1,0:T(8,128)(2,1)} %get-tuple-element.345), channel_id=1, source_target_pairs={{8,0},{16,8},{24,16},{28,24},{20,28},{12,20},{4,12},{0,4},{9,1},{1... | collective-permute-start | bytes 2457608 | tf_op jit(solution)/shard_map/ppermute | solution.py:145
  525.3 19.1 %collective-permute-start.89 = (bf16[2,64,1280]{2,1,0:T(8,128)(2,1)}, bf16[2,64,1280]{2,1,0:T(8,128)(2,1)S(1)}, u32[]{:S(2)}, u32[]{:S(2)}) collective-permute-start(bf16[2,64,1280]{2,1,0:T(8,128)(2,1)} %get-tuple-element.548), channel_id=1, source_target_pairs={{0,2},{2,0},{1,3},{3,1},{4,6},{6,4},{5,7},{7,5},{8,10},{10,8},{9,1... | collective-permute-start | bytes 983048 | tf_op jit(solution)/shard_map/ppermute | solution.py:175
  525.7 18.8 %collective-permute-start.88 = (bf16[2,64,1280]{2,1,0:T(8,128)(2,1)}, bf16[2,64,1280]{2,1,0:T(8,128)(2,1)S(1)}, u32[]{:S(2)}, u32[]{:S(2)}) collective-permute-start(bf16[2,64,1280]{2,1,0:T(8,128)(2,1)} %get-tuple-element.548), channel_id=1, source_target_pairs={{0,1},{1,0},{2,3},{3,2},{4,5},{5,4},{6,7},{7,6},{8,9},{9,8},{10,11... | collective-permute-start | bytes 983048 | tf_op jit(solution)/shard_map/ppermute | solution.py:176
  542.0 19.4 %collective-permute-start.93 = (bf16[160,2560]{1,0:T(8,128)(2,1)}, bf16[160,2560]{1,0:T(8,128)(2,1)}, u32[]{:S(2)}, u32[]{:S(2)}) collective-permute-start(bf16[160,2560]{1,0:T(8,128)(2,1)} %get-tuple-element.347), channel_id=1, source_target_pairs={{0,8},{8,16},{16,24},{24,28},{28,20},{20,12},{12,4},{4,0},{1,9},{9... | collective-permute-start | bytes 2457608 | tf_op jit(solution)/shard_map/ppermute | solution.py:144
  542.9 19.5 %collective-permute-start.94 = (bf16[160,2560]{1,0:T(8,128)(2,1)}, bf16[160,2560]{1,0:T(8,128)(2,1)}, u32[]{:S(2)}, u32[]{:S(2)}) collective-permute-start(bf16[160,2560]{1,0:T(8,128)(2,1)} %get-tuple-element.348), channel_id=1, source_target_pairs={{8,0},{16,8},{24,16},{28,24},{20,28},{12,20},{4,12},{0,4},{9,1},{1... | collective-permute-start | bytes 2457608 | tf_op jit(solution)/shard_map/ppermute | solution.py:145
  594.1 14.8 %collective-permute-start.104 = (bf16[416,640]{1,0:T(8,128)(2,1)}, bf16[416,640]{1,0:T(8,128)(2,1)}, u32[]{:S(2)}, u32[]{:S(2)}) collective-permute-start(bf16[416,640]{1,0:T(8,128)(2,1)} %add_convert_fusion.3), channel_id=1, source_target_pairs={{0,8},{8,16},{16,24},{24,28},{28,20},{20,12},{12,4},{4,0},{1,9},{9... | collective-permute-start | bytes 1597448 | tf_op jit(solution)/shard_map/ppermute | solution.py:144
  595.9 14.6 %collective-permute-start.105 = (bf16[416,640]{1,0:T(8,128)(2,1)}, bf16[416,640]{1,0:T(8,128)(2,1)}, u32[]{:S(2)}, u32[]{:S(2)}) collective-permute-start(bf16[416,640]{1,0:T(8,128)(2,1)} %add_convert_fusion.2), channel_id=1, source_target_pairs={{8,0},{16,8},{24,16},{28,24},{20,28},{12,20},{4,12},{0,4},{9,1},{1... | collective-permute-start | bytes 1597448 | tf_op jit(solution)/shard_map/ppermute | solution.py:145
  611.7 22.8 %collective-permute-start.106 = (bf16[416,640]{1,0:T(8,128)(2,1)S(1)}, bf16[416,640]{1,0:T(8,128)(2,1)S(1)}, u32[]{:S(2)}, u32[]{:S(2)}) collective-permute-start(bf16[416,640]{1,0:T(8,128)(2,1)S(1)} %add_convert_fusion.1), channel_id=1, source_target_pairs={{0,8},{8,16},{16,24},{24,28},{28,20},{20,12},{12,4},{4,0},{1,9},{9... | collective-permute-start | bytes 1597448 | tf_op jit(solution)/shard_map/ppermute | solution.py:144
  612.6 21.9 %collective-permute-start.107 = (bf16[416,640]{1,0:T(8,128)(2,1)S(1)}, bf16[416,640]{1,0:T(8,128)(2,1)S(1)}, u32[]{:S(2)}, u32[]{:S(2)}) collective-permute-start(bf16[416,640]{1,0:T(8,128)(2,1)S(1)} %add_convert_fusion), channel_id=1, source_target_pairs={{8,0},{16,8},{24,16},{28,24},{20,28},{12,20},{4,12},{0,4},{9,1},{1... | collective-permute-start | bytes 1597448 | tf_op jit(solution)/shard_map/ppermute | solution.py:145
  698.5 19.1 %collective-permute-start.120 = (bf16[160,2880]{1,0:T(8,128)(2,1)S(1)}, bf16[160,2880]{1,0:T(8,128)(2,1)S(1)}, u32[]{:S(2)}, u32[]{:S(2)}) collective-permute-start(bf16[160,2880]{1,0:T(8,128)(2,1)S(1)} %pad_maximum_fusion.14), channel_id=1, source_target_pairs={{0,8},{8,16},{16,24},{24,28},{28,20},{20,12},{12,4},{4,0},{1,9},{9... | collective-permute-start | bytes 2764808 | tf_op jit(solution)/shard_map/ppermute | solution.py:144
  699.7 20.5 %collective-permute-start.121 = (bf16[160,2880]{1,0:T(8,128)(2,1)S(1)}, bf16[160,2880]{1,0:T(8,128)(2,1)S(1)}, u32[]{:S(2)}, u32[]{:S(2)}) collective-permute-start(bf16[160,2880]{1,0:T(8,128)(2,1)S(1)} %pad_maximum_fusion.15), channel_id=1, source_target_pairs={{8,0},{16,8},{24,16},{28,24},{20,28},{12,20},{4,12},{0,4},{9,1},{1... | collective-permute-start | bytes 2764808 | tf_op jit(solution)/shard_map/ppermute | solution.py:145
  701.7 22.4 %collective-permute-start.115 = (bf16[2,64,1280]{2,1,0:T(8,128)(2,1)S(1)}, bf16[2,64,1280]{2,1,0:T(8,128)(2,1)S(1)}, u32[]{:S(2)}, u32[]{:S(2)}) collective-permute-start(bf16[2,64,1280]{2,1,0:T(8,128)(2,1)S(1)} %fusion.124), channel_id=1, source_target_pairs={{0,2},{2,0},{1,3},{3,1},{4,6},{6,4},{5,7},{7,5},{8,10},{10,8},{9,1... | collective-permute-start | bytes 983048 | tf_op jit(solution)/shard_map/ppermute | solution.py:208
  720.6 17.9 %collective-permute-start.123 = (bf16[160,2880]{1,0:T(8,128)(2,1)S(1)}, bf16[160,2880]{1,0:T(8,128)(2,1)S(1)}, u32[]{:S(2)}, u32[]{:S(2)}) collective-permute-start(bf16[160,2880]{1,0:T(8,128)(2,1)S(1)} %get-tuple-element.391), channel_id=1, source_target_pairs={{8,0},{16,8},{24,16},{28,24},{20,28},{12,20},{4,12},{0,4},{9,1},{1... | collective-permute-start | bytes 2764808 | tf_op jit(solution)/shard_map/ppermute | solution.py:145
  721.6 17.1 %collective-permute-start.122 = (bf16[160,2880]{1,0:T(8,128)(2,1)S(1)}, bf16[160,2880]{1,0:T(8,128)(2,1)S(1)}, u32[]{:S(2)}, u32[]{:S(2)}) collective-permute-start(bf16[160,2880]{1,0:T(8,128)(2,1)S(1)} %get-tuple-element.390), channel_id=1, source_target_pairs={{0,8},{8,16},{16,24},{24,28},{28,20},{20,12},{12,4},{4,0},{1,9},{9... | collective-permute-start | bytes 2764808 | tf_op jit(solution)/shard_map/ppermute | solution.py:144
  740.4 17.7 %collective-permute-start.124 = (bf16[160,2880]{1,0:T(8,128)(2,1)}, bf16[160,2880]{1,0:T(8,128)(2,1)}, u32[]{:S(2)}, u32[]{:S(2)}) collective-permute-start(bf16[160,2880]{1,0:T(8,128)(2,1)} %get-tuple-element.392), channel_id=1, source_target_pairs={{0,8},{8,16},{16,24},{24,28},{28,20},{20,12},{12,4},{4,0},{1,9},{9... | collective-permute-start | bytes 2764808 | tf_op jit(solution)/shard_map/ppermute | solution.py:144
  741.9 16.7 %collective-permute-start.125 = (bf16[160,2880]{1,0:T(8,128)(2,1)}, bf16[160,2880]{1,0:T(8,128)(2,1)}, u32[]{:S(2)}, u32[]{:S(2)}) collective-permute-start(bf16[160,2880]{1,0:T(8,128)(2,1)} %get-tuple-element.393), channel_id=1, source_target_pairs={{8,0},{16,8},{24,16},{28,24},{20,28},{12,20},{4,12},{0,4},{9,1},{1... | collective-permute-start | bytes 2764808 | tf_op jit(solution)/shard_map/ppermute | solution.py:145
  760.1 24.4 %all-to-all-start.3 = ((f32[32,1,1440]{2,1,0:T(1,128)}), f32[32,1,1440]{2,1,0:T(1,128)S(1)}, u32[]{:S(2)}, u32[]{:S(2)}) async-start(f32[32,1,1440]{2,1,0:T(1,128)} %copy.294), calls=%async_computation.3 | async-start | bytes 393216 | tf_op jit(solution)/shard_map/all_to_all | solution.py:767
  765.6 14.7 %collective-permute-start.137 = (bf16[80,1472]{1,0:T(8,128)(2,1)}, bf16[80,1472]{1,0:T(8,128)(2,1)S(1)}, u32[]{:S(2)}, u32[]{:S(2)}) collective-permute-start(bf16[80,1472]{1,0:T(8,128)(2,1)} %get-tuple-element.408), channel_id=1, source_target_pairs={{8,0},{16,8},{24,16},{28,24},{20,28},{12,20},{4,12},{0,4},{9,1},{1... | collective-permute-start | bytes 706568 | tf_op jit(solution)/shard_map/ppermute | solution.py:145
  782.5 19.8 %collective-permute-start.139 = (bf16[160,1472]{1,0:T(8,128)(2,1)}, bf16[160,1472]{1,0:T(8,128)(2,1)S(1)}, u32[]{:S(2)}, u32[]{:S(2)}) collective-permute-start(bf16[160,1472]{1,0:T(8,128)(2,1)} %pad_maximum_fusion.37), channel_id=1, source_target_pairs={{8,0},{16,8},{24,16},{28,24},{20,28},{12,20},{4,12},{0,4},{9,1},{1... | collective-permute-start | bytes 1413128 | tf_op jit(solution)/shard_map/ppermute | solution.py:145
  783.9 20.0 %collective-permute-start.138 = (bf16[160,1472]{1,0:T(8,128)(2,1)S(1)}, bf16[160,1472]{1,0:T(8,128)(2,1)}, u32[]{:S(2)}, u32[]{:S(2)}) collective-permute-start(bf16[160,1472]{1,0:T(8,128)(2,1)S(1)} %pad_maximum_fusion.36), channel_id=1, source_target_pairs={{0,8},{8,16},{16,24},{24,28},{28,20},{20,12},{12,4},{4,0},{1,9},{9... | collective-permute-start | bytes 1413128 | tf_op jit(solution)/shard_map/ppermute | solution.py:144
  790.1 17.1 %collective-permute-start.128 = (bf16[2,2,64,1280]{3,2,0,1:T(8,128)(2,1)S(1)}, bf16[2,2,64,1280]{3,2,0,1:T(8,128)(2,1)S(1)}, u32[]{:S(2)}, u32[]{:S(2)}) collective-permute-start(bf16[2,2,64,1280]{3,2,0,1:T(8,128)(2,1)S(1)} %fusion.93), channel_id=1, source_target_pairs={{0,1},{1,0},{2,3},{3,2},{4,5},{5,4},{6,7},{7,6},{8,9},{9,8},{10,11... | collective-permute-start | bytes 1966088 | tf_op jit(solution)/shard_map/ppermute | solution.py:196
  794.8 17.2 %collective-permute-start.133 = (bf16[160,1408]{1,0:T(8,128)(2,1)S(1)}, bf16[160,1408]{1,0:T(8,128)(2,1)S(1)}, u32[]{:S(2)}, u32[]{:S(2)}) collective-permute-start(bf16[160,1408]{1,0:T(8,128)(2,1)S(1)} %get-tuple-element.404), channel_id=1, source_target_pairs={{8,0},{16,8},{24,16},{28,24},{20,28},{12,20},{4,12},{0,4},{9,1},{1... | collective-permute-start | bytes 1351688 | tf_op jit(solution)/shard_map/ppermute | solution.py:145
  796.8 16.6 %collective-permute-start.132 = (bf16[160,1408]{1,0:T(8,128)(2,1)S(1)}, bf16[160,1408]{1,0:T(8,128)(2,1)S(1)}, u32[]{:S(2)}, u32[]{:S(2)}) collective-permute-start(bf16[160,1408]{1,0:T(8,128)(2,1)S(1)} %get-tuple-element.403), channel_id=1, source_target_pairs={{0,8},{8,16},{16,24},{24,28},{28,20},{20,12},{12,4},{4,0},{1,9},{9... | collective-permute-start | bytes 1351688 | tf_op jit(solution)/shard_map/ppermute | solution.py:144
  805.2 17.3 %collective-permute-start.141 = (bf16[160,1472]{1,0:T(8,128)(2,1)S(1)}, bf16[160,1472]{1,0:T(8,128)(2,1)S(1)}, u32[]{:S(2)}, u32[]{:S(2)}) collective-permute-start(bf16[160,1472]{1,0:T(8,128)(2,1)S(1)} %get-tuple-element.412), channel_id=1, source_target_pairs={{8,0},{16,8},{24,16},{28,24},{20,28},{12,20},{4,12},{0,4},{9,1},{1... | collective-permute-start | bytes 1413128 | tf_op jit(solution)/shard_map/ppermute | solution.py:145
  807.3 16.7 %collective-permute-start.140 = (bf16[160,1472]{1,0:T(8,128)(2,1)S(1)}, bf16[160,1472]{1,0:T(8,128)(2,1)S(1)}, u32[]{:S(2)}, u32[]{:S(2)}) collective-permute-start(bf16[160,1472]{1,0:T(8,128)(2,1)S(1)} %get-tuple-element.411), channel_id=1, source_target_pairs={{0,8},{8,16},{16,24},{24,28},{28,20},{20,12},{12,4},{4,0},{1,9},{9... | collective-permute-start | bytes 1413128 | tf_op jit(solution)/shard_map/ppermute | solution.py:144
  807.5 18.9 %collective-permute-start.129 = (bf16[2,64,1280]{2,1,0:T(8,128)(2,1)S(1)}, bf16[2,64,1280]{2,1,0:T(8,128)(2,1)S(1)}, u32[]{:S(2)}, u32[]{:S(2)}) collective-permute-start(bf16[2,64,1280]{2,1,0:T(8,128)(2,1)S(1)} %fusion.125), channel_id=1, source_target_pairs={{0,2},{2,0},{1,3},{3,1},{4,6},{6,4},{5,7},{7,5},{8,10},{10,8},{9,1... | collective-permute-start | bytes 983048 | tf_op jit(solution)/shard_map/ppermute | solution.py:208
  813.7 18.5 %collective-permute-start.135 = (bf16[160,1408]{1,0:T(8,128)(2,1)S(1)}, bf16[160,1408]{1,0:T(8,128)(2,1)S(1)}, u32[]{:S(2)}, u32[]{:S(2)}) collective-permute-start(bf16[160,1408]{1,0:T(8,128)(2,1)S(1)} %get-tuple-element.406), channel_id=1, source_target_pairs={{8,0},{16,8},{24,16},{28,24},{20,28},{12,20},{4,12},{0,4},{9,1},{1... | collective-permute-start | bytes 1351688 | tf_op jit(solution)/shard_map/ppermute | solution.py:145
  815.8 17.8 %collective-permute-start.134 = (bf16[160,1408]{1,0:T(8,128)(2,1)S(1)}, bf16[160,1408]{1,0:T(8,128)(2,1)S(1)}, u32[]{:S(2)}, u32[]{:S(2)}) collective-permute-start(bf16[160,1408]{1,0:T(8,128)(2,1)S(1)} %get-tuple-element.405), channel_id=1, source_target_pairs={{0,8},{8,16},{16,24},{24,28},{28,20},{20,12},{12,4},{4,0},{1,9},{9... | collective-permute-start | bytes 1351688 | tf_op jit(solution)/shard_map/ppermute | solution.py:144
  824.3 16.9 %collective-permute-start.143 = (bf16[160,1472]{1,0:T(8,128)(2,1)S(1)}, bf16[160,1472]{1,0:T(8,128)(2,1)S(1)}, u32[]{:S(2)}, u32[]{:S(2)}) collective-permute-start(bf16[160,1472]{1,0:T(8,128)(2,1)S(1)} %get-tuple-element.414), channel_id=1, source_target_pairs={{8,0},{16,8},{24,16},{28,24},{20,28},{12,20},{4,12},{0,4},{9,1},{1... | collective-permute-start | bytes 1413128 | tf_op jit(solution)/shard_map/ppermute | solution.py:145
  826.3 16.0 %collective-permute-start.142 = (bf16[160,1472]{1,0:T(8,128)(2,1)S(1)}, bf16[160,1472]{1,0:T(8,128)(2,1)S(1)}, u32[]{:S(2)}, u32[]{:S(2)}) collective-permute-start(bf16[160,1472]{1,0:T(8,128)(2,1)S(1)} %get-tuple-element.413), channel_id=1, source_target_pairs={{0,8},{8,16},{16,24},{24,28},{28,20},{20,12},{12,4},{4,0},{1,9},{9... | collective-permute-start | bytes 1413128 | tf_op jit(solution)/shard_map/ppermute | solution.py:144
  (245 other events, 2339.2 us)

commit v5 on v4

--- a/solution.py
+++ b/solution.py
@@ -571,8 +571,8 @@
     co_full = w_self[:, 5 * own_channels :]
     g_text.step()
     qkv = product(attend_all, qkv_full).astype(bf16)
-    qkv = rows3(ring.hold(qkv))
     g_text.step()
+    qkv = rows3(qkv)
     query_rows, key_rows, value_rows = jnp.split(qkv, 3, axis=2)
     mixture, self_chances = attend(query_rows, key_rows, value_rows, key_valid)
     self_part = product_back(flat(mixture), so_full)

time: 854 us -> 871 us (1.020)
  starting transfers between devices: 144 us -> 160 us
    ppermute x52, starting transfers between devices: 56.3 us -> 66.1 us  [step(): lax.ppermute(to_left, 'dp', self.left)]
  transfers between devices with their start and end apart: 148 -> 148, of which waited for: 87 -> 88; matrix products, arithmetic and copies ran while one was open for 36% -> 35% of each run, Pallas kernels for 0% -> 0%
where the time goes in v5:
time: 871 us; the launch traced here: 861 us
  waiting for transfers between devices  328 us (38%)
  starting transfers between devices  160 us (18%)
  local copies, waits for them, and re-layouts  151 us (17%)
  matrix products  114 us (13%)
  other arithmetic  91.8 us (11%)
  between operations  10.7 us (1%)
    ppermute x52, waiting for transfers between devices, step(): lax.ppermute(to_right, 'dp', self.right)  228 us
    ppermute x52, waiting for transfers between devices, step(): lax.ppermute(to_left, 'dp', self.left)  79.5 us
    ppermute x52, starting transfers between devices, step(): lax.ppermute(to_left, 'dp', self.left)  66.1 us
    ppermute x52, starting transfers between devices, step(): lax.ppermute(to_right, 'dp', self.right)  56.1 us
    dynamic_update_slice x53, local copies, waits for them, and re-layouts, put(): self.whole = lax.dynamic_update_slice(self.whole, part[None], place)  48 us
    dot_general x13, matrix products, product(): return jnp.dot(former, latter, preferred_element_type=f32)  37.6 us
    dot_general x8, matrix products, product_back(): lax.dot_general(former, latter, (((1,), (1,)), ((), ())), preferred_eleme...  31.2 us
    unnamed x365, local copies, waits for them, and re-layouts  28.8 us
  transfers between devices with their start and end apart: 148, of which 88 were waited for; matrix products, arithmetic and copies ran while one was open for 35% of the time, Pallas kernels for 0%

profile of v5, /device:TPU:0, one launch (start us, length us, event | category | flops | bytes accessed | tf_op | source)
XLA Modules:
  0.0 861.4 jit_solution(2109497367734116614)
XLA Ops:
  2.9 3.1 collective-permute-start
  6.9 6.2 all-to-all-start.1
  18.8 3.6 broadcast.529.clone
  24.9 3.6 broadcast.529.clone.1
  36.7 3.2 all-to-all-start
  47.1 16.5 %collective-permute-done.2 = bf16[160,2880]{1,0:T(8,128)(2,1)} collective-permute-done((bf16[160,2880]{1,0:T(8,128)(2,1)S(1)}, bf16[160,2880]{1,0:T(8,128)(2,1)}, u32[]{:S(2)}, u32[]{:S(2)}) %collective-permute-start.2) | collective-permute-done | bytes 921632 | tf_op jit(solution)/shard_map/ppermute | solution.py:144
  78.5 16.6 %collective-permute-done.7 = bf16[160,2880]{1,0:T(8,128)(2,1)S(1)} collective-permute-done((bf16[160,2880]{1,0:T(8,128)(2,1)}, bf16[160,2880]{1,0:T(8,128)(2,1)S(1)}, u32[]{:S(2)}, u32[]{:S(2)}) %collective-permute-start.7) | collective-permute-done | bytes 921632 | tf_op jit(solution)/shard_map/ppermute | solution.py:144
  100.6 8.1 collective-permute-done.9
  112.0 3.3 all-to-all-start.2
  120.3 9.2 %convolution_convert_fusion.5 = bf16[512,2880]{0,1:T(8,128)(2,1)} fusion(bf16[512,1280]{1,0:T(8,128)(2,1)} %bitcast.913, bf16[1280,2880]{1,0:T(8,128)(2,1)} %bitcast.35), kind=kOutput, calls=%fused_computation.12 | convolution fusion | flops 3776348160 | bytes 11632640 | tf_op jit(solution)/shard_map/dot_general | solution.py:221
  132.1 4.8 collective-permute-done.11
  155.8 3.9 collective-permute-done.13
  169.1 11.9 %collective-permute-done.15 = bf16[160,2880]{1,0:T(8,128)(2,1)S(1)} collective-permute-done((bf16[160,2880]{1,0:T(8,128)(2,1)}, bf16[160,2880]{1,0:T(8,128)(2,1)S(1)}, u32[]{:S(2)}, u32[]{:S(2)}) %collective-permute-start.15) | collective-permute-done | bytes 921632 | tf_op jit(solution)/shard_map/ppermute | solution.py:144
  192.1 2.6 concatenate.217
  202.9 12.5 %collective-permute-start.20 = (bf16[160,1920]{1,0:T(8,128)(2,1)S(1)}, bf16[160,1920]{1,0:T(8,128)(2,1)S(1)}, u32[]{:S(2)}, u32[]{:S(2)}) collective-permute-start(bf16[160,1920]{1,0:T(8,128)(2,1)S(1)} %concatenate.220), channel_id=1, source_target_pairs={{8,0},{16,8},{24,16},{28,24},{20,28},{12,20},{4,12},{0,4},{9,1},{1... | collective-permute-start | bytes 1843208 | tf_op jit(solution)/shard_map/ppermute | solution.py:145
  219.0 6.7 fusion.239
  228.1 14.1 %collective-permute-done.23 = bf16[160,1920]{1,0:T(8,128)(2,1)} collective-permute-done((bf16[160,1920]{1,0:T(8,128)(2,1)S(1)}, bf16[160,1920]{1,0:T(8,128)(2,1)}, u32[]{:S(2)}, u32[]{:S(2)}) %collective-permute-start.23) | collective-permute-done | bytes 614432 | tf_op jit(solution)/shard_map/ppermute | solution.py:144
  250.5 4.5 collective-permute-done.22
  296.0 4.8 collective-permute-done.34
  305.9 5.5 collective-permute-done.38
  322.6 4.4 collective-permute-done.37
  329.2 9.9 %collective-permute-done.45 = bf16[160,2560]{1,0:T(8,128)(2,1)} collective-permute-done((bf16[160,2560]{1,0:T(8,128)(2,1)}, bf16[160,2560]{1,0:T(8,128)(2,1)}, u32[]{:S(2)}, u32[]{:S(2)}) %collective-permute-start.45) | collective-permute-done | bytes 819232 | tf_op jit(solution)/shard_map/ppermute | solution.py:144
  367.1 12.6 %collective-permute-done.54 = bf16[160,2560]{1,0:T(8,128)(2,1)S(1)} collective-permute-done((bf16[160,2560]{1,0:T(8,128)(2,1)}, bf16[160,2560]{1,0:T(8,128)(2,1)S(1)}, u32[]{:S(2)}, u32[]{:S(2)}) %collective-permute-start.54) | collective-permute-done | bytes 819232 | tf_op jit(solution)/shard_map/ppermute | solution.py:144
  387.4 4.1 collective-permute-done.56
  394.8 7.2 collective-permute-done.58
  405.2 3.5 fusion.240
  408.8 5.7 multiply_convert_fusion.1
  419.0 4.7 collective-permute-done.62
  427.5 5.2 collective-permute-done.64
  439.5 3.6 fusion.241
  445.4 3.8 convolution_convert_fusion.2
  449.3 6.1 collective-permute-done.71
  459.9 5.8 collective-permute-done.75
  471.5 6.7 collective-permute-done.80
  499.1 3.0 convolution_convert_fusion.16
  509.2 3.2 convolution_convert_fusion.12
  530.9 3.4 fusion.31
  536.4 2.9 collective-permute-done.87
  542.9 12.0 %collective-permute-done.91 = bf16[160,2560]{1,0:T(8,128)(2,1)} collective-permute-done((bf16[160,2560]{1,0:T(8,128)(2,1)}, bf16[160,2560]{1,0:T(8,128)(2,1)}, u32[]{:S(2)}, u32[]{:S(2)}) %collective-permute-start.91) | collective-permute-done | bytes 819232 | tf_op jit(solution)/shard_map/ppermute | solution.py:144
  555.6 3.4 fusion.29
  573.9 4.5 collective-permute-done.93
  587.5 4.4 collective-permute-done.97
  597.2 9.4 %collective-permute-done.102 = bf16[416,640]{1,0:T(8,128)(2,1)S(1)} collective-permute-done((bf16[416,640]{1,0:T(8,128)(2,1)S(1)}, bf16[416,640]{1,0:T(8,128)(2,1)S(1)}, u32[]{:S(2)}, u32[]{:S(2)}) %collective-permute-start.102) | collective-permute-done | bytes 532512 | tf_op jit(solution)/shard_map/ppermute | solution.py:144
  612.8 3.6 collective-permute-done.100
  617.4 7.0 collective-permute-done.104
  630.6 9.4 %convolution_convert_fusion.4 = bf16[512,2880]{0,1:T(8,128)(2,1)S(1)} fusion(bf16[512,1280]{1,0:T(8,128)(2,1)S(1)} %bitcast.927, bf16[1280,2880]{1,0:T(8,128)(2,1)} %bitcast.69), kind=kOutput, calls=%fused_computation.11 | convolution fusion | flops 3776348160 | bytes 11632640 | tf_op jit(solution)/shard_map/dot_general | solution.py:221
  640.0 4.5 convolution_convert_fusion.1
  676.1 3.8 concatenate.264
  685.7 8.1 fusion.242
  696.1 4.5 convolution_convert_fusion
  708.6 4.3 collective-permute-done.118
  719.3 13.8 %collective-permute-done.120 = bf16[160,2880]{1,0:T(8,128)(2,1)S(1)} collective-permute-done((bf16[160,2880]{1,0:T(8,128)(2,1)S(1)}, bf16[160,2880]{1,0:T(8,128)(2,1)S(1)}, u32[]{:S(2)}, u32[]{:S(2)}) %collective-permute-start.120) | collective-permute-done | bytes 921632 | tf_op jit(solution)/shard_map/ppermute | solution.py:144
  733.1 2.7 collective-permute-done.121
  739.9 14.8 %collective-permute-done.123 = bf16[160,2880]{1,0:T(8,128)(2,1)S(1)} collective-permute-done((bf16[160,2880]{1,0:T(8,128)(2,1)S(1)}, bf16[160,2880]{1,0:T(8,128)(2,1)S(1)}, u32[]{:S(2)}, u32[]{:S(2)}) %collective-permute-start.123) | collective-permute-done | bytes 921632 | tf_op jit(solution)/shard_map/ppermute | solution.py:145
  759.5 6.0 all-reduce
  767.0 6.6 collective-permute-done.124
  776.0 4.4 all-to-all-start.3
  787.2 3.4 collective-permute-done.126
  802.9 4.0 fusion.243
  813.7 5.5 collective-permute-done.139
  825.8 3.0 collective-permute-done.133
  832.6 6.7 collective-permute-done.141
  844.0 5.0 collective-permute-done.135
  850.9 7.0 collective-permute-done.143
  (1055 shorter events, 448.2 us)
Async XLA Ops:
  2.9 31.2 %collective-permute-start = (bf16[160,2880]{1,0:T(8,128)(2,1)S(1)}, bf16[160,2880]{1,0:T(8,128)(2,1)S(1)}, u32[]{:S(2)}, u32[]{:S(2)}) collective-permute-start(bf16[160,2880]{1,0:T(8,128)(2,1)S(1)} %concatenate.209), channel_id=1, source_target_pairs={{0,8},{8,16},{16,24},{24,28},{28,20},{20,12},{12,4},{4,0},{1,9},{9... | collective-permute-start | bytes 2764808 | tf_op jit(solution)/shard_map/ppermute | solution.py:144
  5.9 28.1 %collective-permute-start.1 = (bf16[160,2880]{1,0:T(8,128)(2,1)S(1)}, bf16[160,2880]{1,0:T(8,128)(2,1)}, u32[]{:S(2)}, u32[]{:S(2)}) collective-permute-start(bf16[160,2880]{1,0:T(8,128)(2,1)S(1)} %concatenate.209), channel_id=1, source_target_pairs={{8,0},{16,8},{24,16},{28,24},{20,28},{12,20},{4,12},{0,4},{9,1},{1... | collective-permute-start | bytes 2764808 | tf_op jit(solution)/shard_map/ppermute | solution.py:145
  6.9 27.1 %all-to-all-start.1 = ((f32[8,1,802]{2,1,0:T(1,128)}), f32[8,1,802]{2,1,0:T(1,128)S(1)}, u32[]{:S(2)}, u32[]{:S(2)}) async-start(f32[8,1,802]{2,1,0:T(1,128)} %broadcast_in_dim.341), calls=%async_computation.1 | async-start | bytes 57344 | tf_op jit(solution)/shard_map/all_to_all | solution.py:159
  40.0 23.7 %collective-permute-start.2 = (bf16[160,2880]{1,0:T(8,128)(2,1)S(1)}, bf16[160,2880]{1,0:T(8,128)(2,1)}, u32[]{:S(2)}, u32[]{:S(2)}) collective-permute-start(bf16[160,2880]{1,0:T(8,128)(2,1)S(1)} %collective-permute-done), channel_id=1, source_target_pairs={{0,8},{8,16},{16,24},{24,28},{28,20},{20,12},{12,4},{4,0},{1,9},{9... | collective-permute-start | bytes 2764808 | tf_op jit(solution)/shard_map/ppermute | solution.py:144
  42.1 23.1 %collective-permute-start.3 = (bf16[160,2880]{1,0:T(8,128)(2,1)}, bf16[160,2880]{1,0:T(8,128)(2,1)S(1)}, u32[]{:S(2)}, u32[]{:S(2)}) collective-permute-start(bf16[160,2880]{1,0:T(8,128)(2,1)} %collective-permute-done.1), channel_id=1, source_target_pairs={{8,0},{16,8},{24,16},{28,24},{20,28},{12,20},{4,12},{0,4},{9,1},{1... | collective-permute-start | bytes 2764808 | tf_op jit(solution)/shard_map/ppermute | solution.py:145
  71.6 23.5 %collective-permute-start.7 = (bf16[160,2880]{1,0:T(8,128)(2,1)}, bf16[160,2880]{1,0:T(8,128)(2,1)S(1)}, u32[]{:S(2)}, u32[]{:S(2)}) collective-permute-start(bf16[160,2880]{1,0:T(8,128)(2,1)} %collective-permute-done.2), channel_id=1, source_target_pairs={{0,8},{8,16},{16,24},{24,28},{28,20},{20,12},{12,4},{4,0},{1,9},{9... | collective-permute-start | bytes 2764808 | tf_op jit(solution)/shard_map/ppermute | solution.py:144
  73.2 23.2 %collective-permute-start.8 = (bf16[160,2880]{1,0:T(8,128)(2,1)}, bf16[160,2880]{1,0:T(8,128)(2,1)S(1)}, u32[]{:S(2)}, u32[]{:S(2)}) collective-permute-start(bf16[160,2880]{1,0:T(8,128)(2,1)} %copy-done.76), channel_id=1, source_target_pairs={{8,0},{16,8},{24,16},{28,24},{20,28},{12,20},{4,12},{0,4},{9,1},{1... | collective-permute-start | bytes 2764808 | tf_op jit(solution)/shard_map/ppermute | solution.py:145
  112.0 20.1 %all-to-all-start.2 = ((f32[8,2,320]{2,1,0:T(2,128)}), f32[8,2,320]{2,1,0:T(2,128)S(1)}, u32[]{:S(2)}, u32[]{:S(2)}) async-start(f32[8,2,320]{2,1,0:T(2,128)} %reshape.857), calls=%async_computation.2 | async-start | bytes 49152 | tf_op jit(solution)/shard_map/all_to_all | solution.py:527
  115.3 21.6 %collective-permute-start.11 = (bf16[160,2880]{1,0:T(8,128)(2,1)}, bf16[160,2880]{1,0:T(8,128)(2,1)}, u32[]{:S(2)}, u32[]{:S(2)}) collective-permute-start(bf16[160,2880]{1,0:T(8,128)(2,1)} %copy-done.32), channel_id=1, source_target_pairs={{0,8},{8,16},{16,24},{24,28},{28,20},{20,12},{12,4},{4,0},{1,9},{9... | collective-permute-start | bytes 2764808 | tf_op jit(solution)/shard_map/ppermute | solution.py:144
  117.3 21.2 %collective-permute-start.12 = (bf16[160,2880]{1,0:T(8,128)(2,1)}, bf16[160,2880]{1,0:T(8,128)(2,1)}, u32[]{:S(2)}, u32[]{:S(2)}) collective-permute-start(bf16[160,2880]{1,0:T(8,128)(2,1)} %copy-done.32), channel_id=1, source_target_pairs={{8,0},{16,8},{24,16},{28,24},{20,28},{12,20},{4,12},{0,4},{9,1},{1... | collective-permute-start | bytes 2764808 | tf_op jit(solution)/shard_map/ppermute | solution.py:145
  139.5 20.1 %collective-permute-start.13 = (bf16[160,2880]{1,0:T(8,128)(2,1)}, bf16[160,2880]{1,0:T(8,128)(2,1)}, u32[]{:S(2)}, u32[]{:S(2)}) collective-permute-start(bf16[160,2880]{1,0:T(8,128)(2,1)} %collective-permute-done.11), channel_id=1, source_target_pairs={{0,8},{8,16},{16,24},{24,28},{28,20},{20,12},{12,4},{4,0},{1,9},{9... | collective-permute-start | bytes 2764808 | tf_op jit(solution)/shard_map/ppermute | solution.py:144
  141.1 19.8 %collective-permute-start.14 = (bf16[160,2880]{1,0:T(8,128)(2,1)}, bf16[160,2880]{1,0:T(8,128)(2,1)}, u32[]{:S(2)}, u32[]{:S(2)}) collective-permute-start(bf16[160,2880]{1,0:T(8,128)(2,1)} %collective-permute-done.12), channel_id=1, source_target_pairs={{8,0},{16,8},{24,16},{28,24},{20,28},{12,20},{4,12},{0,4},{9,1},{1... | collective-permute-start | bytes 2764808 | tf_op jit(solution)/shard_map/ppermute | solution.py:145
  162.2 18.8 %collective-permute-start.15 = (bf16[160,2880]{1,0:T(8,128)(2,1)}, bf16[160,2880]{1,0:T(8,128)(2,1)S(1)}, u32[]{:S(2)}, u32[]{:S(2)}) collective-permute-start(bf16[160,2880]{1,0:T(8,128)(2,1)} %collective-permute-done.13), channel_id=1, source_target_pairs={{0,8},{8,16},{16,24},{24,28},{28,20},{20,12},{12,4},{4,0},{1,9},{9... | collective-permute-start | bytes 2764808 | tf_op jit(solution)/shard_map/ppermute | solution.py:144
  163.6 18.4 %collective-permute-start.16 = (bf16[160,2880]{1,0:T(8,128)(2,1)}, bf16[160,2880]{1,0:T(8,128)(2,1)S(1)}, u32[]{:S(2)}, u32[]{:S(2)}) collective-permute-start(bf16[160,2880]{1,0:T(8,128)(2,1)} %collective-permute-done.14), channel_id=1, source_target_pairs={{8,0},{16,8},{24,16},{28,24},{20,28},{12,20},{4,12},{0,4},{9,1},{1... | collective-permute-start | bytes 2764808 | tf_op jit(solution)/shard_map/ppermute | solution.py:145
  201.6 24.0 %collective-permute-start.19 = (bf16[160,1920]{1,0:T(8,128)(2,1)S(1)}, bf16[160,1920]{1,0:T(8,128)(2,1)S(1)}, u32[]{:S(2)}, u32[]{:S(2)}) collective-permute-start(bf16[160,1920]{1,0:T(8,128)(2,1)S(1)} %concatenate.220), channel_id=1, source_target_pairs={{0,8},{8,16},{16,24},{24,28},{28,20},{20,12},{12,4},{4,0},{1,9},{9... | collective-permute-start | bytes 1843208 | tf_op jit(solution)/shard_map/ppermute | solution.py:144
  202.9 22.8 %collective-permute-start.20 = (bf16[160,1920]{1,0:T(8,128)(2,1)S(1)}, bf16[160,1920]{1,0:T(8,128)(2,1)S(1)}, u32[]{:S(2)}, u32[]{:S(2)}) collective-permute-start(bf16[160,1920]{1,0:T(8,128)(2,1)S(1)} %concatenate.220), channel_id=1, source_target_pairs={{8,0},{16,8},{24,16},{28,24},{20,28},{12,20},{4,12},{0,4},{9,1},{1... | collective-permute-start | bytes 1843208 | tf_op jit(solution)/shard_map/ppermute | solution.py:145
  225.8 20.6 %collective-permute-start.21 = (bf16[2,2,64,1280]{3,2,0,1:T(8,128)(2,1)S(1)}, bf16[2,2,64,1280]{3,2,0,1:T(8,128)(2,1)S(1)}, u32[]{:S(2)}, u32[]{:S(2)}) collective-permute-start(bf16[2,2,64,1280]{3,2,0,1:T(8,128)(2,1)S(1)} %fusion.87), channel_id=1, source_target_pairs={{0,1},{1,0},{2,3},{3,2},{4,5},{5,4},{6,7},{7,6},{8,9},{9,8},{10,11... | collective-permute-start | bytes 1966088 | tf_op jit(solution)/shard_map/ppermute | solution.py:196
  225.9 16.4 %collective-permute-start.23 = (bf16[160,1920]{1,0:T(8,128)(2,1)S(1)}, bf16[160,1920]{1,0:T(8,128)(2,1)}, u32[]{:S(2)}, u32[]{:S(2)}) collective-permute-start(bf16[160,1920]{1,0:T(8,128)(2,1)S(1)} %collective-permute-done.19), channel_id=1, source_target_pairs={{0,8},{8,16},{16,24},{24,28},{28,20},{20,12},{12,4},{4,0},{1,9},{9... | collective-permute-start | bytes 1843208 | tf_op jit(solution)/shard_map/ppermute | solution.py:144
  227.2 16.0 %collective-permute-start.24 = (bf16[160,1920]{1,0:T(8,128)(2,1)S(1)}, bf16[160,1920]{1,0:T(8,128)(2,1)}, u32[]{:S(2)}, u32[]{:S(2)}) collective-permute-start(bf16[160,1920]{1,0:T(8,128)(2,1)S(1)} %collective-permute-done.20), channel_id=1, source_target_pairs={{8,0},{16,8},{24,16},{28,24},{20,28},{12,20},{4,12},{0,4},{9,1},{1... | collective-permute-start | bytes 1843208 | tf_op jit(solution)/shard_map/ppermute | solution.py:145
  243.2 15.3 %collective-permute-start.28 = (bf16[160,1920]{1,0:T(8,128)(2,1)}, bf16[160,1920]{1,0:T(8,128)(2,1)S(1)}, u32[]{:S(2)}, u32[]{:S(2)}) collective-permute-start(bf16[160,1920]{1,0:T(8,128)(2,1)} %collective-permute-done.23), channel_id=1, source_target_pairs={{0,8},{8,16},{16,24},{24,28},{28,20},{20,12},{12,4},{4,0},{1,9},{9... | collective-permute-start | bytes 1843208 | tf_op jit(solution)/shard_map/ppermute | solution.py:144
  269.9 20.6 %collective-permute-start.32 = (bf16[256,640]{1,0:T(8,128)(2,1)}, bf16[256,640]{1,0:T(8,128)(2,1)}, u32[]{:S(2)}, u32[]{:S(2)}) collective-permute-start(bf16[256,640]{1,0:T(8,128)(2,1)} %get-tuple-element.287), channel_id=1, source_target_pairs={{0,8},{8,16},{16,24},{24,28},{28,20},{20,12},{12,4},{4,0},{1,9},{9... | collective-permute-start | bytes 983048 | tf_op jit(solution)/shard_map/ppermute | solution.py:144
  270.6 20.0 %collective-permute-start.33 = (bf16[256,640]{1,0:T(8,128)(2,1)}, bf16[256,640]{1,0:T(8,128)(2,1)}, u32[]{:S(2)}, u32[]{:S(2)}) collective-permute-start(bf16[256,640]{1,0:T(8,128)(2,1)} %get-tuple-element.287), channel_id=1, source_target_pairs={{8,0},{16,8},{24,16},{28,24},{20,28},{12,20},{4,12},{0,4},{9,1},{1... | collective-permute-start | bytes 983048 | tf_op jit(solution)/shard_map/ppermute | solution.py:145
  275.6 19.1 %collective-permute-start.52 = (bf16[2,64,1280]{2,1,0:T(8,128)(2,1)S(1)}, bf16[2,64,1280]{2,1,0:T(8,128)(2,1)}, u32[]{:S(2)}, u32[]{:S(2)}) collective-permute-start(bf16[2,64,1280]{2,1,0:T(8,128)(2,1)S(1)} %fusion.102), channel_id=1, source_target_pairs={{0,2},{2,0},{1,3},{3,1},{4,6},{6,4},{5,7},{7,5},{8,10},{10,8},{9,1... | collective-permute-start | bytes 983048 | tf_op jit(solution)/shard_map/ppermute | solution.py:175
  277.3 17.5 %collective-permute-start.51 = (bf16[2,64,1280]{2,1,0:T(8,128)(2,1)S(1)}, bf16[2,64,1280]{2,1,0:T(8,128)(2,1)}, u32[]{:S(2)}, u32[]{:S(2)}) collective-permute-start(bf16[2,64,1280]{2,1,0:T(8,128)(2,1)S(1)} %fusion.102), channel_id=1, source_target_pairs={{0,1},{1,0},{2,3},{3,2},{4,5},{5,4},{6,7},{7,6},{8,9},{9,8},{10,11... | collective-permute-start | bytes 983048 | tf_op jit(solution)/shard_map/ppermute | solution.py:176
  301.2 16.7 %collective-permute-start.36 = (bf16[2,2,64,1280]{3,2,0,1:T(8,128)(2,1)S(1)}, bf16[2,2,64,1280]{3,2,0,1:T(8,128)(2,1)S(1)}, u32[]{:S(2)}, u32[]{:S(2)}) collective-permute-start(bf16[2,2,64,1280]{3,2,0,1:T(8,128)(2,1)S(1)} %fusion.88), channel_id=1, source_target_pairs={{0,1},{1,0},{2,3},{3,2},{4,5},{5,4},{6,7},{7,6},{8,9},{9,8},{10,11... | collective-permute-start | bytes 1966088 | tf_op jit(solution)/shard_map/ppermute | solution.py:196
  320.5 18.6 %collective-permute-start.45 = (bf16[160,2560]{1,0:T(8,128)(2,1)}, bf16[160,2560]{1,0:T(8,128)(2,1)}, u32[]{:S(2)}, u32[]{:S(2)}) collective-permute-start(bf16[160,2560]{1,0:T(8,128)(2,1)} %copy-done.45), channel_id=1, source_target_pairs={{0,8},{8,16},{16,24},{24,28},{28,20},{20,12},{12,4},{4,0},{1,9},{9... | collective-permute-start | bytes 2457608 | tf_op jit(solution)/shard_map/ppermute | solution.py:144
  321.9 18.1 %collective-permute-start.46 = (bf16[160,2560]{1,0:T(8,128)(2,1)}, bf16[160,2560]{1,0:T(8,128)(2,1)}, u32[]{:S(2)}, u32[]{:S(2)}) collective-permute-start(bf16[160,2560]{1,0:T(8,128)(2,1)} %copy-done.45), channel_id=1, source_target_pairs={{8,0},{16,8},{24,16},{28,24},{20,28},{12,20},{4,12},{0,4},{9,1},{1... | collective-permute-start | bytes 2457608 | tf_op jit(solution)/shard_map/ppermute | solution.py:145
  328.7 17.9 %collective-permute-start.43 = (bf16[2,64,1280]{2,1,0:T(8,128)(2,1)S(1)}, bf16[2,64,1280]{2,1,0:T(8,128)(2,1)S(1)}, u32[]{:S(2)}, u32[]{:S(2)}) collective-permute-start(bf16[2,64,1280]{2,1,0:T(8,128)(2,1)S(1)} %multiply_convert_fusion.7), channel_id=1, source_target_pairs={{0,2},{2,0},{1,3},{3,1},{4,6},{6,4},{5,7},{7,5},{8,10},{10,8},{9,1... | collective-permute-start | bytes 983048 | tf_op jit(solution)/shard_map/ppermute | solution.py:175
  329.2 17.5 %collective-permute-start.42 = (bf16[2,64,1280]{2,1,0:T(8,128)(2,1)S(1)}, bf16[2,64,1280]{2,1,0:T(8,128)(2,1)S(1)}, u32[]{:S(2)}, u32[]{:S(2)}) collective-permute-start(bf16[2,64,1280]{2,1,0:T(8,128)(2,1)S(1)} %multiply_convert_fusion.7), channel_id=1, source_target_pairs={{0,1},{1,0},{2,3},{3,2},{4,5},{5,4},{6,7},{7,6},{8,9},{9,8},{10,11... | collective-permute-start | bytes 983048 | tf_op jit(solution)/shard_map/ppermute | solution.py:176
  340.0 17.2 %collective-permute-start.47 = (bf16[160,2560]{1,0:T(8,128)(2,1)}, bf16[160,2560]{1,0:T(8,128)(2,1)}, u32[]{:S(2)}, u32[]{:S(2)}) collective-permute-start(bf16[160,2560]{1,0:T(8,128)(2,1)} %collective-permute-done.45), channel_id=1, source_target_pairs={{0,8},{8,16},{16,24},{24,28},{28,20},{20,12},{12,4},{4,0},{1,9},{9... | collective-permute-start | bytes 2457608 | tf_op jit(solution)/shard_map/ppermute | solution.py:144
  341.5 17.3 %collective-permute-start.48 = (bf16[160,2560]{1,0:T(8,128)(2,1)}, bf16[160,2560]{1,0:T(8,128)(2,1)}, u32[]{:S(2)}, u32[]{:S(2)}) collective-permute-start(bf16[160,2560]{1,0:T(8,128)(2,1)} %collective-permute-done.46), channel_id=1, source_target_pairs={{8,0},{16,8},{24,16},{28,24},{20,28},{12,20},{4,12},{0,4},{9,1},{1... | collective-permute-start | bytes 2457608 | tf_op jit(solution)/shard_map/ppermute | solution.py:145
  358.9 20.9 %collective-permute-start.54 = (bf16[160,2560]{1,0:T(8,128)(2,1)}, bf16[160,2560]{1,0:T(8,128)(2,1)S(1)}, u32[]{:S(2)}, u32[]{:S(2)}) collective-permute-start(bf16[160,2560]{1,0:T(8,128)(2,1)} %collective-permute-done.47), channel_id=1, source_target_pairs={{0,8},{8,16},{16,24},{24,28},{28,20},{20,12},{12,4},{4,0},{1,9},{9... | collective-permute-start | bytes 2457608 | tf_op jit(solution)/shard_map/ppermute | solution.py:144
  360.2 20.5 %collective-permute-start.55 = (bf16[160,2560]{1,0:T(8,128)(2,1)}, bf16[160,2560]{1,0:T(8,128)(2,1)S(1)}, u32[]{:S(2)}, u32[]{:S(2)}) collective-permute-start(bf16[160,2560]{1,0:T(8,128)(2,1)} %collective-permute-done.48), channel_id=1, source_target_pairs={{8,0},{16,8},{24,16},{28,24},{20,28},{12,20},{4,12},{0,4},{9,1},{1... | collective-permute-start | bytes 2457608 | tf_op jit(solution)/shard_map/ppermute | solution.py:145
  365.4 19.6 %collective-permute-start.50 = (bf16[2,64,1280]{2,1,0:T(8,128)(2,1)S(1)}, bf16[2,64,1280]{2,1,0:T(8,128)(2,1)S(1)}, u32[]{:S(2)}, u32[]{:S(2)}) collective-permute-start(bf16[2,64,1280]{2,1,0:T(8,128)(2,1)S(1)} %fusion.120), channel_id=1, source_target_pairs={{0,2},{2,0},{1,3},{3,1},{4,6},{6,4},{5,7},{7,5},{8,10},{10,8},{9,1... | collective-permute-start | bytes 983048 | tf_op jit(solution)/shard_map/ppermute | solution.py:208
  492.6 36.5 %collective-permute-start.85 = (bf16[160,2560]{1,0:T(8,128)(2,1)}, bf16[160,2560]{1,0:T(8,128)(2,1)}, u32[]{:S(2)}, u32[]{:S(2)}) collective-permute-start(bf16[160,2560]{1,0:T(8,128)(2,1)} %pad_maximum_fusion.16), channel_id=1, source_target_pairs={{0,8},{8,16},{16,24},{24,28},{28,20},{20,12},{12,4},{4,0},{1,9},{9... | collective-permute-start | bytes 2457608 | tf_op jit(solution)/shard_map/ppermute | solution.py:144
  493.6 35.5 %collective-permute-start.86 = (bf16[160,2560]{1,0:T(8,128)(2,1)}, bf16[160,2560]{1,0:T(8,128)(2,1)}, u32[]{:S(2)}, u32[]{:S(2)}) collective-permute-start(bf16[160,2560]{1,0:T(8,128)(2,1)} %pad_maximum_fusion.17), channel_id=1, source_target_pairs={{8,0},{16,8},{24,16},{28,24},{20,28},{12,20},{4,12},{0,4},{9,1},{1... | collective-permute-start | bytes 2457608 | tf_op jit(solution)/shard_map/ppermute | solution.py:145
  534.4 20.5 %collective-permute-start.91 = (bf16[160,2560]{1,0:T(8,128)(2,1)}, bf16[160,2560]{1,0:T(8,128)(2,1)}, u32[]{:S(2)}, u32[]{:S(2)}) collective-permute-start(bf16[160,2560]{1,0:T(8,128)(2,1)} %get-tuple-element.342), channel_id=1, source_target_pairs={{0,8},{8,16},{16,24},{24,28},{28,20},{20,12},{12,4},{4,0},{1,9},{9... | collective-permute-start | bytes 2457608 | tf_op jit(solution)/shard_map/ppermute | solution.py:144
  535.3 20.3 %collective-permute-start.92 = (bf16[160,2560]{1,0:T(8,128)(2,1)}, bf16[160,2560]{1,0:T(8,128)(2,1)}, u32[]{:S(2)}, u32[]{:S(2)}) collective-permute-start(bf16[160,2560]{1,0:T(8,128)(2,1)} %get-tuple-element.343), channel_id=1, source_target_pairs={{8,0},{16,8},{24,16},{28,24},{20,28},{12,20},{4,12},{0,4},{9,1},{1... | collective-permute-start | bytes 2457608 | tf_op jit(solution)/shard_map/ppermute | solution.py:145
  541.1 20.3 %collective-permute-start.89 = (bf16[2,64,1280]{2,1,0:T(8,128)(2,1)}, bf16[2,64,1280]{2,1,0:T(8,128)(2,1)S(1)}, u32[]{:S(2)}, u32[]{:S(2)}) collective-permute-start(bf16[2,64,1280]{2,1,0:T(8,128)(2,1)} %get-tuple-element.546), channel_id=1, source_target_pairs={{0,2},{2,0},{1,3},{3,1},{4,6},{6,4},{5,7},{7,5},{8,10},{10,8},{9,1... | collective-permute-start | bytes 983048 | tf_op jit(solution)/shard_map/ppermute | solution.py:175
  542.8 18.7 %collective-permute-start.88 = (bf16[2,64,1280]{2,1,0:T(8,128)(2,1)}, bf16[2,64,1280]{2,1,0:T(8,128)(2,1)S(1)}, u32[]{:S(2)}, u32[]{:S(2)}) collective-permute-start(bf16[2,64,1280]{2,1,0:T(8,128)(2,1)} %get-tuple-element.546), channel_id=1, source_target_pairs={{0,1},{1,0},{2,3},{3,2},{4,5},{5,4},{6,7},{7,6},{8,9},{9,8},{10,11... | collective-permute-start | bytes 983048 | tf_op jit(solution)/shard_map/ppermute | solution.py:176
  559.0 19.4 %collective-permute-start.93 = (bf16[160,2560]{1,0:T(8,128)(2,1)}, bf16[160,2560]{1,0:T(8,128)(2,1)}, u32[]{:S(2)}, u32[]{:S(2)}) collective-permute-start(bf16[160,2560]{1,0:T(8,128)(2,1)} %get-tuple-element.345), channel_id=1, source_target_pairs={{0,8},{8,16},{16,24},{24,28},{28,20},{20,12},{12,4},{4,0},{1,9},{9... | collective-permute-start | bytes 2457608 | tf_op jit(solution)/shard_map/ppermute | solution.py:144
  559.9 19.5 %collective-permute-start.94 = (bf16[160,2560]{1,0:T(8,128)(2,1)}, bf16[160,2560]{1,0:T(8,128)(2,1)}, u32[]{:S(2)}, u32[]{:S(2)}) collective-permute-start(bf16[160,2560]{1,0:T(8,128)(2,1)} %get-tuple-element.346), channel_id=1, source_target_pairs={{8,0},{16,8},{24,16},{28,24},{20,28},{12,20},{4,12},{0,4},{9,1},{1... | collective-permute-start | bytes 2457608 | tf_op jit(solution)/shard_map/ppermute | solution.py:145
  627.2 22.8 %collective-permute-start.106 = (bf16[416,640]{1,0:T(8,128)(2,1)S(1)}, bf16[416,640]{1,0:T(8,128)(2,1)S(1)}, u32[]{:S(2)}, u32[]{:S(2)}) collective-permute-start(bf16[416,640]{1,0:T(8,128)(2,1)S(1)} %add_convert_fusion.1), channel_id=1, source_target_pairs={{0,8},{8,16},{16,24},{24,28},{28,20},{20,12},{12,4},{4,0},{1,9},{9... | collective-permute-start | bytes 1597448 | tf_op jit(solution)/shard_map/ppermute | solution.py:144
  628.5 21.5 %collective-permute-start.107 = (bf16[416,640]{1,0:T(8,128)(2,1)S(1)}, bf16[416,640]{1,0:T(8,128)(2,1)S(1)}, u32[]{:S(2)}, u32[]{:S(2)}) collective-permute-start(bf16[416,640]{1,0:T(8,128)(2,1)S(1)} %add_convert_fusion), channel_id=1, source_target_pairs={{8,0},{16,8},{24,16},{28,24},{20,28},{12,20},{4,12},{0,4},{9,1},{1... | collective-permute-start | bytes 1597448 | tf_op jit(solution)/shard_map/ppermute | solution.py:145
  714.3 18.8 %collective-permute-start.120 = (bf16[160,2880]{1,0:T(8,128)(2,1)S(1)}, bf16[160,2880]{1,0:T(8,128)(2,1)S(1)}, u32[]{:S(2)}, u32[]{:S(2)}) collective-permute-start(bf16[160,2880]{1,0:T(8,128)(2,1)S(1)} %pad_maximum_fusion.14), channel_id=1, source_target_pairs={{0,8},{8,16},{16,24},{24,28},{28,20},{20,12},{12,4},{4,0},{1,9},{9... | collective-permute-start | bytes 2764808 | tf_op jit(solution)/shard_map/ppermute | solution.py:144
  715.3 20.5 %collective-permute-start.121 = (bf16[160,2880]{1,0:T(8,128)(2,1)S(1)}, bf16[160,2880]{1,0:T(8,128)(2,1)S(1)}, u32[]{:S(2)}, u32[]{:S(2)}) collective-permute-start(bf16[160,2880]{1,0:T(8,128)(2,1)S(1)} %pad_maximum_fusion.15), channel_id=1, source_target_pairs={{8,0},{16,8},{24,16},{28,24},{20,28},{12,20},{4,12},{0,4},{9,1},{1... | collective-permute-start | bytes 2764808 | tf_op jit(solution)/shard_map/ppermute | solution.py:145
  717.6 22.3 %collective-permute-start.115 = (bf16[2,64,1280]{2,1,0:T(8,128)(2,1)S(1)}, bf16[2,64,1280]{2,1,0:T(8,128)(2,1)S(1)}, u32[]{:S(2)}, u32[]{:S(2)}) collective-permute-start(bf16[2,64,1280]{2,1,0:T(8,128)(2,1)S(1)} %fusion.124), channel_id=1, source_target_pairs={{0,2},{2,0},{1,3},{3,1},{4,6},{6,4},{5,7},{7,5},{8,10},{10,8},{9,1... | collective-permute-start | bytes 983048 | tf_op jit(solution)/shard_map/ppermute | solution.py:208
  736.3 18.4 %collective-permute-start.123 = (bf16[160,2880]{1,0:T(8,128)(2,1)S(1)}, bf16[160,2880]{1,0:T(8,128)(2,1)S(1)}, u32[]{:S(2)}, u32[]{:S(2)}) collective-permute-start(bf16[160,2880]{1,0:T(8,128)(2,1)S(1)} %get-tuple-element.389), channel_id=1, source_target_pairs={{8,0},{16,8},{24,16},{28,24},{20,28},{12,20},{4,12},{0,4},{9,1},{1... | collective-permute-start | bytes 2764808 | tf_op jit(solution)/shard_map/ppermute | solution.py:145
  737.0 17.8 %collective-permute-start.122 = (bf16[160,2880]{1,0:T(8,128)(2,1)S(1)}, bf16[160,2880]{1,0:T(8,128)(2,1)S(1)}, u32[]{:S(2)}, u32[]{:S(2)}) collective-permute-start(bf16[160,2880]{1,0:T(8,128)(2,1)S(1)} %get-tuple-element.388), channel_id=1, source_target_pairs={{0,8},{8,16},{16,24},{24,28},{28,20},{20,12},{12,4},{4,0},{1,9},{9... | collective-permute-start | bytes 2764808 | tf_op jit(solution)/shard_map/ppermute | solution.py:144
  756.5 17.1 %collective-permute-start.124 = (bf16[160,2880]{1,0:T(8,128)(2,1)}, bf16[160,2880]{1,0:T(8,128)(2,1)}, u32[]{:S(2)}, u32[]{:S(2)}) collective-permute-start(bf16[160,2880]{1,0:T(8,128)(2,1)} %get-tuple-element.390), channel_id=1, source_target_pairs={{0,8},{8,16},{16,24},{24,28},{28,20},{20,12},{12,4},{4,0},{1,9},{9... | collective-permute-start | bytes 2764808 | tf_op jit(solution)/shard_map/ppermute | solution.py:144
  757.5 17.0 %collective-permute-start.125 = (bf16[160,2880]{1,0:T(8,128)(2,1)}, bf16[160,2880]{1,0:T(8,128)(2,1)}, u32[]{:S(2)}, u32[]{:S(2)}) collective-permute-start(bf16[160,2880]{1,0:T(8,128)(2,1)} %get-tuple-element.391), channel_id=1, source_target_pairs={{8,0},{16,8},{24,16},{28,24},{20,28},{12,20},{4,12},{0,4},{9,1},{1... | collective-permute-start | bytes 2764808 | tf_op jit(solution)/shard_map/ppermute | solution.py:145
  776.0 25.3 %all-to-all-start.3 = ((f32[32,1,1440]{2,1,0:T(1,128)}), f32[32,1,1440]{2,1,0:T(1,128)S(1)}, u32[]{:S(2)}, u32[]{:S(2)}) async-start(f32[32,1,1440]{2,1,0:T(1,128)} %copy.294), calls=%async_computation.3 | async-start | bytes 393216 | tf_op jit(solution)/shard_map/all_to_all | solution.py:767
  799.3 19.8 %collective-permute-start.139 = (bf16[160,1472]{1,0:T(8,128)(2,1)}, bf16[160,1472]{1,0:T(8,128)(2,1)S(1)}, u32[]{:S(2)}, u32[]{:S(2)}) collective-permute-start(bf16[160,1472]{1,0:T(8,128)(2,1)} %pad_maximum_fusion.37), channel_id=1, source_target_pairs={{8,0},{16,8},{24,16},{28,24},{20,28},{12,20},{4,12},{0,4},{9,1},{1... | collective-permute-start | bytes 1413128 | tf_op jit(solution)/shard_map/ppermute | solution.py:145
  800.7 20.0 %collective-permute-start.138 = (bf16[160,1472]{1,0:T(8,128)(2,1)S(1)}, bf16[160,1472]{1,0:T(8,128)(2,1)}, u32[]{:S(2)}, u32[]{:S(2)}) collective-permute-start(bf16[160,1472]{1,0:T(8,128)(2,1)S(1)} %pad_maximum_fusion.36), channel_id=1, source_target_pairs={{0,8},{8,16},{16,24},{24,28},{28,20},{20,12},{12,4},{4,0},{1,9},{9... | collective-permute-start | bytes 1413128 | tf_op jit(solution)/shard_map/ppermute | solution.py:144
  807.0 17.1 %collective-permute-start.128 = (bf16[2,2,64,1280]{3,2,0,1:T(8,128)(2,1)S(1)}, bf16[2,2,64,1280]{3,2,0,1:T(8,128)(2,1)S(1)}, u32[]{:S(2)}, u32[]{:S(2)}) collective-permute-start(bf16[2,2,64,1280]{3,2,0,1:T(8,128)(2,1)S(1)} %fusion.93), channel_id=1, source_target_pairs={{0,1},{1,0},{2,3},{3,2},{4,5},{5,4},{6,7},{7,6},{8,9},{9,8},{10,11... | collective-permute-start | bytes 1966088 | tf_op jit(solution)/shard_map/ppermute | solution.py:196
  811.6 17.2 %collective-permute-start.133 = (bf16[160,1408]{1,0:T(8,128)(2,1)S(1)}, bf16[160,1408]{1,0:T(8,128)(2,1)S(1)}, u32[]{:S(2)}, u32[]{:S(2)}) collective-permute-start(bf16[160,1408]{1,0:T(8,128)(2,1)S(1)} %get-tuple-element.402), channel_id=1, source_target_pairs={{8,0},{16,8},{24,16},{28,24},{20,28},{12,20},{4,12},{0,4},{9,1},{1... | collective-permute-start | bytes 1351688 | tf_op jit(solution)/shard_map/ppermute | solution.py:145
  813.7 16.6 %collective-permute-start.132 = (bf16[160,1408]{1,0:T(8,128)(2,1)S(1)}, bf16[160,1408]{1,0:T(8,128)(2,1)S(1)}, u32[]{:S(2)}, u32[]{:S(2)}) collective-permute-start(bf16[160,1408]{1,0:T(8,128)(2,1)S(1)} %get-tuple-element.401), channel_id=1, source_target_pairs={{0,8},{8,16},{16,24},{24,28},{28,20},{20,12},{12,4},{4,0},{1,9},{9... | collective-permute-start | bytes 1351688 | tf_op jit(solution)/shard_map/ppermute | solution.py:144
  822.0 17.3 %collective-permute-start.141 = (bf16[160,1472]{1,0:T(8,128)(2,1)S(1)}, bf16[160,1472]{1,0:T(8,128)(2,1)S(1)}, u32[]{:S(2)}, u32[]{:S(2)}) collective-permute-start(bf16[160,1472]{1,0:T(8,128)(2,1)S(1)} %get-tuple-element.410), channel_id=1, source_target_pairs={{8,0},{16,8},{24,16},{28,24},{20,28},{12,20},{4,12},{0,4},{9,1},{1... | collective-permute-start | bytes 1413128 | tf_op jit(solution)/shard_map/ppermute | solution.py:145
  824.1 16.7 %collective-permute-start.140 = (bf16[160,1472]{1,0:T(8,128)(2,1)S(1)}, bf16[160,1472]{1,0:T(8,128)(2,1)S(1)}, u32[]{:S(2)}, u32[]{:S(2)}) collective-permute-start(bf16[160,1472]{1,0:T(8,128)(2,1)S(1)} %get-tuple-element.409), channel_id=1, source_target_pairs={{0,8},{8,16},{16,24},{24,28},{28,20},{20,12},{12,4},{4,0},{1,9},{9... | collective-permute-start | bytes 1413128 | tf_op jit(solution)/shard_map/ppermute | solution.py:144
  824.3 18.9 %collective-permute-start.129 = (bf16[2,64,1280]{2,1,0:T(8,128)(2,1)S(1)}, bf16[2,64,1280]{2,1,0:T(8,128)(2,1)S(1)}, u32[]{:S(2)}, u32[]{:S(2)}) collective-permute-start(bf16[2,64,1280]{2,1,0:T(8,128)(2,1)S(1)} %fusion.125), channel_id=1, source_target_pairs={{0,2},{2,0},{1,3},{3,1},{4,6},{6,4},{5,7},{7,5},{8,10},{10,8},{9,1... | collective-permute-start | bytes 983048 | tf_op jit(solution)/shard_map/ppermute | solution.py:208
  830.5 18.5 %collective-permute-start.135 = (bf16[160,1408]{1,0:T(8,128)(2,1)S(1)}, bf16[160,1408]{1,0:T(8,128)(2,1)S(1)}, u32[]{:S(2)}, u32[]{:S(2)}) collective-permute-start(bf16[160,1408]{1,0:T(8,128)(2,1)S(1)} %get-tuple-element.404), channel_id=1, source_target_pairs={{8,0},{16,8},{24,16},{28,24},{20,28},{12,20},{4,12},{0,4},{9,1},{1... | collective-permute-start | bytes 1351688 | tf_op jit(solution)/shard_map/ppermute | solution.py:145
  832.6 17.8 %collective-permute-start.134 = (bf16[160,1408]{1,0:T(8,128)(2,1)S(1)}, bf16[160,1408]{1,0:T(8,128)(2,1)S(1)}, u32[]{:S(2)}, u32[]{:S(2)}) collective-permute-start(bf16[160,1408]{1,0:T(8,128)(2,1)S(1)} %get-tuple-element.403), channel_id=1, source_target_pairs={{0,8},{8,16},{16,24},{24,28},{28,20},{20,12},{12,4},{4,0},{1,9},{9... | collective-permute-start | bytes 1351688 | tf_op jit(solution)/shard_map/ppermute | solution.py:144
  841.1 16.9 %collective-permute-start.143 = (bf16[160,1472]{1,0:T(8,128)(2,1)S(1)}, bf16[160,1472]{1,0:T(8,128)(2,1)S(1)}, u32[]{:S(2)}, u32[]{:S(2)}) collective-permute-start(bf16[160,1472]{1,0:T(8,128)(2,1)S(1)} %get-tuple-element.412), channel_id=1, source_target_pairs={{8,0},{16,8},{24,16},{28,24},{20,28},{12,20},{4,12},{0,4},{9,1},{1... | collective-permute-start | bytes 1413128 | tf_op jit(solution)/shard_map/ppermute | solution.py:145
  843.2 16.0 %collective-permute-start.142 = (bf16[160,1472]{1,0:T(8,128)(2,1)S(1)}, bf16[160,1472]{1,0:T(8,128)(2,1)S(1)}, u32[]{:S(2)}, u32[]{:S(2)}) collective-permute-start(bf16[160,1472]{1,0:T(8,128)(2,1)S(1)} %get-tuple-element.411), channel_id=1, source_target_pairs={{0,8},{8,16},{16,24},{24,28},{28,20},{20,12},{12,4},{4,0},{1,9},{9... | collective-permute-start | bytes 1413128 | tf_op jit(solution)/shard_map/ppermute | solution.py:144
  (245 other events, 2357.6 us)
